TPU v7x, 256 devices: a whole 4x4x8 slice. The times are simulated.
256 devices in a mesh: role: 2 (over x_lo), shard: 128 (over z, y, x_hi, core).
Axes of the slice: x: 4 (x_hi: 2, x_lo: 2; x = x_hi * 2 + x_lo), y: 4, z: 8, core: 2. Of those that a mesh axis runs over, the one named last changes fastest.
Arguments:
- tables: float32 [2, 262144, 128], P('role', 'shard'), may hold values from -6 to 6
- row_squares: float32 [262144, 128], P('shard'), may hold values from 0.01 to 1
- update_slots: int32 [65536], P('shard'), may hold values from 0 to 2047, as said below
- update_counts: int32 [128], P('shard'), may hold values from 1 to 512, 32768 in all
- row_grads: float32 [65536, 128], P('shard'), may hold values from -6 to 6
- dense_state: float32 [2, 3, 512, 512], P('role'), may hold values from -0.6 to 0.6
- dense_squares: float32 [3, 512, 512], replicated, may hold values from 0.01 to 1
- dense_grads: float32 [128, 3, 512, 512], P('shard'), may hold values from -0.06 to 0.06
- cross_bias: float32 [3, 512], replicated, may hold values from -3 to 3
- out_weight: float32 [512], replicated, may hold values from -0.75 to 0.75
- cand_owner: int32 [2, 65536, 4], P('role', 'shard'), may hold values from 0 to 127, all different within a row; in each aligned block of 512 rows (0 to 511, 512 to 1023, ..., all dimensions but the last counted through in order) at most 32 rows name the same one
- cand_slot: int32 [2, 65536, 4], P('role', 'shard'), may hold values from 0 to 2047
Outputs:
- tables_out: float32 [2, 262144, 128], P('role', 'shard')
- scores: float32 [2, 65536], P('role', 'shard')
Inputs may be any that keep to these rules, and one draw needn't show every extreme that they name: `update_slots`: the 512 slots of one shard name distinct rows. `update_counts`: the counts sum to 32768. `cand_owner`: the 4 owners of one example are distinct; among the 512 examples of one device no shard is named more than 32 times, a bound that some block reaches.
All inputs are finite; a program needn't handle non-finite values. No bound on the sum of `update_counts` on one device may be relied on, other than what follows from the above.
Results may differ from a plain program's by a relative error of at most 0.0084.
Values may be sent and summed in bfloat16 or wider, within the bound.
No kernel may reach another device: no remote copies, remote signals or barrier semaphores. Data moves between devices by JAX's collectives and lax.ppermute only.
A program may use at most 64 MiB of HBM per device.

v0:
```python
import jax
import jax.numpy as jnp
from jax import lax
from jax.sharding import PartitionSpec as P

ROW_SHRINK = 0.25
DENSE_SHRINK = 0.05


def passed_along(value, axis, steps):
    count = lax.axis_size(axis)
    leading, last = (max(0, -steps), min(count, count - steps))
    return lax.ppermute(value, axis, [(source, source + steps) for source in range(leading, last)])


def ftrl_weight(linear, squares, shrink):
    return -(linear - jnp.clip(linear, -shrink, shrink)) / (1.0 + jnp.sqrt(squares))


def ftrl_step(linear, squares, gradient, shrink):
    prior = ftrl_weight(linear, squares, shrink)
    fresh_squares = squares + gradient * gradient
    sigma_step = jnp.sqrt(fresh_squares) - jnp.sqrt(squares)
    return (linear + gradient - sigma_step * prior, fresh_squares, prior)


def on_device(
    tables,
    row_squares,
    update_slots,
    update_counts,
    row_grads,
    dense_state,
    dense_squares,
    dense_grads,
    cross_bias,
    out_weight,
    cand_owner,
    cand_slot,
):
    trainer = lax.axis_index("role") == 0
    row_count = row_squares.shape[0]
    usable = jnp.arange(update_slots.shape[0], dtype=jnp.int32) < update_counts[0]
    targets = jnp.where(usable, update_slots, row_count)
    held_table = tables[0]
    fresh_linear, fresh_sumsq, unused = ftrl_step(
        held_table[update_slots], row_squares[update_slots], row_grads, ROW_SHRINK
    )
    new_linear = held_table.at[targets].set(fresh_linear, mode="drop")
    new_squares = row_squares.at[targets].set(fresh_sumsq, mode="drop")
    fresh_weights = ftrl_weight(fresh_linear, fresh_sumsq, ROW_SHRINK)
    arrived = passed_along(fresh_weights.astype(jnp.bfloat16), "role", 1).astype(
        fresh_weights.dtype
    )
    serving_table = held_table.at[targets].set(arrived, mode="drop")
    trainer_table = ftrl_weight(new_linear, new_squares, ROW_SHRINK)
    lookup_table = jnp.where(trainer, trainer_table, serving_table).astype(jnp.bfloat16)
    table_result = jnp.where(trainer, new_linear, serving_table)
    held_dense = dense_state[0]
    summed = lax.psum(dense_grads[0], "shard")
    dense_linear, dense_sumsq, prior_weights = ftrl_step(
        held_dense, dense_squares, summed, DENSE_SHRINK
    )
    fresh_dense = ftrl_weight(dense_linear, dense_sumsq, DENSE_SHRINK)
    dense_change = passed_along(fresh_dense - prior_weights, "role", 1)
    cross_weights = jnp.where(trainer, fresh_dense, held_dense + dense_change).astype(jnp.bfloat16)
    examples = cand_owner.shape[1]
    owners = cand_owner[0].reshape(-1)
    slot_ids = cand_slot[0].reshape(-1)
    shards = lax.axis_size("shard")
    capacity = 2 * owners.shape[0] // shards
    ordering = jnp.argsort(owners, stable=True)
    counts = jnp.sum(
        (owners[:, None] == jnp.arange(shards, dtype=jnp.int32)[None, :]).astype(jnp.int32), axis=0
    )
    starts = jnp.cumsum(counts) - counts
    ranked = jnp.arange(owners.shape[0], dtype=jnp.int32) - starts[owners[ordering]]
    ranks = jnp.zeros(owners.shape[0], jnp.int32).at[ordering].set(ranked)
    requests = jnp.zeros((shards, capacity), jnp.int32).at[owners, ranks].set(slot_ids)
    answered = lax.all_to_all(
        lookup_table[lax.all_to_all(requests, "shard", split_axis=0, concat_axis=0, tiled=True)],
        "shard",
        split_axis=0,
        concat_axis=0,
        tiled=True,
    )
    base_feats = answered[owners, ranks].reshape(examples, -1).astype(jnp.float32)
    crossed = base_feats
    for layer_idx in range(cross_weights.shape[0]):
        mixed_rows = jnp.dot(
            crossed.astype(jnp.bfloat16),
            cross_weights[layer_idx],
            preferred_element_type=jnp.float32,
        )
        crossed = base_feats * (mixed_rows + cross_bias[layer_idx]) + crossed
    scores = jnp.sum(crossed * out_weight, axis=1)
    return (table_result[None], scores[None])


def solution(mesh):
    return jax.shard_map(
        on_device,
        mesh=mesh,
        in_specs=(
            P("role", "shard", None),
            P("shard", None),
            P("shard"),
            P("shard"),
            P("shard", None),
            P("role", None, None, None),
            P(),
            P("shard", None, None, None),
            P(),
            P(),
            P("role", "shard", None),
            P("role", "shard", None),
        ),
        out_specs=(P("role", "shard", None), P("role", "shard")),
        check_vma=False,
    )
```

profile of v0, /device:TPU:2, one launch (start us, length us, event | category | flops | bytes accessed | tf_op | source)
XLA Modules:
  0.0 1456.4 jit_solution(6400572309420608194)
XLA Ops:
  7.2 1.2 copy.46
  8.4 1.2 copy.47
  10.2 5.0 sort.17
  16.0 11.8 gather_fusion.2
  28.2 12.6 gather_fusion.3
  40.9 8.0 scatter_custom_fusion.3
  49.2 8.1 scatter_custom_fusion.4
  58.0 14.9 %all-to-all-start = ((s32[128,1,32]{2,1,0:T(1,128)}), s32[128,1,32]{2,1,0:T(1,128)S(1)}, u32[]{:S(2)}, u32[]{:S(2)}) async-start(s32[128,1,32]{2,1,0:T(1,128)} %copy.36), calls=%async_computation | async-start | bytes 131072 | tf_op jit(solution)/shard_map/all_to_all | solution.py:81
  75.7 1215.4 %all-reduce.2.cloned.1.call-done = f32[3,512,512]{2,1,0:T(8,128)} async-done(((f32[3,512,512]{2,1,0:T(8,128)}), f32[3,512,512]{2,1,0:T(8,128)}) %all-reduce.2.cloned.1.call-update) | async-done | bytes 3145744 | tf_op jit(solution)/shard_map/psum | solution.py:60
  1291.1 6.9 fusion.7
  1298.0 1.3 collective-permute-start.1
  1299.6 1.3 collective-permute-start
  1301.9 2.1 scatter_custom_fusion.2
  1304.0 2.5 scatter_custom_fusion
  1306.7 61.3 %collective-permute-done = bf16[512,128]{1,0:T(8,128)(2,1)S(1)} collective-permute-done((bf16[512,128]{1,0:T(8,128)(2,1)S(1)}, bf16[512,128]{1,0:T(8,128)(2,1)S(1)}, u32[]{:S(2)}, u32[]{:S(2)}) %collective-permute-start) | collective-permute-done | bytes 131104 | tf_op jit(solution)/shard_map/ppermute | solution.py:13
  1368.0 3.9 scatter_custom_fusion.1
  1371.8 1.7 fusion.15
  1373.6 14.9 %gather_fusion.4 = bf16[4096,128]{1,0:T(8,128)(2,1)} fusion(bf16[2048,128]{1,0:T(8,128)(2,1)S(1)} %fusion.15, s32[4096]{0:T(1024)S(1)} %broadcast_clamp_fusion), kind=kCustom, calls=%fused_computation.4 | custom fusion | bytes 2113536 | tf_op jit(solution)/shard_map/gather | solution.py:81
  1388.5 9.0 all-to-all-start.1
  1397.5 2.3 select_bitcast_fusion
  1399.8 29.4 %all-to-all-done.1 = bf16[128,32,128]{2,1,0:T(8,128)(2,1)S(1)} async-done(((bf16[128,32,128]{2,1,0:T(8,128)(2,1)}), bf16[128,32,128]{2,1,0:T(8,128)(2,1)S(1)}, u32[]{:S(2)}, u32[]{:S(2)}) %all-to-all-start.1) | async-done | bytes 1048608 | tf_op jit(solution)/shard_map/all_to_all | solution.py:80
  1429.3 11.1 gather_fusion.5
  1440.9 6.4 fusion.6
  1448.4 1.2 fusion.11
  (55 shorter events, 7.6 us)
Async XLA Ops:
  7.2 1283.9 %all-reduce.2.cloned.1.call-start = ((), (), s32[]{:S(2)}) async-start(), calls=%async_computation.2 | async-start | bytes 6291456 | tf_op jit(solution)/shard_map/psum | solution.py:60
  8.4 1.3 copy-start.1
  16.0 11.8 copy-start.2
  28.2 20.8 %copy-start.6 = (s32[2]{0:T(128)S(1)}, s32[2]{0:T(128)}, u32[]{:S(2)}) copy-start(s32[2]{0:T(128)} %constant.43) | copy-start | bytes 28
  28.2 20.9 %copy-start.5 = (s32[2]{0:T(128)S(1)}, s32[2]{0:T(128)}, u32[]{:S(2)}) copy-start(s32[2]{0:T(128)} %constant.46) | copy-start | bytes 28
  28.2 45.3 %copy-start.4 = (s32[512]{0:T(512)S(1)}, s32[512]{0:T(512)}, u32[]{:S(2)}) copy-start(s32[512]{0:T(512)} %param.14) | copy-start | bytes 6148
  58.0 1248.6 %all-to-all-start = ((s32[128,1,32]{2,1,0:T(1,128)}), s32[128,1,32]{2,1,0:T(1,128)S(1)}, u32[]{:S(2)}, u32[]{:S(2)}) async-start(s32[128,1,32]{2,1,0:T(1,128)} %copy.36), calls=%async_computation | async-start | bytes 131072 | tf_op jit(solution)/shard_map/all_to_all | solution.py:81
  75.7 1223.7 %copy-start = (f32[512,128]{1,0:T(8,128)S(1)}, f32[512,128]{1,0:T(8,128)}, u32[]{:S(2)}) copy-start(f32[512,128]{1,0:T(8,128)} %param.16) | copy-start | bytes 786436
  1298.0 142.9 %collective-permute-start.1 = (f32[3,512,512]{2,1,0:T(8,128)}, f32[3,512,512]{2,1,0:T(8,128)}, u32[]{:S(2)}, u32[]{:S(2)}) collective-permute-start(f32[3,512,512]{2,1,0:T(8,128)} %fusion.7), channel_id=1, source_target_pairs={{0,128},{1,129},{2,130},{3,131},{4,132},{5,133},{6,134},{7,135},{8... | collective-permute-start | bytes 9437192 | tf_op jit(solution)/shard_map/ppermute | solution.py:13
  1299.6 68.3 %collective-permute-start = (bf16[512,128]{1,0:T(8,128)(2,1)S(1)}, bf16[512,128]{1,0:T(8,128)(2,1)S(1)}, u32[]{:S(2)}, u32[]{:S(2)}) collective-permute-start(bf16[512,128]{1,0:T(8,128)(2,1)S(1)} %fusion.26), channel_id=1, source_target_pairs={{0,128},{1,129},{2,130},{3,131},{4,132},{5,133},{6,134},{7,135},{8... | collective-permute-start | bytes 393224 | tf_op jit(solution)/shard_map/ppermute | solution.py:13
  1373.6 23.9 %copy-start.3 = (f32[3,512]{1,0:T(4,128)S(1)}, f32[3,512]{1,0:T(4,128)}, u32[]{:S(2)}) copy-start(f32[3,512]{1,0:T(4,128)} %param.20) | copy-start | bytes 18436
  1388.5 40.7 %all-to-all-start.1 = ((bf16[128,32,128]{2,1,0:T(8,128)(2,1)}), bf16[128,32,128]{2,1,0:T(8,128)(2,1)S(1)}, u32[]{:S(2)}, u32[]{:S(2)}) async-start(bf16[128,32,128]{2,1,0:T(8,128)(2,1)} %bitcast.58), calls=%async_computation.1 | async-start | bytes 2097152 | tf_op jit(solution)/shard_map/all_to_all | solution.py:80
  1447.4 1.0 copy-start.7
Sparse Core Ops, SparseCore 0:
  10.6 1280.4 all-reduce.1
where the time goes:
time: 1460 us
  waiting for transfers between devices  1310 us (90%)
  local copies, waits for them, and re-layouts  74.3 us (5%)
  other arithmetic  32.2 us (2%)
  starting transfers between devices  26.5 us (2%)
  between operations  15.1 us (1%)
    psum x1, waiting for transfers between devices, on_device(): summed = lax.psum(dense_grads[0], 'shard')  1220 us
    ppermute x2, waiting for transfers between devices, passed_along(): lax.ppermute(value, axis, [(source, source + steps) for source in range(l...  61.3 us
    all_to_all x1, waiting for transfers between devices, on_device(): lax.all_to_all(lookup_table[lax.all_to_all(requests, 'shard', split_axis=...  29.4 us
  transfers between devices with their start and end apart: 5, of which 3 were waited for; matrix products, arithmetic and copies ran while one was open for 7% of the time, Pallas kernels for 0%

commit v1 on v0

v1 whole, which is shorter than its diff:
```python
import functools

import jax
import jax.numpy as jnp
from jax import lax
from jax.experimental import pallas as pl
from jax.experimental.pallas import tpu as pltpu
from jax.sharding import PartitionSpec as P

ROW_SHRINK = 0.25
DENSE_SHRINK = 0.05
CAP = 32
LANES = 128
SHARDS = 128
ROLES = 2
Z_SIZE, Y_SIZE, X_SIZE, CORES = 8, 4, 2, 2
VMEM_LIMIT = 40 * 1024 * 1024


def shard_at(z, y, x, core):
    return ((z * Y_SIZE + y) * X_SIZE + x) * CORES + core


def ftrl_weight(linear, squares, shrink):
    return -(linear - jnp.clip(linear, -shrink, shrink)) / (1.0 + jnp.sqrt(squares))


def ftrl_step(linear, squares, gradient, shrink):
    prior = ftrl_weight(linear, squares, shrink)
    fresh_squares = squares + gradient * gradient
    sigma_step = jnp.sqrt(fresh_squares) - jnp.sqrt(squares)
    return (linear + gradient - sigma_step * prior, fresh_squares, prior)


def iota(shape, dim):
    return lax.broadcasted_iota(jnp.int32, shape, dim)


def kernel_call(body, out_shape, flops=0, bytes_accessed=0, **options):
    return pl.pallas_call(
        body,
        out_shape=out_shape,
        compiler_params=pltpu.CompilerParams(vmem_limit_bytes=VMEM_LIMIT),
        cost_estimate=pl.CostEstimate(
            flops=flops, bytes_accessed=bytes_accessed, transcendentals=0
        ),
        **options,
    )


VMEM = pl.BlockSpec(memory_space=pltpu.VMEM)
SMEM = pl.BlockSpec(memory_space=pltpu.SMEM)


def routing_body(owner_ref, slot_ref, request_ref, place_ref):
    fields, examples = owner_ref.shape
    shape = (SHARDS, examples)
    shard_ids = iota(shape, 0)
    member = jnp.zeros(shape, jnp.float32)
    wanted = jnp.zeros(shape, jnp.float32)
    for field in range(fields):
        named = owner_ref[field : field + 1, :] == shard_ids
        member = jnp.where(named, 1.0, member)
        wanted = jnp.where(named, slot_ref[field : field + 1, :].astype(jnp.float32), wanted)
    earlier = jnp.where(iota((examples, examples), 0) < iota((examples, examples), 1), 1.0, 0.0)
    ranks = jnp.dot(
        member.astype(jnp.bfloat16),
        earlier.astype(jnp.bfloat16),
        preferred_element_type=jnp.float32,
    )
    places = []
    for field in range(fields):
        owners = owner_ref[field : field + 1, :]
        rank = jnp.sum(jnp.where(owners == shard_ids, ranks, 0.0), axis=0, keepdims=True)
        places.append(owners * CAP + rank.astype(jnp.int32))
    place_ref[...] = jnp.concatenate(
        places + [jnp.zeros((8 - fields, examples), jnp.int32)], axis=0
    )
    ranks = jnp.where(member > 0.5, ranks, -1.0)
    requests = jnp.zeros((SHARDS, LANES), jnp.float32)
    lanes = iota((SHARDS, LANES), 1)
    for rank in range(CAP):
        column = jnp.sum(
            jnp.where(ranks == float(rank), wanted, 0.0), axis=1, keepdims=True
        )
        requests = jnp.where(lanes == rank, column, requests)
    request_ref[...] = requests[:, :CAP].astype(jnp.int32)


def route(owners, slots):
    fields, examples = owners.shape
    return kernel_call(
        routing_body,
        (
            jax.ShapeDtypeStruct((SHARDS, CAP), jnp.int32),
            jax.ShapeDtypeStruct((8, examples), jnp.int32),
        ),
        flops=10_000_000,
        bytes_accessed=100_000,
        in_specs=[VMEM, VMEM],
        out_specs=(VMEM, VMEM),
    )(owners, slots)


def used_slots(slot_ref, count):
    slots = slot_ref[...]
    return jnp.where(iota(slots.shape, 1) < count, slots, -1)


def rows_of_block(slots, first, rows):
    hit = slots == iota((rows, slots.shape[1]), 0) + first
    return jnp.where(hit, 1.0, 0.0).astype(jnp.bfloat16)


def train_body(count_ref, slot_ref, held_ref, square_ref, grad_ref, new_ref, weight_ref, fresh_ref, parts, total):
    step = pl.program_id(0)
    rows = held_ref.shape[0]

    @pl.when(step == 0)
    def _():
        grads = grad_ref[...]
        high = grads.astype(jnp.bfloat16)
        rest = grads - high.astype(jnp.float32)
        middle = rest.astype(jnp.bfloat16)
        low = (rest - middle.astype(jnp.float32)).astype(jnp.bfloat16)
        parts[...] = jnp.concatenate([high, middle, low], axis=1)
        total[...] = jnp.zeros_like(total)

    spread = rows_of_block(used_slots(slot_ref, count_ref[0]), step * rows, rows)
    sums = jnp.dot(spread, parts[...], preferred_element_type=jnp.float32)
    gradient = (sums[:, :LANES] + sums[:, LANES : 2 * LANES]) + sums[:, 2 * LANES :]
    linear, squares, _ = ftrl_step(held_ref[...], square_ref[...], gradient, ROW_SHRINK)
    new_ref[...] = linear
    weights = ftrl_weight(linear, squares, ROW_SHRINK).astype(jnp.bfloat16)
    weight_ref[...] = weights
    total[...] += lax.dot_general(
        spread, weights, (((0,), (0,)), ((), ())), preferred_element_type=jnp.float32
    )

    @pl.when(step == pl.num_programs(0) - 1)
    def _():
        fresh_ref[...] = total[...].astype(jnp.bfloat16)


def train_rows(count, slots, held, squares, grads):
    rows, width = held.shape
    updates = grads.shape[0]
    block = 512
    by_rows = pl.BlockSpec((block, width), lambda i: (i, 0))
    return kernel_call(
        train_body,
        (
            jax.ShapeDtypeStruct((rows, width), jnp.float32),
            jax.ShapeDtypeStruct((rows, width), jnp.bfloat16),
            jax.ShapeDtypeStruct((updates, width), jnp.bfloat16),
        ),
        flops=2 * rows * updates * width * 4,
        bytes_accessed=8_000_000,
        grid=(rows // block,),
        in_specs=[
            SMEM,
            pl.BlockSpec((1, updates), lambda i: (0, 0)),
            by_rows,
            by_rows,
            pl.BlockSpec((updates, width), lambda i: (0, 0)),
        ],
        out_specs=(by_rows, by_rows, pl.BlockSpec((updates, width), lambda i: (0, 0))),
        scratch_shapes=[
            pltpu.VMEM((updates, 3 * width), jnp.bfloat16),
            pltpu.VMEM((updates, width), jnp.float32),
        ],
    )(count, slots, held, squares, grads)


def serve_body(role_ref, count_ref, slot_ref, arrived_ref, held_ref, new_ref, weight_ref, table_ref, lookup_ref):
    step = pl.program_id(0)
    rows = held_ref.shape[0]

    @pl.when(role_ref[0] == 0)
    def _():
        table_ref[...] = new_ref[...]
        lookup_ref[...] = weight_ref[...]

    @pl.when(role_ref[0] != 0)
    def _():
        spread = rows_of_block(used_slots(slot_ref, count_ref[0]), step * rows, rows)
        arrived = arrived_ref[...]
        sums = jnp.dot(
            spread,
            jnp.concatenate([arrived, jnp.ones_like(arrived)], axis=1),
            preferred_element_type=jnp.float32,
        )
        table = jnp.where(sums[:, LANES:] > 0.5, sums[:, :LANES], held_ref[...])
        table_ref[...] = table
        lookup_ref[...] = table.astype(jnp.bfloat16)


def serve_rows(role, count, slots, arrived, held, new_linear, weights):
    rows, width = held.shape
    updates = arrived.shape[0]
    block = 1024
    by_rows = pl.BlockSpec((block, width), lambda i: (i, 0))
    return kernel_call(
        serve_body,
        (
            jax.ShapeDtypeStruct((rows, width), jnp.float32),
            jax.ShapeDtypeStruct((rows, width), jnp.bfloat16),
        ),
        flops=2 * rows * updates * width * 2,
        bytes_accessed=5_000_000,
        grid=(rows // block,),
        in_specs=[
            SMEM,
            SMEM,
            pl.BlockSpec((1, updates), lambda i: (0, 0)),
            pl.BlockSpec((updates, width), lambda i: (0, 0)),
            by_rows,
            by_rows,
            by_rows,
        ],
        out_specs=(by_rows, by_rows),
    )(role, count, slots, arrived, held, new_linear, weights)


def one_hot_rows(column, width):
    rows = column.shape[0]
    spread = jnp.broadcast_to(column, (rows, LANES))
    within = jnp.where((spread & (LANES - 1)) == iota((rows, LANES), 1), 1.0, 0.0).astype(
        jnp.bfloat16
    )
    block = (spread >> 7).astype(jnp.float32).astype(jnp.bfloat16)
    none = jnp.zeros_like(within)
    return jnp.concatenate(
        [jnp.where(block == jnp.bfloat16(at), within, none) for at in range(width // LANES)],
        axis=1,
    )


def answer_body(request_ref, table_ref, answer_ref, columns):
    shards, capacity = request_ref.shape
    wide = jnp.concatenate(
        [request_ref[...], jnp.zeros((shards, LANES - capacity), jnp.int32)], axis=1
    )
    columns[...] = jnp.transpose(wide)[:capacity, :]
    group = 8
    for at in range(0, shards, group):
        asked = jnp.concatenate(
            [columns[:, shard : shard + 1] for shard in range(at, at + group)], axis=0
        )
        rows = jnp.dot(
            one_hot_rows(asked, table_ref.shape[0]),
            table_ref[...],
            preferred_element_type=jnp.float32,
        )
        answer_ref[at * capacity : (at + group) * capacity, :] = rows.astype(jnp.bfloat16)


def answer_rows(requests, table):
    shards, capacity = requests.shape
    rows, width = table.shape
    return kernel_call(
        answer_body,
        jax.ShapeDtypeStruct((shards * capacity, width), jnp.bfloat16),
        flops=2 * shards * capacity * rows * width,
        bytes_accessed=2_000_000,
        in_specs=[VMEM, VMEM],
        out_specs=VMEM,
        scratch_shapes=[pltpu.VMEM((capacity, shards), jnp.int32)],
    )(requests, table)


def arrange_body(place_ref, answer_ref, base_ref, columns):
    columns[...] = jnp.transpose(place_ref[...])
    examples = columns.shape[0]
    block = 256
    for field in range(base_ref.shape[1] // LANES):
        for at in range(0, examples, block):
            rows = jnp.dot(
                one_hot_rows(columns[at : at + block, field : field + 1], answer_ref.shape[0]),
                answer_ref[...],
                preferred_element_type=jnp.float32,
            )
            base_ref[at : at + block, field * LANES : (field + 1) * LANES] = rows.astype(
                jnp.bfloat16
            )


def arrange_rows(places, answers, fields):
    examples = places.shape[1]
    rows, width = answers.shape
    return kernel_call(
        arrange_body,
        jax.ShapeDtypeStruct((examples, fields * width), jnp.bfloat16),
        flops=2 * examples * fields * rows * width,
        bytes_accessed=2_000_000,
        in_specs=[VMEM, VMEM],
        out_specs=VMEM,
        scratch_shapes=[pltpu.VMEM((examples, 8), jnp.int32)],
    )(places, answers)


def cross_body(where_ref, base_ref, bias_ref, out_ref, *refs):
    block_refs, score_ref, weights = refs[: 2 * Y_SIZE], refs[2 * Y_SIZE], refs[2 * Y_SIZE + 1]
    y, core = where_ref[0], where_ref[1]
    rows, columns = block_refs[0].shape
    for ahead in range(Y_SIZE):
        first = pl.multiple_of(lax.rem(y + ahead, Y_SIZE) * rows, rows)
        for other in range(CORES):
            left = pl.multiple_of(lax.rem(core + other, CORES) * columns, columns)
            weights[pl.ds(first, rows), pl.ds(left, columns)] = block_refs[
                other * Y_SIZE + ahead
            ][...]
    width = base_ref.shape[1]
    base = base_ref[...].astype(jnp.float32)
    crossed = base
    for layer in range(bias_ref.shape[0]):
        mixed = jnp.dot(
            crossed.astype(jnp.bfloat16),
            weights[layer * width : (layer + 1) * width, :],
            preferred_element_type=jnp.float32,
        )
        crossed = base * (mixed + bias_ref[layer : layer + 1, :]) + crossed
    scores = jnp.sum(crossed * out_ref[...], axis=1, keepdims=True)
    score_ref[...] = jnp.transpose(jnp.broadcast_to(scores, (scores.shape[0], LANES)))[:8, :]


def cross_scores(where, base, bias, out_weight, blocks):
    examples, width = base.shape
    layers = bias.shape[0]
    return kernel_call(
        cross_body,
        jax.ShapeDtypeStruct((8, examples), jnp.float32),
        flops=2 * examples * width * width * layers,
        bytes_accessed=3_000_000,
        in_specs=[SMEM] + [VMEM] * (3 + len(blocks)),
        out_specs=VMEM,
        scratch_shapes=[pltpu.VMEM((layers * width, width), jnp.bfloat16)],
    )(where, base, bias, out_weight, *blocks)


def along(value, axis, partner):
    count = lax.axis_size(axis)
    return lax.ppermute(value, axis, [(source, partner(source)) for source in range(count)])


def ahead_in_y(source, steps):
    z, rest = divmod(source, Y_SIZE * X_SIZE * CORES)
    y, rest = divmod(rest, X_SIZE * CORES)
    return (z * Y_SIZE + (y - steps) % Y_SIZE) * X_SIZE * CORES + rest


Z_GROUPS = [
    [shard_at(z, y, x, core) for z in range(Z_SIZE)]
    for y in range(Y_SIZE)
    for x in range(X_SIZE)
    for core in range(CORES)
]
YZ_GROUPS = [
    [shard_at(z, y, x, core) for y in range(Y_SIZE) for z in range(Z_SIZE)]
    for x in range(X_SIZE)
    for core in range(CORES)
]


def exchange(value, axis, groups):
    return lax.all_to_all(
        value, axis, split_axis=0, concat_axis=0, tiled=True, axis_index_groups=groups
    )


def fresh_weight_blocks(role, shard, dense_state, dense_squares, dense_grads):
    layers, width, _ = dense_grads.shape
    rows = layers * width
    parts = Y_SIZE * Z_SIZE
    half = width // CORES
    piece = rows // parts
    core = shard % CORES
    at = (shard // (X_SIZE * CORES)) % Y_SIZE * Z_SIZE + shard // (Y_SIZE * X_SIZE * CORES)

    def own_piece(array):
        return lax.dynamic_slice(
            array.reshape(rows, width), (at * piece, core * half), (piece, half)
        )

    state = own_piece(dense_state)
    squares = own_piece(dense_squares)
    trained = lax.ppermute(state, "role", [(0, 1)])

    grads = dense_grads.reshape(parts, ROLES, piece // ROLES, width)

    def half_of(which):
        return lax.dynamic_slice(
            grads, (0, role, 0, which * half), (parts, 1, piece // ROLES, half)
        )[:, 0]

    pair = half_of(core) + along(half_of(1 - core), "shard", lambda s: s ^ 1)
    term = jnp.sum(exchange(pair, "shard", YZ_GROUPS), axis=0)
    both = ("role", "shard")
    side = X_SIZE * CORES // 2

    def from_ring(other_role, other_x):
        return along(term, both, lambda s: s ^ (SHARDS * other_role + side * other_x))

    mine = term + from_ring(0, 1)
    theirs = from_ring(1, 0) + from_ring(1, 1)
    trainer = role == 0
    summed = jnp.concatenate(
        [jnp.where(trainer, mine, theirs), jnp.where(trainer, theirs, mine)], axis=0
    )
    linear = jnp.where(trainer, state, trained)
    dense_linear, dense_sumsq, prior = ftrl_step(linear, squares, summed, DENSE_SHRINK)
    fresh = ftrl_weight(dense_linear, dense_sumsq, DENSE_SHRINK)
    weights = jnp.where(trainer, fresh, state + (fresh - prior)).astype(jnp.bfloat16)
    gathered = exchange(
        jnp.broadcast_to(weights, (Z_SIZE,) + weights.shape), "shard", Z_GROUPS
    ).reshape(Z_SIZE * piece, half)
    own = [gathered]
    for steps in range(1, Y_SIZE):
        own.append(along(gathered, "shard", functools.partial(ahead_in_y, steps=steps)))
    other = [along(block, "shard", lambda s: s ^ 1) for block in own]
    return own + other


def on_device(
    tables,
    row_squares,
    update_slots,
    update_counts,
    row_grads,
    dense_state,
    dense_squares,
    dense_grads,
    cross_bias,
    out_weight,
    cand_owner,
    cand_slot,
):
    role = lax.axis_index("role")
    shard = lax.axis_index("shard")
    fields = cand_owner.shape[2]
    requests, places = route(cand_owner[0].T, cand_slot[0].T)
    asked = exchange(requests, "shard", None)
    slots = update_slots.reshape(1, -1)
    new_linear, weights, fresh = train_rows(
        update_counts, slots, tables[0], row_squares, row_grads
    )
    arrived = lax.ppermute(fresh, "role", [(0, 1)])
    table_result, lookup = serve_rows(
        role.reshape(1), update_counts, slots, arrived, tables[0], new_linear, weights
    )
    blocks = fresh_weight_blocks(role, shard, dense_state[0], dense_squares, dense_grads[0])
    answers = answer_rows(asked, lookup)
    answered = exchange(answers.reshape(SHARDS, CAP, LANES), "shard", None)
    base = arrange_rows(places, answered.reshape(SHARDS * CAP, LANES), fields)
    where = jnp.stack([(shard // (X_SIZE * CORES)) % Y_SIZE, shard % CORES]).astype(jnp.int32)
    scores = cross_scores(where, base, cross_bias, out_weight.reshape(1, -1), blocks)
    return (table_result[None], scores[:1])


def solution(mesh):
    return jax.shard_map(
        on_device,
        mesh=mesh,
        in_specs=(
            P("role", "shard", None),
            P("shard", None),
            P("shard"),
            P("shard"),
            P("shard", None),
            P("role", None, None, None),
            P(),
            P("shard", None, None, None),
            P(),
            P(),
            P("role", "shard", None),
            P("role", "shard", None),
        ),
        out_specs=(P("role", "shard", None), P("role", "shard")),
        check_vma=False,
    )
```

time: 1460 us -> 139 us (0.10)
  waiting for transfers between devices: 1310 us -> 62.8 us
  local copies, waits for them, and re-layouts: 74.3 us -> 4.65 us
  other arithmetic: 32.2 us -> 3.21 us
  Pallas kernels: 0 us -> 19.9 us
  starting transfers between devices: 26.5 us -> 46.3 us
    psum x1 -> x0, waiting for transfers between devices: 1220 us -> none  [on_device(): summed = lax.psum(dense_grads[0], 'shard')]
    gather x6 -> x0, local copies, waits for them, and re-layouts: 52.5 us -> none  [the longest x1 14.9 us: on_device(): lookup_table[lax.all_to_all(requests, 'shard', split_axis=0, concat_axis=...]
    ppermute x2 -> x13, waiting for transfers between devices: 61.3 us -> 25 us  [the longest x11 19.7 us: along(): lax.ppermute(value, axis, [(source, partner(source)) for source in range(...]
    pallas_call x0 -> x6, Pallas kernels: none -> 19.9 us  [the longest x1 5.82 us: answer_rows(): kernel_call(answer_body, jax.ShapeDtypeStruct((shards * capacity, width),...]
    all_to_all x2 -> x4, starting transfers between devices: 23.8 us -> 34.8 us  [exchange(): lax.all_to_all(value, axis, split_axis=0, concat_axis=0, tiled=True, axis...]
    all_to_all x2 -> x4, waiting for transfers between devices: 29.4 us -> 37.8 us  [exchange(): lax.all_to_all(value, axis, split_axis=0, concat_axis=0, tiled=True, axis...]
  transfers between devices with their start and end apart: 5 -> 17, of which waited for: 3 -> 8; matrix products, arithmetic and copies ran while one was open for 7% -> 2% of each run, Pallas kernels for 0% -> 13%
where the time goes in v1:
time: 139 us
  waiting for transfers between devices  62.8 us (45%)
  starting transfers between devices  46.3 us (33%)
  Pallas kernels  19.9 us (14%)
  local copies, waits for them, and re-layouts  4.65 us (3%)
  other arithmetic  3.21 us (2%)
  between operations  1.58 us (1%)
    all_to_all x4, waiting for transfers between devices, exchange(): lax.all_to_all(value, axis, split_axis=0, concat_axis=0, tiled=True, axis...  37.8 us
    all_to_all x4, starting transfers between devices, exchange(): lax.all_to_all(value, axis, split_axis=0, concat_axis=0, tiled=True, axis...  34.8 us
    ppermute x11, waiting for transfers between devices, along(): lax.ppermute(value, axis, [(source, partner(source)) for source in range(...  19.7 us
    ppermute x11, starting transfers between devices, along(): lax.ppermute(value, axis, [(source, partner(source)) for source in range(...  8.94 us
    pallas_call x1, Pallas kernels, answer_rows(): kernel_call(answer_body, jax.ShapeDtypeStruct((shards * capacity, width),...  5.82 us
    ppermute x1, waiting for transfers between devices, fresh_weight_blocks(): trained = lax.ppermute(state, 'role', [(0, 1)])  5.3 us
    pallas_call x1, Pallas kernels, arrange_rows(): kernel_call(arrange_body, jax.ShapeDtypeStruct((examples, fields * width)...  4.79 us
    pallas_call x1, Pallas kernels, train_rows(): kernel_call(train_body, (jax.ShapeDtypeStruct((rows, width), jnp.float32)...  3.76 us
  transfers between devices with their start and end apart: 17, of which 8 were waited for; matrix products, arithmetic and copies ran while one was open for 2% of the time, Pallas kernels for 13%

profile of v1, /device:TPU:2, one launch (start us, length us, event | category | flops | bytes accessed | tf_op | source)
XLA Modules:
  0.0 138.5 jit_solution(9133807803098910942)
XLA Ops:
  0.7 1.3 dynamic-slice_bitcast_fusion
  2.1 2.3 %collective-permute-done.2 = f32[32,24,256]{2,1,0:T(8,128)S(1)} collective-permute-done((f32[32,24,256]{2,1,0:T(8,128)S(1)}, f32[32,24,256]{2,1,0:T(8,128)S(1)}, u32[]{:S(2)}, u32[]{:S(2)}) %collective-permute-start.2) | collective-permute-done | bytes 786464 | tf_op jit(solution)/shard_map/ppermute | solution.py:343
  4.4 2.2 %bitcast_add_fusion = f32[32,24,256]{2,1,0:T(8,128)} fusion(f32[32,24,256]{2,1,0:T(8,128)S(1)} %collective-permute-done.2, f32[32,2,24,512]{3,2,1,0:T(8,128)} %bitcast.42, s32[]{:T(128)S(6)} %select_n.72, s32[]{:T(128)S(6)} %select_n.69), kind=kLoop, calls=%fused_computation | loop fusion | flops 196608 | bytes 2359304 | tf_op jit(solution)/shard_map/add | solution.py:396
  6.5 11.6 %all-to-all-start.2 = ((f32[32,24,256]{2,1,0:T(8,128)}), f32[32,24,256]{2,1,0:T(8,128)S(1)}, u32[]{:S(2)}, u32[]{:S(2)}) async-start(f32[32,24,256]{2,1,0:T(8,128)} %bitcast_add_fusion), calls=%async_computation.2 | async-start | bytes 1572864 | tf_op jit(solution)/shard_map/all_to_all | solution.py:366
  18.8 22.2 %all-to-all-done.2 = f32[32,24,256]{2,1,0:T(8,128)S(1)} async-done(((f32[32,24,256]{2,1,0:T(8,128)}), f32[32,24,256]{2,1,0:T(8,128)S(1)}, u32[]{:S(2)}, u32[]{:S(2)}) %all-to-all-start.2) | async-done | bytes 786464 | tf_op jit(solution)/shard_map/all_to_all | solution.py:366
  41.7 2.2 %collective-permute-start.5 = (f32[24,256]{1,0:T(8,128)S(1)}, f32[24,256]{1,0:T(8,128)S(1)}, u32[]{:S(2)}, u32[]{:S(2)}) collective-permute-start(f32[24,256]{1,0:T(8,128)S(1)} %reduce_sum.9), channel_id=1, source_target_pairs={{0,130},{1,131},{2,128},{3,129},{4,134},{5,135},{6,132},{7,133},{8... | collective-permute-start | bytes 73736 | tf_op jit(solution)/shard_map/ppermute | solution.py:343
  43.9 1.4 %collective-permute-start.3 = (f32[24,256]{1,0:T(8,128)S(1)}, f32[24,256]{1,0:T(8,128)S(1)}, u32[]{:S(2)}, u32[]{:S(2)}) collective-permute-start(f32[24,256]{1,0:T(8,128)S(1)} %reduce_sum.9), channel_id=1, source_target_pairs={{0,2},{1,3},{2,0},{3,1},{4,6},{5,7},{6,4},{7,5},{8,10},{9,11},{10,... | collective-permute-start | bytes 73736 | tf_op jit(solution)/shard_map/ppermute | solution.py:343
  46.5 3.8 %shard_map.131 = (f32[2048,128]{1,0:T(8,128)S(1)}, bf16[2048,128]{1,0:T(8,128)(2,1)S(1)}, bf16[512,128]{1,0:T(8,128)(2,1)S(1)}) custom-call(s32[1]{0:T(128)S(6)} %copy.15.count_ref, s32[1,512]{1,0:T(1,128)S(1)} %bitcast.36, f32[2048,128]{1,0:T(8,128)S(1)} %bitcast.27, f32[2048,128]{1,0:T(8,128)S(1)} %copy-done.2, f32[512,128]{1,0:T(8,128)S(1)} %copy-done.3), custom_call_target="tpu_custom_call" | custom-call | flops 1073741824 | bytes 8000000 | tf_op jit(solution)/shard_map/pallas_call | solution.py:150
  50.3 1.3 collective-permute-start
  51.6 1.9 %shard_map.133 = (s32[128,32]{1,0:T(8,128)}, s32[8,512]{1,0:T(8,128)S(1)}) custom-call(s32[4,512]{1,0:T(4,128)S(1)} %bitcast.38, s32[4,512]{1,0:T(4,128)S(1)} %bitcast.39), custom_call_target="tpu_custom_call" | custom-call | flops 10000000 | bytes 100000 | tf_op jit(solution)/shard_map/pallas_call | solution.py:92
  53.5 8.9 %all-to-all-start = ((s32[128,1,32]{2,1,0:T(1,128)}), s32[128,1,32]{2,1,0:T(1,128)S(1)}, u32[]{:S(2)}, u32[]{:S(2)}) async-start(s32[128,1,32]{2,1,0:T(1,128)} %bitcast.11), calls=%async_computation | async-start | bytes 131072 | tf_op jit(solution)/shard_map/all_to_all | solution.py:366
  64.7 5.3 %collective-permute-done.1 = f32[48,256]{1,0:T(8,128)S(1)} collective-permute-done((f32[48,256]{1,0:T(8,128)S(1)}, f32[48,256]{1,0:T(8,128)S(1)}, u32[]{:S(2)}, u32[]{:S(2)}) %collective-permute-start.1) | collective-permute-done | bytes 49184 | tf_op jit(solution)/shard_map/ppermute | solution.py:387
  70.9 3.5 %all-to-all-done = s32[128,1,32]{2,1,0:T(1,128)S(1)} async-done(((s32[128,1,32]{2,1,0:T(1,128)}), s32[128,1,32]{2,1,0:T(1,128)S(1)}, u32[]{:S(2)}, u32[]{:S(2)}) %all-to-all-start) | async-done | bytes 16416 | tf_op jit(solution)/shard_map/all_to_all | solution.py:366
  75.0 3.6 %all-to-all-start.3 = ((bf16[8,48,256]{2,1,0:T(8,128)(2,1)}), bf16[8,48,256]{2,1,0:T(8,128)(2,1)S(1)}, u32[]{:S(2)}, u32[]{:S(2)}) async-start(bf16[8,48,256]{2,1,0:T(8,128)(2,1)} %broadcast_in_dim.7), calls=%async_computation.3 | async-start | bytes 393216 | tf_op jit(solution)/shard_map/all_to_all | solution.py:366
  78.6 1.7 %shard_map.132 = (f32[2048,128]{1,0:T(8,128)}, bf16[2048,128]{1,0:T(8,128)(2,1)S(1)}) custom-call(s32[1]{0:T(128)} %bitcast.role_ref, s32[1]{0:T(128)S(6)} %copy.15.count_ref, s32[1,512]{1,0:T(1,128)S(1)} %bitcast.37, bf16[512,128]{1,0:T(8,128)(2,1)S(1)} %collective-permute-done.arrived_ref, f32[2048,128]{1,0:T(8,128)S(1)} %bitcast.28, ...), custom_call_target="tpu_custom_call" | custom-call | flops 536870912 | bytes 5000000 | tf_op jit(solution)/shard_map/pallas_call | solution.py:203
  80.3 5.8 %shard_map.134 = bf16[4096,128]{1,0:T(8,128)(2,1)} custom-call(s32[128,32]{1,0:T(8,128)S(1)} %bitcast.35, bf16[2048,128]{1,0:T(8,128)(2,1)S(1)} %get-tuple-element.15.table_ref), custom_call_target="tpu_custom_call" | custom-call | flops 2147483648 | bytes 2000000 | tf_op jit(solution)/shard_map/pallas_call | solution.py:261
  86.2 2.5 %all-to-all-done.3 = bf16[8,48,256]{2,1,0:T(8,128)(2,1)S(1)} async-done(((bf16[8,48,256]{2,1,0:T(8,128)(2,1)}), bf16[8,48,256]{2,1,0:T(8,128)(2,1)S(1)}, u32[]{:S(2)}, u32[]{:S(2)}) %all-to-all-start.3) | async-done | bytes 196640 | tf_op jit(solution)/shard_map/all_to_all | solution.py:366
  88.7 10.7 %all-to-all-start.1 = ((bf16[128,32,128]{2,1,0:T(8,128)(2,1)}), bf16[128,32,128]{2,1,0:T(8,128)(2,1)S(1)}, u32[]{:S(2)}, u32[]{:S(2)}) async-start(bf16[128,32,128]{2,1,0:T(8,128)(2,1)} %bitcast.13), calls=%async_computation.1 | async-start | bytes 2097152 | tf_op jit(solution)/shard_map/all_to_all | solution.py:366
  99.4 2.4 %collective-permute-start.6 = (bf16[384,256]{1,0:T(8,128)(2,1)S(1)}, bf16[384,256]{1,0:T(8,128)(2,1)S(1)}, u32[]{:S(2)}, u32[]{:S(2)}) collective-permute-start(bf16[384,256]{1,0:T(8,128)(2,1)S(1)} %bitcast.30), channel_id=1, source_target_pairs={{0,12},{1,13},{2,14},{3,15},{4,0},{5,1},{6,2},{7,3},{8,4},{9,5},{1... | collective-permute-start | bytes 589832 | tf_op jit(solution)/shard_map/ppermute | solution.py:343
  103.6 12.4 %collective-permute-done.6.refs_1_ = bf16[384,256]{1,0:T(8,128)(2,1)S(1)} collective-permute-done((bf16[384,256]{1,0:T(8,128)(2,1)S(1)}, bf16[384,256]{1,0:T(8,128)(2,1)S(1)}, u32[]{:S(2)}, u32[]{:S(2)}) %collective-permute-start.6) | collective-permute-done | bytes 196640 | tf_op jit(solution)/shard_map/ppermute | solution.py:343
  116.5 5.0 %collective-permute-done.8.refs_3_ = bf16[384,256]{1,0:T(8,128)(2,1)S(1)} collective-permute-done((bf16[384,256]{1,0:T(8,128)(2,1)S(1)}, bf16[384,256]{1,0:T(8,128)(2,1)S(1)}, u32[]{:S(2)}, u32[]{:S(2)}) %collective-permute-start.8) | collective-permute-done | bytes 196640 | tf_op jit(solution)/shard_map/ppermute | solution.py:343
  121.6 9.6 %all-to-all-done.1 = bf16[128,32,128]{2,1,0:T(8,128)(2,1)S(1)} async-done(((bf16[128,32,128]{2,1,0:T(8,128)(2,1)}), bf16[128,32,128]{2,1,0:T(8,128)(2,1)S(1)}, u32[]{:S(2)}, u32[]{:S(2)}) %all-to-all-start.1) | async-done | bytes 1048608 | tf_op jit(solution)/shard_map/all_to_all | solution.py:366
  131.2 4.8 %shard_map.135.base_ref = bf16[512,512]{1,0:T(8,128)(2,1)S(1)} custom-call(s32[8,512]{1,0:T(8,128)S(1)} %get-tuple-element.13.place_ref, bf16[4096,128]{1,0:T(8,128)(2,1)S(1)} %bitcast.29), custom_call_target="tpu_custom_call" | custom-call | flops 2147483648 | bytes 2000000 | tf_op jit(solution)/shard_map/pallas_call | solution.py:291
  136.0 1.9 %shard_map.136 = f32[8,512]{1,0:T(8,128)S(1)} custom-call(s32[2]{0:T(128)S(1)} %pad_add_fusion.where_ref, bf16[512,512]{1,0:T(8,128)(2,1)S(1)} %shard_map.135.base_ref, f32[3,512]{1,0:T(4,128)S(1)} %copy-done.6, f32[1,512]{1,0:T(1,128)S(1)} %bitcast.40, bf16[384,256]{1,0:T(8,128)(2,1)S(1)} %bitcast.34, bf16[384,256]{1,0:T(8,128)(2,1)S(1)} %collective-permute-done.6.refs_1_, ...), custom_call_target="tpu_custom_call" | custom-call | flops 805306368 | bytes 3000000 | tf_op jit(solution)/shard_map/pallas_call | solution.py:330
  (41 shorter events, 8.6 us)
Async XLA Ops:
  0.6 44.6 %copy-start = (f32[1,2048,128]{2,1,0:T(8,128)S(1)}, f32[1,2048,128]{2,1,0:T(8,128)}, u32[]{:S(2)}) copy-start(f32[1,2048,128]{2,1,0:T(8,128)} %param.12) | copy-start | bytes 3145732
  0.7 44.6 %copy-start.1 = (s32[512]{0:T(512)S(1)}, s32[512]{0:T(512)}, u32[]{:S(2)}) copy-start(s32[512]{0:T(512)} %param.14) | copy-start | bytes 6148
  0.7 44.6 %copy-start.3 = (f32[512,128]{1,0:T(8,128)S(1)}, f32[512,128]{1,0:T(8,128)}, u32[]{:S(2)}) copy-start(f32[512,128]{1,0:T(8,128)} %grad_ref.1) | copy-start | bytes 786436
  2.0 2.4 %collective-permute-start.2 = (f32[32,24,256]{2,1,0:T(8,128)S(1)}, f32[32,24,256]{2,1,0:T(8,128)S(1)}, u32[]{:S(2)}, u32[]{:S(2)}) collective-permute-start(f32[32,24,256]{2,1,0:T(8,128)S(1)} %dynamic-slice_bitcast_fusion), channel_id=1, source_target_pairs={{0,1},{1,0},{2,3},{3,2},{4,5},{5,4},{6,7},{7,6},{8,9},{9,8},{10,11... | collective-permute-start | bytes 2359304 | tf_op jit(solution)/shard_map/ppermute | solution.py:343
  6.5 45.1 %copy-start.4 = (s32[1,512,4]{1,2,0:T(4,128)S(1)}, s32[1,512,4]{1,2,0:T(4,128)}, u32[]{:S(2)}) copy-start(s32[1,512,4]{1,2,0:T(4,128)} %param.22) | copy-start | bytes 24580
  6.5 45.1 %copy-start.5 = (s32[1,512,4]{1,2,0:T(4,128)S(1)}, s32[1,512,4]{1,2,0:T(4,128)}, u32[]{:S(2)}) copy-start(s32[1,512,4]{1,2,0:T(4,128)} %param.23) | copy-start | bytes 24580
  6.5 34.5 %all-to-all-start.2 = ((f32[32,24,256]{2,1,0:T(8,128)}), f32[32,24,256]{2,1,0:T(8,128)S(1)}, u32[]{:S(2)}, u32[]{:S(2)}) async-start(f32[32,24,256]{2,1,0:T(8,128)} %bitcast_add_fusion), calls=%async_computation.2 | async-start | bytes 1572864 | tf_op jit(solution)/shard_map/all_to_all | solution.py:366
  41.1 23.5 %collective-permute-start.4 = (f32[24,256]{1,0:T(8,128)S(1)}, f32[24,256]{1,0:T(8,128)S(1)}, u32[]{:S(2)}, u32[]{:S(2)}) collective-permute-start(f32[24,256]{1,0:T(8,128)S(1)} %reduce_sum.9), channel_id=1, source_target_pairs={{0,128},{1,129},{2,130},{3,131},{4,132},{5,133},{6,134},{7,135},{8... | collective-permute-start | bytes 73736 | tf_op jit(solution)/shard_map/ppermute | solution.py:343
  41.7 22.9 %collective-permute-start.5 = (f32[24,256]{1,0:T(8,128)S(1)}, f32[24,256]{1,0:T(8,128)S(1)}, u32[]{:S(2)}, u32[]{:S(2)}) collective-permute-start(f32[24,256]{1,0:T(8,128)S(1)} %reduce_sum.9), channel_id=1, source_target_pairs={{0,130},{1,131},{2,128},{3,129},{4,134},{5,135},{6,132},{7,133},{8... | collective-permute-start | bytes 73736 | tf_op jit(solution)/shard_map/ppermute | solution.py:343
  43.9 20.8 %collective-permute-start.3 = (f32[24,256]{1,0:T(8,128)S(1)}, f32[24,256]{1,0:T(8,128)S(1)}, u32[]{:S(2)}, u32[]{:S(2)}) collective-permute-start(f32[24,256]{1,0:T(8,128)S(1)} %reduce_sum.9), channel_id=1, source_target_pairs={{0,2},{1,3},{2,0},{3,1},{4,6},{5,7},{6,4},{7,5},{8,10},{9,11},{10,... | collective-permute-start | bytes 73736 | tf_op jit(solution)/shard_map/ppermute | solution.py:343
  50.3 28.3 %collective-permute-start = (bf16[512,128]{1,0:T(8,128)(2,1)S(1)}, bf16[512,128]{1,0:T(8,128)(2,1)S(1)}, u32[]{:S(2)}, u32[]{:S(2)}) collective-permute-start(bf16[512,128]{1,0:T(8,128)(2,1)S(1)} %get-tuple-element.9), channel_id=1, source_target_pairs={{0,128},{1,129},{2,130},{3,131},{4,132},{5,133},{6,134},{7,135},{8... | collective-permute-start | bytes 393224 | tf_op jit(solution)/shard_map/ppermute | solution.py:447
  53.5 20.8 %all-to-all-start = ((s32[128,1,32]{2,1,0:T(1,128)}), s32[128,1,32]{2,1,0:T(1,128)S(1)}, u32[]{:S(2)}, u32[]{:S(2)}) async-start(s32[128,1,32]{2,1,0:T(1,128)} %bitcast.11), calls=%async_computation | async-start | bytes 131072 | tf_op jit(solution)/shard_map/all_to_all | solution.py:366
  63.3 6.6 %collective-permute-start.1 = (f32[48,256]{1,0:T(8,128)S(1)}, f32[48,256]{1,0:T(8,128)S(1)}, u32[]{:S(2)}, u32[]{:S(2)}) collective-permute-start(f32[48,256]{1,0:T(8,128)S(1)} %dynamic_slice.12), channel_id=1, source_target_pairs={{0,128},{1,129},{2,130},{3,131},{4,132},{5,133},{6,134},{7,135},{8... | collective-permute-start | bytes 147464 | tf_op jit(solution)/shard_map/ppermute | solution.py:387
  75.0 13.7 %all-to-all-start.3 = ((bf16[8,48,256]{2,1,0:T(8,128)(2,1)}), bf16[8,48,256]{2,1,0:T(8,128)(2,1)S(1)}, u32[]{:S(2)}, u32[]{:S(2)}) async-start(bf16[8,48,256]{2,1,0:T(8,128)(2,1)} %broadcast_in_dim.7), calls=%async_computation.3 | async-start | bytes 393216 | tf_op jit(solution)/shard_map/all_to_all | solution.py:366
  88.7 42.5 %all-to-all-start.1 = ((bf16[128,32,128]{2,1,0:T(8,128)(2,1)}), bf16[128,32,128]{2,1,0:T(8,128)(2,1)S(1)}, u32[]{:S(2)}, u32[]{:S(2)}) async-start(bf16[128,32,128]{2,1,0:T(8,128)(2,1)} %bitcast.13), calls=%async_computation.1 | async-start | bytes 2097152 | tf_op jit(solution)/shard_map/all_to_all | solution.py:366
  99.4 16.6 %collective-permute-start.6 = (bf16[384,256]{1,0:T(8,128)(2,1)S(1)}, bf16[384,256]{1,0:T(8,128)(2,1)S(1)}, u32[]{:S(2)}, u32[]{:S(2)}) collective-permute-start(bf16[384,256]{1,0:T(8,128)(2,1)S(1)} %bitcast.30), channel_id=1, source_target_pairs={{0,12},{1,13},{2,14},{3,15},{4,0},{5,1},{6,2},{7,3},{8,4},{9,5},{1... | collective-permute-start | bytes 589832 | tf_op jit(solution)/shard_map/ppermute | solution.py:343
  101.8 14.2 %collective-permute-start.7 = (bf16[384,256]{1,0:T(8,128)(2,1)S(1)}, bf16[384,256]{1,0:T(8,128)(2,1)S(1)}, u32[]{:S(2)}, u32[]{:S(2)}) collective-permute-start(bf16[384,256]{1,0:T(8,128)(2,1)S(1)} %bitcast.31), channel_id=1, source_target_pairs={{0,8},{1,9},{2,10},{3,11},{4,12},{5,13},{6,14},{7,15},{8,0},{9,1},... | collective-permute-start | bytes 589832 | tf_op jit(solution)/shard_map/ppermute | solution.py:343
  102.7 18.9 %collective-permute-start.8 = (bf16[384,256]{1,0:T(8,128)(2,1)S(1)}, bf16[384,256]{1,0:T(8,128)(2,1)S(1)}, u32[]{:S(2)}, u32[]{:S(2)}) collective-permute-start(bf16[384,256]{1,0:T(8,128)(2,1)S(1)} %bitcast.32), channel_id=1, source_target_pairs={{0,4},{1,5},{2,6},{3,7},{4,8},{5,9},{6,10},{7,11},{8,12},{9,13},{1... | collective-permute-start | bytes 589832 | tf_op jit(solution)/shard_map/ppermute | solution.py:343
  103.6 32.4 %collective-permute-start.9 = (bf16[384,256]{1,0:T(8,128)(2,1)S(1)}, bf16[384,256]{1,0:T(8,128)(2,1)S(1)}, u32[]{:S(2)}, u32[]{:S(2)}) collective-permute-start(bf16[384,256]{1,0:T(8,128)(2,1)S(1)} %bitcast.33), channel_id=1, source_target_pairs={{0,1},{1,0},{2,3},{3,2},{4,5},{5,4},{6,7},{7,6},{8,9},{9,8},{10,11... | collective-permute-start | bytes 589832 | tf_op jit(solution)/shard_map/ppermute | solution.py:343
  116.0 20.0 %collective-permute-start.10 = (bf16[384,256]{1,0:T(8,128)(2,1)S(1)}, bf16[384,256]{1,0:T(8,128)(2,1)S(1)}, u32[]{:S(2)}, u32[]{:S(2)}) collective-permute-start(bf16[384,256]{1,0:T(8,128)(2,1)S(1)} %collective-permute-done.6.refs_1_), channel_id=1, source_target_pairs={{0,1},{1,0},{2,3},{3,2},{4,5},{5,4},{6,7},{7,6},{8,9},{9,8},{10,11... | collective-permute-start | bytes 589832 | tf_op jit(solution)/shard_map/ppermute | solution.py:343
  116.0 20.0 %collective-permute-start.11 = (bf16[384,256]{1,0:T(8,128)(2,1)S(1)}, bf16[384,256]{1,0:T(8,128)(2,1)S(1)}, u32[]{:S(2)}, u32[]{:S(2)}) collective-permute-start(bf16[384,256]{1,0:T(8,128)(2,1)S(1)} %collective-permute-done.7.refs_2_), channel_id=1, source_target_pairs={{0,1},{1,0},{2,3},{3,2},{4,5},{5,4},{6,7},{7,6},{8,9},{9,8},{10,11... | collective-permute-start | bytes 589832 | tf_op jit(solution)/shard_map/ppermute | solution.py:343
  121.6 14.4 %collective-permute-start.12 = (bf16[384,256]{1,0:T(8,128)(2,1)S(1)}, bf16[384,256]{1,0:T(8,128)(2,1)S(1)}, u32[]{:S(2)}, u32[]{:S(2)}) collective-permute-start(bf16[384,256]{1,0:T(8,128)(2,1)S(1)} %collective-permute-done.8.refs_3_), channel_id=1, source_target_pairs={{0,1},{1,0},{2,3},{3,2},{4,5},{5,4},{6,7},{7,6},{8,9},{9,8},{10,11... | collective-permute-start | bytes 589832 | tf_op jit(solution)/shard_map/ppermute | solution.py:343
  131.2 4.8 %copy-start.6 = (f32[3,512]{1,0:T(4,128)S(1)}, f32[3,512]{1,0:T(4,128)}, u32[]{:S(2)}) copy-start(f32[3,512]{1,0:T(4,128)} %bias_ref.1) | copy-start | bytes 18436
  131.2 4.8 %copy-start.7 = (f32[512]{0:T(512)S(1)}, f32[512]{0:T(512)}, u32[]{:S(2)}) copy-start(f32[512]{0:T(512)} %param.21) | copy-start | bytes 6148
  (1 other events, 1.2 us)

commit v2 on v1

v2 whole, which is shorter than its diff:
```python
import jax
import jax.numpy as jnp
from jax import lax
from jax.experimental import pallas as pl
from jax.experimental.pallas import tpu as pltpu
from jax.sharding import PartitionSpec as P

ROW_SHRINK = 0.25
DENSE_SHRINK = 0.05
CAP = 32
LANES = 128
SHARDS = 128
ROLES = 2
Z_SIZE, Y_SIZE, X_SIZE, CORES = 8, 4, 2, 2
PLANE = Y_SIZE * X_SIZE
NEAR = 4
ASKED = 8
VMEM_LIMIT = 40 * 1024 * 1024


def ftrl_weight(linear, squares, shrink):
    return -(linear - jnp.clip(linear, -shrink, shrink)) / (1.0 + jnp.sqrt(squares))


def ftrl_step(linear, squares, gradient, shrink):
    prior = ftrl_weight(linear, squares, shrink)
    fresh_squares = squares + gradient * gradient
    sigma_step = jnp.sqrt(fresh_squares) - jnp.sqrt(squares)
    return (linear + gradient - sigma_step * prior, fresh_squares, prior)


def iota(shape, dim):
    return lax.broadcasted_iota(jnp.int32, shape, dim)


def kernel_call(body, out_shape, flops=0, bytes_accessed=0, vmem=VMEM_LIMIT, **options):
    return pl.pallas_call(
        body,
        out_shape=out_shape,
        compiler_params=pltpu.CompilerParams(vmem_limit_bytes=vmem),
        cost_estimate=pl.CostEstimate(
            flops=flops, bytes_accessed=bytes_accessed, transcendentals=0
        ),
        **options,
    )


VMEM = pl.BlockSpec(memory_space=pltpu.VMEM)
SMEM = pl.BlockSpec(memory_space=pltpu.SMEM)
ANY = pl.BlockSpec(memory_space=pl.ANY)


def position():
    shard = lax.axis_index("shard")
    core, plane = lax.rem(shard, CORES), lax.rem(shard // CORES, PLANE)
    return lax.axis_index("role"), shard, plane, core


def tile_copies(grad_ref, state_ref, square_ref, send_ref, keep_ref, own_state_ref, own_square_ref, arrived):
    role, _, plane, core = position()
    piece = own_state_ref.shape[1]
    share = piece // ROLES
    tiles = own_state_ref.shape[0]
    copies = []

    def copy(source, target):
        copies.append(pltpu.make_async_copy(source, target, arrived.at[len(copies)]))

    def columns(flip, tile):
        return pl.ds(pl.multiple_of(((core ^ flip) * tiles + tile) * LANES, LANES), LANES)

    for tile in range(tiles):
        for flip, target in ((1, send_ref), (0, keep_ref)):
            for at in range(PLANE):
                first = pl.multiple_of((plane ^ at) * piece + role * share, share)
                copy(
                    grad_ref.at[pl.ds(first, share), columns(flip, tile)],
                    target.at[at, pl.ds(tile * share, share)],
                )
        rows = pl.ds(pl.multiple_of(plane * piece, piece), piece)
        copy(state_ref.at[rows, columns(0, tile)], own_state_ref.at[tile])
        copy(square_ref.at[rows, columns(0, tile)], own_square_ref.at[tile])
    return copies


def front_body(owner_ref, slot_ref, grad_ref, state_ref, square_ref, place_ref, send_ref, keep_ref, own_state_ref, own_square_ref, arrived):
    copies = tile_copies(
        grad_ref, state_ref, square_ref, send_ref, keep_ref, own_state_ref, own_square_ref, arrived
    )
    for copy in copies:
        copy.start()
    _, shard, _, _ = position()
    fields, examples = owner_ref.shape
    shape = (SHARDS, examples)
    rows = iota(shape, 0)
    relative = owner_ref[...] ^ shard
    core, plane, z = relative & 1, (relative >> 1) & (PLANE - 1), relative >> 4
    order = (z >> 2) * 64 + core * 32 + plane * NEAR + (z & (NEAR - 1))
    member = jnp.zeros(shape, jnp.float32)
    wanted = jnp.zeros(shape, jnp.float32)
    for field in range(fields):
        named = order[field : field + 1, :] == rows
        member = jnp.where(named, 1.0, member)
        wanted = jnp.where(named, slot_ref[field : field + 1, :].astype(jnp.float32), wanted)
    earlier = jnp.where(iota((examples, examples), 0) < iota((examples, examples), 1), 1.0, 0.0)
    ranks = jnp.dot(
        member.astype(jnp.bfloat16),
        earlier.astype(jnp.bfloat16),
        preferred_element_type=jnp.float32,
    )
    places = []
    for field in range(fields):
        named = order[field : field + 1, :] == rows
        rank = jnp.sum(jnp.where(named, ranks, 0.0), axis=0, keepdims=True)
        places.append(owner_ref[field : field + 1, :] * CAP + rank.astype(jnp.int32))
    place_ref[...] = jnp.concatenate(
        places + [jnp.zeros((8 - fields, examples), jnp.int32)], axis=0
    )
    ranks = jnp.where(member > 0.5, ranks, -1.0)
    requests = jnp.zeros((SHARDS, LANES), jnp.float32)
    lanes = iota((SHARDS, LANES), 1)
    for rank in range(CAP):
        column = jnp.sum(
            jnp.where(ranks == float(rank), wanted, 0.0), axis=1, keepdims=True
        )
        requests = jnp.where(lanes == rank, column, requests)
    packed = jnp.concatenate(
        [requests[at : at + CAP, :CAP] for at in range(0, SHARDS, CAP)], axis=1
    )
    other_core = (iota(packed.shape, 1) & CAP) != 0
    dense = send_ref.shape[1] - ASKED
    for target, asked in (
        (send_ref, jnp.where(other_core, packed, 0.0)),
        (keep_ref, jnp.where(other_core, 0.0, packed)),
    ):
        for at in range(PLANE):
            target[at, dense:, :] = jnp.concatenate(
                [
                    asked[at * NEAR : (at + 1) * NEAR, :],
                    jnp.zeros((ASKED - NEAR, LANES), jnp.float32),
                ],
                axis=0,
            )
    for copy in copies:
        copy.wait()


def front(owners, slots, grads, state, squares):
    fields, examples = owners.shape
    rows, width = grads.shape
    piece, tiles = rows // PLANE, width // CORES // LANES
    blocks = jax.ShapeDtypeStruct(
        (PLANE, piece // ROLES * tiles + ASKED, LANES), jnp.float32
    )
    own = jax.ShapeDtypeStruct((tiles, piece, LANES), jnp.float32)
    return kernel_call(
        front_body,
        (jax.ShapeDtypeStruct((8, examples), jnp.int32), blocks, blocks, own, own),
        flops=10_000_000,
        bytes_accessed=4_000_000,
        vmem=60 * 1024 * 1024,
        in_specs=[VMEM, VMEM, ANY, ANY, ANY],
        out_specs=(VMEM,) * 5,
        scratch_shapes=[pltpu.SemaphoreType.DMA((tiles * (2 * PLANE + 2),))],
    )(owners, slots, grads, state, squares)


def pair_body(keep_ref, arrived_ref, *out_refs):
    for at, out_ref in enumerate(out_refs):
        out_ref[...] = keep_ref[at] + arrived_ref[at]


def pair_sums(keep, arrived):
    shape = jax.ShapeDtypeStruct(keep.shape[1:], keep.dtype)
    return kernel_call(
        pair_body, (shape,) * PLANE, in_specs=[VMEM] * 2, out_specs=(VMEM,) * PLANE
    )(keep, arrived)


def summed(refs, rows):
    values = [ref[:rows, :] for ref in refs]
    while len(values) > 1:
        values = [left + right for left, right in zip(values[::2], values[1::2])]
    return values[0]


def plane_body(*refs):
    in_refs, out_refs = refs[:PLANE], refs[PLANE:]
    dense = out_refs[0].shape[0] - ASKED
    total = summed(in_refs, dense)
    for z, out_ref in enumerate(out_refs):
        out_ref[:dense, :] = total
        out_ref[dense:, :] = jnp.concatenate(
            [ref[dense + z : dense + z + 1, :] for ref in in_refs], axis=0
        )


def plane_sums(parts):
    shape = jax.ShapeDtypeStruct(parts[0].shape, jnp.float32)
    return kernel_call(
        plane_body, (shape,) * NEAR, in_specs=[VMEM] * PLANE, out_specs=(VMEM,) * NEAR
    )(*parts)


def near_body(*refs):
    in_refs, (both_ref, dense_ref) = refs[:NEAR], refs[NEAR:]
    dense = dense_ref.shape[0]
    total = summed(in_refs, dense)
    dense_ref[...] = total
    both_ref[:dense, :] = total
    for z, ref in enumerate(in_refs):
        first = dense + z * ASKED
        both_ref[first : first + ASKED, :] = ref[dense:, :]


def near_sums(parts):
    rows = parts[0].shape[0] - ASKED
    return kernel_call(
        near_body,
        (
            jax.ShapeDtypeStruct((rows + NEAR * ASKED, LANES), jnp.float32),
            jax.ShapeDtypeStruct((rows, LANES), jnp.float32),
        ),
        in_specs=[VMEM] * NEAR,
        out_specs=(VMEM,) * 2,
    )(*parts)


def weight_body(own_ref, far_ref, other_ref, other_far_ref, state_ref, trained_ref, square_ref, out_ref):
    role = lax.axis_index("role")
    tiles, piece, _ = state_ref.shape
    share = piece // ROLES
    dense = tiles * share
    mine = own_ref[:dense, :] + far_ref[:dense, :]
    theirs = other_ref[...] + other_far_ref[...]
    parts = (jnp.where(role == 0, mine, theirs), jnp.where(role == 0, theirs, mine))
    for tile in range(tiles):
        gradient = jnp.concatenate(
            [part[tile * share : (tile + 1) * share, :] for part in parts], axis=0
        )
        state = state_ref[tile]
        linear = jnp.where(role == 0, state, trained_ref[tile * piece : (tile + 1) * piece, :])
        dense_linear, dense_sumsq, prior = ftrl_step(
            linear, square_ref[tile], gradient, DENSE_SHRINK
        )
        fresh = ftrl_weight(dense_linear, dense_sumsq, DENSE_SHRINK)
        weights = jnp.where(role == 0, fresh, state + (fresh - prior))
        out_ref[tile * piece : (tile + 1) * piece, :] = weights.astype(jnp.bfloat16)


def piece_weights(own, far, other, other_far, state, trained, squares):
    tiles, piece, _ = state.shape
    return kernel_call(
        weight_body,
        jax.ShapeDtypeStruct((tiles * piece, LANES), jnp.bfloat16),
        in_specs=[VMEM] * 7,
        out_specs=VMEM,
    )(own, far, other, other_far, state, trained, squares)


def used_slots(slot_ref, count):
    slots = slot_ref[...]
    return jnp.where(iota(slots.shape, 1) < count, slots, -1)


def rows_of_block(slots, first, rows):
    hit = slots == iota((rows, slots.shape[1]), 0) + first
    return jnp.where(hit, 1.0, 0.0).astype(jnp.bfloat16)


def train_body(count_ref, slot_ref, held_ref, square_ref, grad_ref, state_ref, new_ref, weight_ref, fresh_ref, parts, total):
    step = pl.program_id(0)
    rows = held_ref.shape[0]

    @pl.when(step == 0)
    def _():
        grads = grad_ref[...]
        high = grads.astype(jnp.bfloat16)
        rest = grads - high.astype(jnp.float32)
        middle = rest.astype(jnp.bfloat16)
        low = (rest - middle.astype(jnp.float32)).astype(jnp.bfloat16)
        parts[...] = jnp.concatenate([high, middle, low], axis=1)
        total[...] = jnp.zeros_like(total)

    spread = rows_of_block(used_slots(slot_ref, count_ref[0]), step * rows, rows)
    sums = jnp.dot(spread, parts[...], preferred_element_type=jnp.float32)
    gradient = (sums[:, :LANES] + sums[:, LANES : 2 * LANES]) + sums[:, 2 * LANES :]
    linear, squares, _ = ftrl_step(held_ref[...], square_ref[...], gradient, ROW_SHRINK)
    new_ref[...] = linear
    weights = ftrl_weight(linear, squares, ROW_SHRINK).astype(jnp.bfloat16)
    weight_ref[...] = weights
    total[...] += lax.dot_general(
        spread, weights, (((0,), (0,)), ((), ())), preferred_element_type=jnp.float32
    )

    @pl.when(step == pl.num_programs(0) - 1)
    def _():
        updates = total.shape[0]
        fresh_ref[:updates, :] = total[...]
        fresh_ref[updates:, :] = state_ref[...]


def train_rows(count, slots, held, squares, grads, state):
    rows, width = held.shape
    updates = grads.shape[0]
    block = 512
    by_rows = pl.BlockSpec((block, width), lambda i: (i, 0))
    return kernel_call(
        train_body,
        (
            jax.ShapeDtypeStruct((rows, width), jnp.float32),
            jax.ShapeDtypeStruct((rows, width), jnp.bfloat16),
            jax.ShapeDtypeStruct((updates + state.shape[0], width), jnp.float32),
        ),
        grid=(rows // block,),
        in_specs=[
            SMEM,
            pl.BlockSpec((1, updates), lambda i: (0, 0)),
            by_rows,
            by_rows,
            pl.BlockSpec((updates, width), lambda i: (0, 0)),
            pl.BlockSpec(state.shape, lambda i: (0, 0)),
        ],
        out_specs=(
            by_rows,
            by_rows,
            pl.BlockSpec((updates + state.shape[0], width), lambda i: (0, 0)),
        ),
        scratch_shapes=[
            pltpu.VMEM((updates, 3 * width), jnp.bfloat16),
            pltpu.VMEM((updates, width), jnp.float32),
        ],
    )(count, slots, held, squares, grads, state)


def serve_body(count_ref, slot_ref, arrived_ref, held_ref, new_ref, weight_ref, table_ref, lookup_ref):
    step = pl.program_id(0)
    rows = held_ref.shape[0]
    role = lax.axis_index("role")

    @pl.when(role == 0)
    def _():
        table_ref[...] = new_ref[...]
        lookup_ref[...] = weight_ref[...]

    @pl.when(role != 0)
    def _():
        spread = rows_of_block(used_slots(slot_ref, count_ref[0]), step * rows, rows)
        arrived = arrived_ref[: slot_ref.shape[1], :].astype(jnp.bfloat16)
        sums = jnp.dot(
            spread,
            jnp.concatenate([arrived, jnp.ones_like(arrived)], axis=1),
            preferred_element_type=jnp.float32,
        )
        table = jnp.where(sums[:, LANES:] > 0.5, sums[:, :LANES], held_ref[...])
        table_ref[...] = table
        lookup_ref[...] = table.astype(jnp.bfloat16)


def serve_rows(count, slots, arrived, held, new_linear, weights):
    rows, width = held.shape
    updates = slots.shape[1]
    block = 1024
    by_rows = pl.BlockSpec((block, width), lambda i: (i, 0))
    return kernel_call(
        serve_body,
        (
            jax.ShapeDtypeStruct((rows, width), jnp.float32),
            jax.ShapeDtypeStruct((rows, width), jnp.bfloat16),
        ),
        grid=(rows // block,),
        in_specs=[
            SMEM,
            pl.BlockSpec((1, updates), lambda i: (0, 0)),
            pl.BlockSpec((updates, width), lambda i: (0, 0)),
            by_rows,
            by_rows,
            by_rows,
        ],
        out_specs=(by_rows, by_rows),
    )(count, slots, arrived, held, new_linear, weights)


def looked_up(column, folded):
    rows, height = column.shape[0], folded.shape[0]
    spread = jnp.broadcast_to(column, (rows, LANES))
    within = jnp.where((spread & (LANES - 1)) == iota((rows, LANES), 1), 1.0, 0.0).astype(
        jnp.bfloat16
    )
    block = ((spread & (height - 1)) >> 7).astype(jnp.float32).astype(jnp.bfloat16)
    none = jnp.zeros_like(within)
    hot = jnp.concatenate(
        [jnp.where(block == jnp.bfloat16(at), within, none) for at in range(height // LANES)],
        axis=1,
    )
    both = jnp.dot(hot, folded, preferred_element_type=jnp.float32)
    return jnp.where(spread < height, both[:, :LANES], both[:, LANES:]).astype(jnp.bfloat16)


def fold(source_ref, target_ref):
    height = target_ref.shape[0]
    target_ref[:, :LANES] = source_ref[:height, :]
    target_ref[:, LANES:] = source_ref[height:, :]


def answer_body(near_ref, far_ref, table_ref, answer_ref, columns, folded):
    _, shard, _, _ = position()
    first = near_ref.shape[0] - NEAR * ASKED
    near, far = near_ref[first:, :], far_ref[first:, :]
    asked = jnp.where(iota(near.shape, 1) < LANES // 2, near, far)
    wide = jnp.concatenate([asked, jnp.zeros((LANES - asked.shape[0], LANES), jnp.float32)], axis=0)
    columns[...] = jnp.transpose(wide)[:, : asked.shape[0]].astype(jnp.int32)
    fold(table_ref, folded)
    for at in range(0, NEAR * PLANE, 2):
        found = looked_up(
            jnp.concatenate([columns[:, at : at + 1], columns[:, at + 1 : at + 2]], axis=0),
            folded[...],
        )
        for part in range(2 * LANES // CAP):
            row, lane = at + part // NEAR, part % NEAR
            z = (lane >> 1) * NEAR + row // PLANE
            relative = (z * PLANE + row % PLANE) * CORES + (lane & 1)
            to = pl.multiple_of((relative ^ shard) * CAP, CAP)
            answer_ref[pl.ds(to, CAP), :] = found[part * CAP : (part + 1) * CAP, :]


def answer_rows(near, far, table):
    rows, width = table.shape
    return kernel_call(
        answer_body,
        jax.ShapeDtypeStruct((SHARDS * CAP, width), jnp.bfloat16),
        flops=2 * SHARDS * CAP * rows * width,
        bytes_accessed=2_000_000,
        in_specs=[VMEM] * 3,
        out_specs=VMEM,
        scratch_shapes=[
            pltpu.VMEM((LANES, NEAR * PLANE), jnp.int32),
            pltpu.VMEM((rows // 2, 2 * width), jnp.bfloat16),
        ],
    )(near, far, table)


def arrange_body(place_ref, answer_ref, base_ref, columns, folded):
    columns[...] = jnp.transpose(place_ref[...])
    fold(answer_ref, folded)
    examples = columns.shape[0]
    block = 256
    for field in range(base_ref.shape[1] // LANES):
        for at in range(0, examples, block):
            base_ref[at : at + block, field * LANES : (field + 1) * LANES] = looked_up(
                columns[at : at + block, field : field + 1], folded[...]
            )


def arrange_rows(places, answers, fields):
    examples = places.shape[1]
    rows, width = answers.shape
    return kernel_call(
        arrange_body,
        jax.ShapeDtypeStruct((examples, fields * width), jnp.bfloat16),
        flops=2 * examples * fields * rows * width,
        bytes_accessed=2_000_000,
        in_specs=[VMEM, VMEM],
        out_specs=VMEM,
        scratch_shapes=[
            pltpu.VMEM((examples, 8), jnp.int32),
            pltpu.VMEM((rows // 2, 2 * width), jnp.bfloat16),
        ],
    )(places, answers)


def cross_body(base_ref, bias_ref, out_ref, *refs):
    block_refs, score_ref, weights = refs[:-2], refs[-2], refs[-1]
    _, _, plane, core = position()
    tiles = weights.shape[1] // LANES // CORES
    piece = block_refs[0].shape[0] // tiles
    for flip in range(CORES):
        for at in range(PLANE):
            block_ref = block_refs[flip * PLANE + at]
            first = pl.multiple_of((plane ^ at) * piece, piece)
            for tile in range(tiles):
                left = pl.multiple_of(((core ^ flip) * tiles + tile) * LANES, LANES)
                weights[pl.ds(first, piece), pl.ds(left, LANES)] = block_ref[
                    tile * piece : (tile + 1) * piece, :
                ]
    width = base_ref.shape[1]
    base = base_ref[...].astype(jnp.float32)
    crossed = base
    for layer in range(bias_ref.shape[0]):
        mixed = jnp.dot(
            crossed.astype(jnp.bfloat16),
            weights[layer * width : (layer + 1) * width, :],
            preferred_element_type=jnp.float32,
        )
        crossed = base * (mixed + bias_ref[layer : layer + 1, :]) + crossed
    scores = jnp.sum(crossed * out_ref[...], axis=1, keepdims=True)
    score_ref[...] = jnp.transpose(jnp.broadcast_to(scores, (scores.shape[0], LANES)))[:1, :]


def cross_scores(base, bias, out_weight, blocks):
    examples, width = base.shape
    layers = bias.shape[0]
    return kernel_call(
        cross_body,
        jax.ShapeDtypeStruct((1, examples), jnp.float32),
        flops=2 * examples * width * width * layers,
        bytes_accessed=3_000_000,
        in_specs=[VMEM] * (3 + len(blocks)),
        out_specs=VMEM,
        scratch_shapes=[pltpu.VMEM((layers * width, width), jnp.bfloat16)],
    )(base, bias, out_weight, *blocks)


BOTH = ("role", "shard")
CORE_BIT, PLANE_BIT, Z_BIT, FAR_BIT, ROLE_BIT = 1, 2, 16, 64, 128


def swapped(value, bits):
    count = ROLES * SHARDS
    return lax.ppermute(value, BOTH, [(source, source ^ bits) for source in range(count)])


def exchange(value):
    return lax.all_to_all(value, "shard", split_axis=0, concat_axis=0, tiled=True)


def on_device(
    tables,
    row_squares,
    update_slots,
    update_counts,
    row_grads,
    dense_state,
    dense_squares,
    dense_grads,
    cross_bias,
    out_weight,
    cand_owner,
    cand_slot,
):
    fields = cand_owner.shape[2]
    rows = dense_squares.shape[0] * dense_squares.shape[1]
    places, send, keep, own_state, own_squares = front(
        cand_owner[0].T,
        cand_slot[0].T,
        dense_grads[0].reshape(rows, -1),
        dense_state[0].reshape(rows, -1),
        dense_squares.reshape(rows, -1),
    )
    parts = pair_sums(keep, swapped(send, CORE_BIT))
    slots = update_slots.reshape(1, -1)
    new_linear, weights, fresh = train_rows(
        update_counts, slots, tables[0], row_squares, row_grads, own_state.reshape(-1, LANES)
    )
    arrived = lax.ppermute(fresh, "role", [(0, 1)])
    table_result, lookup = serve_rows(
        update_counts, slots, arrived, tables[0], new_linear, weights
    )
    parts = plane_sums(
        [parts[0]] + [swapped(parts[at], at * PLANE_BIT) for at in range(1, PLANE)]
    )
    both, dense = near_sums(
        [parts[0]] + [swapped(parts[z], z * Z_BIT) for z in range(1, NEAR)]
    )
    far = swapped(both, FAR_BIT)
    other, other_far = swapped(dense, ROLE_BIT), swapped(dense, ROLE_BIT + FAR_BIT)
    answers = answer_rows(both, far, lookup)
    answered = exchange(answers.reshape(SHARDS, CAP, LANES))
    piece = piece_weights(
        both, far, other, other_far, own_state, arrived[slots.shape[1] :], own_squares
    )
    blocks = [piece] + [swapped(piece, at * PLANE_BIT) for at in range(1, PLANE)]
    blocks = blocks + [swapped(block, CORE_BIT) for block in blocks]
    base = arrange_rows(places, answered.reshape(SHARDS * CAP, LANES), fields)
    scores = cross_scores(base, cross_bias, out_weight.reshape(1, -1), blocks)
    return (table_result[None], scores)


def solution(mesh):
    return jax.shard_map(
        on_device,
        mesh=mesh,
        in_specs=(
            P("role", "shard", None),
            P("shard", None),
            P("shard"),
            P("shard"),
            P("shard", None),
            P("role", None, None, None),
            P(),
            P("shard", None, None, None),
            P(),
            P(),
            P("role", "shard", None),
            P("role", "shard", None),
        ),
        out_specs=(P("role", "shard", None), P("role", "shard")),
        check_vma=False,
    )
```

time: 139 us -> 143 us (1.029)
  starting transfers between devices: 46.3 us -> 74.4 us
  waiting for transfers between devices: 62.8 us -> 43.4 us
  other arithmetic: 3.21 us -> 0 us
  local copies, waits for them, and re-layouts: 4.65 us -> 2.11 us
    ppermute x12 -> x29, starting transfers between devices: 10.2 us -> 59.7 us  [swapped(): lax.ppermute(value, BOTH, [(source, source ^ bits) for source in range(co...]
    all_to_all x4 -> x1, waiting for transfers between devices: 37.8 us -> 0.01 us  [exchange(): lax.all_to_all(value, 'shard', split_axis=0, concat_axis=0, tiled=True)]
    all_to_all x4 -> x1, starting transfers between devices: 34.8 us -> 13.4 us  [exchange(): lax.all_to_all(value, 'shard', split_axis=0, concat_axis=0, tiled=True)]
    ppermute x12 -> x29, waiting for transfers between devices: 25 us -> 43.4 us  [swapped(): lax.ppermute(value, BOTH, [(source, source ^ bits) for source in range(co...]
    pallas_call x1, Pallas kernels: 4.79 us -> 2.59 us  [arrange_rows(): kernel_call(arrange_body, jax.ShapeDtypeStruct((examples, fields * width)...]
    add x1 -> x0, other arithmetic: 2.17 us -> none  [fresh_weight_blocks(): pair = half_of(core) + along(half_of(1 - core), 'shard', lambda s: s ^ 1)]
    pallas_call x3 -> x7, Pallas kernels: 9.61 us -> 11.7 us  [the longest x1 5.32 us: front(): kernel_call(front_body, (jax.ShapeDtypeStruct((8, examples), jnp.int32),...]
  transfers between devices with their start and end apart: 17 -> 31, of which waited for: 8 -> 11; matrix products, arithmetic and copies ran while one was open for 2% -> 0% of each run, Pallas kernels for 13% -> 6%
where the time goes in v2:
time: 143 us; the launch traced here: 141 us
  starting transfers between devices  74.4 us (52%)
  waiting for transfers between devices  43.4 us (30%)
  Pallas kernels  19.8 us (14%)
  local copies, waits for them, and re-layouts  2.11 us (1%)
  between operations  1.53 us (1%)
    ppermute x29, starting transfers between devices, swapped(): lax.ppermute(value, BOTH, [(source, source ^ bits) for source in range(co...  59.7 us
    ppermute x29, waiting for transfers between devices, swapped(): lax.ppermute(value, BOTH, [(source, source ^ bits) for source in range(co...  43.4 us
    all_to_all x1, starting transfers between devices, exchange(): lax.all_to_all(value, 'shard', split_axis=0, concat_axis=0, tiled=True)  13.4 us
    pallas_call x1, Pallas kernels, front(): kernel_call(front_body, (jax.ShapeDtypeStruct((8, examples), jnp.int32),...  5.32 us
    pallas_call x1, Pallas kernels, answer_rows(): kernel_call(answer_body, jax.ShapeDtypeStruct((SHARDS * CAP, width), jnp....  3.79 us
    pallas_call x1, Pallas kernels, train_rows(): kernel_call(train_body, (jax.ShapeDtypeStruct((rows, width), jnp.float32)...  3.76 us
  transfers between devices with their start and end apart: 31, of which 11 were waited for; matrix products, arithmetic and copies ran while one was open for 0% of the time, Pallas kernels for 6%

profile of v2, /device:TPU:2, one launch (start us, length us, event | category | flops | bytes accessed | tf_op | source)
XLA Modules:
  0.0 141.2 jit_solution(12290038611739489782)
XLA Ops:
  0.7 5.3 %shard_map.131 = (s32[8,512]{1,0:T(8,128)}, f32[8,200,128]{2,1,0:T(8,128)}, f32[8,200,128]{2,1,0:T(8,128)}, f32[2,192,128]{2,1,0:T(8,128)}, f32[2,192,128]{2,1,0:T(8,128)}) custom-call(s32[4,512]{1,0:T(4,128)} %bitcast.26, s32[4,512]{1,0:T(4,128)} %bitcast.27, f32[1536,512]{1,0:T(8,128)} %bitcast.23, f32[1536,512]{1,0:T(8,128)} %bitcast.24, f32[1536,512]{1,0:T(8,128)} %bitcast.25), custom_call_target="tpu_custom_call" | custom-call | flops 10000000 | bytes 4000000 | tf_op jit(solution)/shard_map/pallas_call | solution.py:156
  7.7 3.8 %shard_map.132 = (f32[2048,128]{1,0:T(8,128)S(1)}, bf16[2048,128]{1,0:T(8,128)(2,1)S(1)}, f32[896,128]{1,0:T(8,128)S(1)}) custom-call(s32[1]{0:T(128)S(6)} %copy.14.count_ref, s32[1,512]{1,0:T(1,128)S(1)} %bitcast.20, f32[2048,128]{1,0:T(8,128)S(1)} %bitcast.16, f32[2048,128]{1,0:T(8,128)S(1)} %copy-done.1, f32[512,128]{1,0:T(8,128)S(1)} %copy-done.5, ...), custom_call_target="tpu_custom_call" | custom-call | tf_op jit(solution)/shard_map/pallas_call | solution.py:308
  14.1 2.2 %collective-permute-start.2 = (f32[200,128]{1,0:T(8,128)S(1)}, f32[200,128]{1,0:T(8,128)S(1)}, u32[]{:S(2)}, u32[]{:S(2)}) collective-permute-start(f32[200,128]{1,0:T(8,128)S(1)} %get-tuple-element.35), channel_id=1, source_target_pairs={{0,2},{1,3},{2,0},{3,1},{4,6},{5,7},{6,4},{7,5},{8,10},{9,11},{10,... | collective-permute-start | bytes 307208 | tf_op jit(solution)/shard_map/ppermute | solution.py:520
  19.1 3.2 %collective-permute-start.5 = (f32[200,128]{1,0:T(8,128)S(1)}, f32[200,128]{1,0:T(8,128)S(1)}, u32[]{:S(2)}, u32[]{:S(2)}) collective-permute-start(f32[200,128]{1,0:T(8,128)S(1)} %get-tuple-element.38), channel_id=1, source_target_pairs={{0,8},{1,9},{2,10},{3,11},{4,12},{5,13},{6,14},{7,15},{8,0},{9,1},... | collective-permute-start | bytes 307208 | tf_op jit(solution)/shard_map/ppermute | solution.py:520
  22.3 3.4 %collective-permute-start.6 = (f32[200,128]{1,0:T(8,128)S(1)}, f32[200,128]{1,0:T(8,128)S(1)}, u32[]{:S(2)}, u32[]{:S(2)}) collective-permute-start(f32[200,128]{1,0:T(8,128)S(1)} %get-tuple-element.39), channel_id=1, source_target_pairs={{0,10},{1,11},{2,8},{3,9},{4,14},{5,15},{6,12},{7,13},{8,2},{9,3},... | collective-permute-start | bytes 307208 | tf_op jit(solution)/shard_map/ppermute | solution.py:520
  27.3 2.5 %collective-permute-start.8 = (f32[200,128]{1,0:T(8,128)S(1)}, f32[200,128]{1,0:T(8,128)S(1)}, u32[]{:S(2)}, u32[]{:S(2)}) collective-permute-start(f32[200,128]{1,0:T(8,128)S(1)} %get-tuple-element.41), channel_id=1, source_target_pairs={{0,14},{1,15},{2,12},{3,13},{4,10},{5,11},{6,8},{7,9},{8,6},{9,7},... | collective-permute-start | bytes 307208 | tf_op jit(solution)/shard_map/ppermute | solution.py:520
  31.0 2.7 %collective-permute-done.7.refs_6_ = f32[200,128]{1,0:T(8,128)S(1)} collective-permute-done((f32[200,128]{1,0:T(8,128)S(1)}, f32[200,128]{1,0:T(8,128)S(1)}, u32[]{:S(2)}, u32[]{:S(2)}) %collective-permute-start.7) | collective-permute-done | bytes 102432 | tf_op jit(solution)/shard_map/ppermute | solution.py:520
  33.7 1.8 %collective-permute-done.8.refs_7_ = f32[200,128]{1,0:T(8,128)S(1)} collective-permute-done((f32[200,128]{1,0:T(8,128)S(1)}, f32[200,128]{1,0:T(8,128)S(1)}, u32[]{:S(2)}, u32[]{:S(2)}) %collective-permute-start.8) | collective-permute-done | bytes 102432 | tf_op jit(solution)/shard_map/ppermute | solution.py:520
  35.6 2.0 %collective-permute-start.9 = (f32[200,128]{1,0:T(8,128)S(1)}, f32[200,128]{1,0:T(8,128)S(1)}, u32[]{:S(2)}, u32[]{:S(2)}) collective-permute-start(f32[200,128]{1,0:T(8,128)S(1)} %get-tuple-element.43), channel_id=1, source_target_pairs={{0,16},{1,17},{2,18},{3,19},{4,20},{5,21},{6,22},{7,23},{8,24},{9,... | collective-permute-start | bytes 307208 | tf_op jit(solution)/shard_map/ppermute | solution.py:520
  37.6 3.3 %collective-permute-start.10 = (f32[200,128]{1,0:T(8,128)S(1)}, f32[200,128]{1,0:T(8,128)S(1)}, u32[]{:S(2)}, u32[]{:S(2)}) collective-permute-start(f32[200,128]{1,0:T(8,128)S(1)} %get-tuple-element.44), channel_id=1, source_target_pairs={{0,32},{1,33},{2,34},{3,35},{4,36},{5,37},{6,38},{7,39},{8,40},{9,... | collective-permute-start | bytes 307208 | tf_op jit(solution)/shard_map/ppermute | solution.py:520
  41.3 4.6 %collective-permute-done.10.refs_2_ = f32[200,128]{1,0:T(8,128)S(1)} collective-permute-done((f32[200,128]{1,0:T(8,128)S(1)}, f32[200,128]{1,0:T(8,128)S(1)}, u32[]{:S(2)}, u32[]{:S(2)}) %collective-permute-start.10) | collective-permute-done | bytes 102432 | tf_op jit(solution)/shard_map/ppermute | solution.py:520
  47.5 5.4 %collective-permute-start.12 = (f32[224,128]{1,0:T(8,128)S(1)}, f32[224,128]{1,0:T(8,128)S(1)}, u32[]{:S(2)}, u32[]{:S(2)}) collective-permute-start(f32[224,128]{1,0:T(8,128)S(1)} %get-tuple-element.46.near_ref.own_ref), channel_id=1, source_target_pairs={{0,64},{1,65},{2,66},{3,67},{4,68},{5,69},{6,70},{7,71},{8,72},{9,... | collective-permute-start | bytes 344072 | tf_op jit(solution)/shard_map/ppermute | solution.py:520
  54.6 2.0 %collective-permute-done.12.far_ref = f32[224,128]{1,0:T(8,128)S(1)} collective-permute-done((f32[224,128]{1,0:T(8,128)S(1)}, f32[224,128]{1,0:T(8,128)S(1)}, u32[]{:S(2)}, u32[]{:S(2)}) %collective-permute-start.12) | collective-permute-done | bytes 114720 | tf_op jit(solution)/shard_map/ppermute | solution.py:520
  56.6 3.8 %shard_map.137 = bf16[4096,128]{1,0:T(8,128)(2,1)} custom-call(f32[224,128]{1,0:T(8,128)S(1)} %get-tuple-element.46.near_ref.own_ref, f32[224,128]{1,0:T(8,128)S(1)} %collective-permute-done.12.far_ref, bf16[2048,128]{1,0:T(8,128)(2,1)S(1)} %get-tuple-element.47.table_ref), custom_call_target="tpu_custom_call" | custom-call | flops 2147483648 | bytes 2000000 | tf_op jit(solution)/shard_map/pallas_call | solution.py:429
  60.4 13.4 %all-to-all-start = ((bf16[128,32,128]{2,1,0:T(8,128)(2,1)}), bf16[128,32,128]{2,1,0:T(8,128)(2,1)S(1)}, u32[]{:S(2)}, u32[]{:S(2)}) async-start(bf16[128,32,128]{2,1,0:T(8,128)(2,1)} %bitcast.11), calls=%async_computation | async-start | bytes 2097152 | tf_op jit(solution)/shard_map/all_to_all | solution.py:524
  73.8 14.3 %collective-permute-start.14 = (f32[192,128]{1,0:T(8,128)S(1)}, f32[192,128]{1,0:T(8,128)S(1)}, u32[]{:S(2)}, u32[]{:S(2)}) collective-permute-start(f32[192,128]{1,0:T(8,128)S(1)} %get-tuple-element.48), channel_id=1, source_target_pairs={{0,192},{1,193},{2,194},{3,195},{4,196},{5,197},{6,198},{7,199},{8... | collective-permute-start | bytes 294920 | tf_op jit(solution)/shard_map/ppermute | solution.py:520
  88.1 26.7 %collective-permute-done.14.other_far_ref = f32[192,128]{1,0:T(8,128)S(1)} collective-permute-done((f32[192,128]{1,0:T(8,128)S(1)}, f32[192,128]{1,0:T(8,128)S(1)}, u32[]{:S(2)}, u32[]{:S(2)}) %collective-permute-start.14) | collective-permute-done | bytes 98336 | tf_op jit(solution)/shard_map/ppermute | solution.py:520
  115.2 4.7 %collective-permute-start.21 = (bf16[384,128]{1,0:T(8,128)(2,1)S(1)}, bf16[384,128]{1,0:T(8,128)(2,1)S(1)}, u32[]{:S(2)}, u32[]{:S(2)}) collective-permute-start(bf16[384,128]{1,0:T(8,128)(2,1)S(1)} %shard_map.139.refs_0_), channel_id=1, source_target_pairs={{0,14},{1,15},{2,12},{3,13},{4,10},{5,11},{6,8},{7,9},{8,6},{9,7},... | collective-permute-start | bytes 294920 | tf_op jit(solution)/shard_map/ppermute | solution.py:520
  120.4 2.4 %collective-permute-start.19 = (bf16[384,128]{1,0:T(8,128)(2,1)S(1)}, bf16[384,128]{1,0:T(8,128)(2,1)S(1)}, u32[]{:S(2)}, u32[]{:S(2)}) collective-permute-start(bf16[384,128]{1,0:T(8,128)(2,1)S(1)} %shard_map.139.refs_0_), channel_id=1, source_target_pairs={{0,10},{1,11},{2,8},{3,9},{4,14},{5,15},{6,12},{7,13},{8,2},{9,3},... | collective-permute-start | bytes 294920 | tf_op jit(solution)/shard_map/ppermute | solution.py:520
  124.5 2.2 %collective-permute-start.17 = (bf16[384,128]{1,0:T(8,128)(2,1)S(1)}, bf16[384,128]{1,0:T(8,128)(2,1)S(1)}, u32[]{:S(2)}, u32[]{:S(2)}) collective-permute-start(bf16[384,128]{1,0:T(8,128)(2,1)S(1)} %shard_map.139.refs_0_), channel_id=1, source_target_pairs={{0,6},{1,7},{2,4},{3,5},{4,2},{5,3},{6,0},{7,1},{8,14},{9,15},{10,... | collective-permute-start | bytes 294920 | tf_op jit(solution)/shard_map/ppermute | solution.py:520
  128.6 4.2 %collective-permute-start.15 = (bf16[384,128]{1,0:T(8,128)(2,1)S(1)}, bf16[384,128]{1,0:T(8,128)(2,1)S(1)}, u32[]{:S(2)}, u32[]{:S(2)}) collective-permute-start(bf16[384,128]{1,0:T(8,128)(2,1)S(1)} %shard_map.139.refs_0_), channel_id=1, source_target_pairs={{0,2},{1,3},{2,0},{3,1},{4,6},{5,7},{6,4},{7,5},{8,10},{9,11},{10,... | collective-permute-start | bytes 294920 | tf_op jit(solution)/shard_map/ppermute | solution.py:520
  133.9 2.0 %collective-permute-done.15.refs_1_ = bf16[384,128]{1,0:T(8,128)(2,1)S(1)} collective-permute-done((bf16[384,128]{1,0:T(8,128)(2,1)S(1)}, bf16[384,128]{1,0:T(8,128)(2,1)S(1)}, u32[]{:S(2)}, u32[]{:S(2)}) %collective-permute-start.15) | collective-permute-done | bytes 98336 | tf_op jit(solution)/shard_map/ppermute | solution.py:520
  136.4 2.6 %shard_map.138.base_ref = bf16[512,512]{1,0:T(8,128)(2,1)S(1)} custom-call(s32[8,512]{1,0:T(8,128)S(1)} %copy-done.8, bf16[4096,128]{1,0:T(8,128)(2,1)S(1)} %bitcast.18), custom_call_target="tpu_custom_call" | custom-call | flops 2147483648 | bytes 2000000 | tf_op jit(solution)/shard_map/pallas_call | solution.py:458
  139.1 2.1 %shard_map.140 = f32[1,512]{1,0:T(1,128)} custom-call(bf16[512,512]{1,0:T(8,128)(2,1)S(1)} %shard_map.138.base_ref, f32[3,512]{1,0:T(4,128)S(1)} %copy-done.9, f32[1,512]{1,0:T(1,128)S(1)} %bitcast.22, bf16[384,128]{1,0:T(8,128)(2,1)S(1)} %shard_map.139.refs_0_, bf16[384,128]{1,0:T(8,128)(2,1)S(1)} %collective-permute-done.15.refs_1_, ...), custom_call_target="tpu_custom_call" | custom-call | flops 805306368 | bytes 3000000 | tf_op jit(solution)/shard_map/pallas_call | solution.py:503
  (71 shorter events, 19.2 us)
Async XLA Ops:
  6.0 6.8 %collective-permute-start.1 = (f32[8,200,128]{2,1,0:T(8,128)}, f32[8,200,128]{2,1,0:T(8,128)S(1)}, u32[]{:S(2)}, u32[]{:S(2)}) collective-permute-start(f32[8,200,128]{2,1,0:T(8,128)} %get-tuple-element.33), channel_id=1, source_target_pairs={{0,1},{1,0},{2,3},{3,2},{4,5},{5,4},{6,7},{7,6},{8,9},{9,8},{10,11... | collective-permute-start | bytes 2457608 | tf_op jit(solution)/shard_map/ppermute | solution.py:520
  11.5 41.4 %collective-permute-start = (f32[896,128]{1,0:T(8,128)S(1)}, f32[896,128]{1,0:T(8,128)S(1)}, u32[]{:S(2)}, u32[]{:S(2)}) collective-permute-start(f32[896,128]{1,0:T(8,128)S(1)} %get-tuple-element.27), channel_id=1, source_target_pairs={{0,128},{1,129},{2,130},{3,131},{4,132},{5,133},{6,134},{7,135},{8... | collective-permute-start | bytes 1376264 | tf_op jit(solution)/shard_map/ppermute | solution.py:555
  14.1 8.3 %collective-permute-start.2 = (f32[200,128]{1,0:T(8,128)S(1)}, f32[200,128]{1,0:T(8,128)S(1)}, u32[]{:S(2)}, u32[]{:S(2)}) collective-permute-start(f32[200,128]{1,0:T(8,128)S(1)} %get-tuple-element.35), channel_id=1, source_target_pairs={{0,2},{1,3},{2,0},{3,1},{4,6},{5,7},{6,4},{7,5},{8,10},{9,11},{10,... | collective-permute-start | bytes 307208 | tf_op jit(solution)/shard_map/ppermute | solution.py:520
  16.3 9.4 %collective-permute-start.3 = (f32[200,128]{1,0:T(8,128)S(1)}, f32[200,128]{1,0:T(8,128)S(1)}, u32[]{:S(2)}, u32[]{:S(2)}) collective-permute-start(f32[200,128]{1,0:T(8,128)S(1)} %get-tuple-element.36), channel_id=1, source_target_pairs={{0,4},{1,5},{2,6},{3,7},{4,0},{5,1},{6,2},{7,3},{8,12},{9,13},{10,... | collective-permute-start | bytes 307208 | tf_op jit(solution)/shard_map/ppermute | solution.py:520
  17.8 9.4 %collective-permute-start.4 = (f32[200,128]{1,0:T(8,128)S(1)}, f32[200,128]{1,0:T(8,128)S(1)}, u32[]{:S(2)}, u32[]{:S(2)}) collective-permute-start(f32[200,128]{1,0:T(8,128)S(1)} %get-tuple-element.37), channel_id=1, source_target_pairs={{0,6},{1,7},{2,4},{3,5},{4,2},{5,3},{6,0},{7,1},{8,14},{9,15},{10,... | collective-permute-start | bytes 307208 | tf_op jit(solution)/shard_map/ppermute | solution.py:520
  19.1 10.6 %collective-permute-start.5 = (f32[200,128]{1,0:T(8,128)S(1)}, f32[200,128]{1,0:T(8,128)S(1)}, u32[]{:S(2)}, u32[]{:S(2)}) collective-permute-start(f32[200,128]{1,0:T(8,128)S(1)} %get-tuple-element.38), channel_id=1, source_target_pairs={{0,8},{1,9},{2,10},{3,11},{4,12},{5,13},{6,14},{7,15},{8,0},{9,1},... | collective-permute-start | bytes 307208 | tf_op jit(solution)/shard_map/ppermute | solution.py:520
  22.3 8.6 %collective-permute-start.6 = (f32[200,128]{1,0:T(8,128)S(1)}, f32[200,128]{1,0:T(8,128)S(1)}, u32[]{:S(2)}, u32[]{:S(2)}) collective-permute-start(f32[200,128]{1,0:T(8,128)S(1)} %get-tuple-element.39), channel_id=1, source_target_pairs={{0,10},{1,11},{2,8},{3,9},{4,14},{5,15},{6,12},{7,13},{8,2},{9,3},... | collective-permute-start | bytes 307208 | tf_op jit(solution)/shard_map/ppermute | solution.py:520
  25.7 8.0 %collective-permute-start.7 = (f32[200,128]{1,0:T(8,128)S(1)}, f32[200,128]{1,0:T(8,128)S(1)}, u32[]{:S(2)}, u32[]{:S(2)}) collective-permute-start(f32[200,128]{1,0:T(8,128)S(1)} %get-tuple-element.40), channel_id=1, source_target_pairs={{0,12},{1,13},{2,14},{3,15},{4,8},{5,9},{6,10},{7,11},{8,4},{9,5},... | collective-permute-start | bytes 307208 | tf_op jit(solution)/shard_map/ppermute | solution.py:520
  27.3 8.3 %collective-permute-start.8 = (f32[200,128]{1,0:T(8,128)S(1)}, f32[200,128]{1,0:T(8,128)S(1)}, u32[]{:S(2)}, u32[]{:S(2)}) collective-permute-start(f32[200,128]{1,0:T(8,128)S(1)} %get-tuple-element.41), channel_id=1, source_target_pairs={{0,14},{1,15},{2,12},{3,13},{4,10},{5,11},{6,8},{7,9},{8,6},{9,7},... | collective-permute-start | bytes 307208 | tf_op jit(solution)/shard_map/ppermute | solution.py:520
  37.6 8.2 %collective-permute-start.10 = (f32[200,128]{1,0:T(8,128)S(1)}, f32[200,128]{1,0:T(8,128)S(1)}, u32[]{:S(2)}, u32[]{:S(2)}) collective-permute-start(f32[200,128]{1,0:T(8,128)S(1)} %get-tuple-element.44), channel_id=1, source_target_pairs={{0,32},{1,33},{2,34},{3,35},{4,36},{5,37},{6,38},{7,39},{8,40},{9,... | collective-permute-start | bytes 307208 | tf_op jit(solution)/shard_map/ppermute | solution.py:520
  40.9 6.6 %collective-permute-start.11 = (f32[200,128]{1,0:T(8,128)S(1)}, f32[200,128]{1,0:T(8,128)S(1)}, u32[]{:S(2)}, u32[]{:S(2)}) collective-permute-start(f32[200,128]{1,0:T(8,128)S(1)} %get-tuple-element.45), channel_id=1, source_target_pairs={{0,48},{1,49},{2,50},{3,51},{4,52},{5,53},{6,54},{7,55},{8,56},{9,... | collective-permute-start | bytes 307208 | tf_op jit(solution)/shard_map/ppermute | solution.py:520
  47.5 9.1 %collective-permute-start.12 = (f32[224,128]{1,0:T(8,128)S(1)}, f32[224,128]{1,0:T(8,128)S(1)}, u32[]{:S(2)}, u32[]{:S(2)}) collective-permute-start(f32[224,128]{1,0:T(8,128)S(1)} %get-tuple-element.46.near_ref.own_ref), channel_id=1, source_target_pairs={{0,64},{1,65},{2,66},{3,67},{4,68},{5,69},{6,70},{7,71},{8,72},{9,... | collective-permute-start | bytes 344072 | tf_op jit(solution)/shard_map/ppermute | solution.py:520
  60.4 76.1 %all-to-all-start = ((bf16[128,32,128]{2,1,0:T(8,128)(2,1)}), bf16[128,32,128]{2,1,0:T(8,128)(2,1)S(1)}, u32[]{:S(2)}, u32[]{:S(2)}) async-start(bf16[128,32,128]{2,1,0:T(8,128)(2,1)} %bitcast.11), calls=%async_computation | async-start | bytes 2097152 | tf_op jit(solution)/shard_map/all_to_all | solution.py:524
  73.8 41.0 %collective-permute-start.14 = (f32[192,128]{1,0:T(8,128)S(1)}, f32[192,128]{1,0:T(8,128)S(1)}, u32[]{:S(2)}, u32[]{:S(2)}) collective-permute-start(f32[192,128]{1,0:T(8,128)S(1)} %get-tuple-element.48), channel_id=1, source_target_pairs={{0,192},{1,193},{2,194},{3,195},{4,196},{5,197},{6,198},{7,199},{8... | collective-permute-start | bytes 294920 | tf_op jit(solution)/shard_map/ppermute | solution.py:520
  88.1 26.8 %collective-permute-start.13 = (f32[192,128]{1,0:T(8,128)S(1)}, f32[192,128]{1,0:T(8,128)S(1)}, u32[]{:S(2)}, u32[]{:S(2)}) collective-permute-start(f32[192,128]{1,0:T(8,128)S(1)} %get-tuple-element.48), channel_id=1, source_target_pairs={{0,128},{1,129},{2,130},{3,131},{4,132},{5,133},{6,134},{7,135},{8... | collective-permute-start | bytes 294920 | tf_op jit(solution)/shard_map/ppermute | solution.py:520
  115.1 9.4 %collective-permute-start.22 = (bf16[384,128]{1,0:T(8,128)(2,1)S(1)}, bf16[384,128]{1,0:T(8,128)(2,1)S(1)}, u32[]{:S(2)}, u32[]{:S(2)}) collective-permute-start(bf16[384,128]{1,0:T(8,128)(2,1)S(1)} %shard_map.139.refs_0_), channel_id=1, source_target_pairs={{0,1},{1,0},{2,3},{3,2},{4,5},{5,4},{6,7},{7,6},{8,9},{9,8},{10,11... | collective-permute-start | bytes 294920 | tf_op jit(solution)/shard_map/ppermute | solution.py:520
  115.2 11.4 %collective-permute-start.21 = (bf16[384,128]{1,0:T(8,128)(2,1)S(1)}, bf16[384,128]{1,0:T(8,128)(2,1)S(1)}, u32[]{:S(2)}, u32[]{:S(2)}) collective-permute-start(bf16[384,128]{1,0:T(8,128)(2,1)S(1)} %shard_map.139.refs_0_), channel_id=1, source_target_pairs={{0,14},{1,15},{2,12},{3,13},{4,10},{5,11},{6,8},{7,9},{8,6},{9,7},... | collective-permute-start | bytes 294920 | tf_op jit(solution)/shard_map/ppermute | solution.py:520
  119.9 8.7 %collective-permute-start.20 = (bf16[384,128]{1,0:T(8,128)(2,1)S(1)}, bf16[384,128]{1,0:T(8,128)(2,1)S(1)}, u32[]{:S(2)}, u32[]{:S(2)}) collective-permute-start(bf16[384,128]{1,0:T(8,128)(2,1)S(1)} %shard_map.139.refs_0_), channel_id=1, source_target_pairs={{0,12},{1,13},{2,14},{3,15},{4,8},{5,9},{6,10},{7,11},{8,4},{9,5},... | collective-permute-start | bytes 294920 | tf_op jit(solution)/shard_map/ppermute | solution.py:520
  120.4 12.4 %collective-permute-start.19 = (bf16[384,128]{1,0:T(8,128)(2,1)S(1)}, bf16[384,128]{1,0:T(8,128)(2,1)S(1)}, u32[]{:S(2)}, u32[]{:S(2)}) collective-permute-start(bf16[384,128]{1,0:T(8,128)(2,1)S(1)} %shard_map.139.refs_0_), channel_id=1, source_target_pairs={{0,10},{1,11},{2,8},{3,9},{4,14},{5,15},{6,12},{7,13},{8,2},{9,3},... | collective-permute-start | bytes 294920 | tf_op jit(solution)/shard_map/ppermute | solution.py:520
  122.8 10.0 %collective-permute-start.18 = (bf16[384,128]{1,0:T(8,128)(2,1)S(1)}, bf16[384,128]{1,0:T(8,128)(2,1)S(1)}, u32[]{:S(2)}, u32[]{:S(2)}) collective-permute-start(bf16[384,128]{1,0:T(8,128)(2,1)S(1)} %shard_map.139.refs_0_), channel_id=1, source_target_pairs={{0,8},{1,9},{2,10},{3,11},{4,12},{5,13},{6,14},{7,15},{8,0},{9,1},... | collective-permute-start | bytes 294920 | tf_op jit(solution)/shard_map/ppermute | solution.py:520
  124.5 8.9 %collective-permute-start.17 = (bf16[384,128]{1,0:T(8,128)(2,1)S(1)}, bf16[384,128]{1,0:T(8,128)(2,1)S(1)}, u32[]{:S(2)}, u32[]{:S(2)}) collective-permute-start(bf16[384,128]{1,0:T(8,128)(2,1)S(1)} %shard_map.139.refs_0_), channel_id=1, source_target_pairs={{0,6},{1,7},{2,4},{3,5},{4,2},{5,3},{6,0},{7,1},{8,14},{9,15},{10,... | collective-permute-start | bytes 294920 | tf_op jit(solution)/shard_map/ppermute | solution.py:520
  126.6 7.2 %collective-permute-start.16 = (bf16[384,128]{1,0:T(8,128)(2,1)S(1)}, bf16[384,128]{1,0:T(8,128)(2,1)S(1)}, u32[]{:S(2)}, u32[]{:S(2)}) collective-permute-start(bf16[384,128]{1,0:T(8,128)(2,1)S(1)} %shard_map.139.refs_0_), channel_id=1, source_target_pairs={{0,4},{1,5},{2,6},{3,7},{4,0},{5,1},{6,2},{7,3},{8,12},{9,13},{10,... | collective-permute-start | bytes 294920 | tf_op jit(solution)/shard_map/ppermute | solution.py:520
  128.6 7.2 %collective-permute-start.15 = (bf16[384,128]{1,0:T(8,128)(2,1)S(1)}, bf16[384,128]{1,0:T(8,128)(2,1)S(1)}, u32[]{:S(2)}, u32[]{:S(2)}) collective-permute-start(bf16[384,128]{1,0:T(8,128)(2,1)S(1)} %shard_map.139.refs_0_), channel_id=1, source_target_pairs={{0,2},{1,3},{2,0},{3,1},{4,6},{5,7},{6,4},{7,5},{8,10},{9,11},{10,... | collective-permute-start | bytes 294920 | tf_op jit(solution)/shard_map/ppermute | solution.py:520
  133.3 5.7 %collective-permute-start.27 = (bf16[384,128]{1,0:T(8,128)(2,1)S(1)}, bf16[384,128]{1,0:T(8,128)(2,1)S(1)}, u32[]{:S(2)}, u32[]{:S(2)}) collective-permute-start(bf16[384,128]{1,0:T(8,128)(2,1)S(1)} %collective-permute-done.19.refs_5_), channel_id=1, source_target_pairs={{0,1},{1,0},{2,3},{3,2},{4,5},{5,4},{6,7},{7,6},{8,9},{9,8},{10,11... | collective-permute-start | bytes 294920 | tf_op jit(solution)/shard_map/ppermute | solution.py:520
  (18 other events, 251.1 us)

commit v3 on v2

v3 whole, which is shorter than its diff:
```python
import jax
import jax.numpy as jnp
from jax import lax
from jax.experimental import pallas as pl
from jax.experimental.pallas import tpu as pltpu
from jax.sharding import PartitionSpec as P

ROW_SHRINK = 0.25
DENSE_SHRINK = 0.05
CAP = 32
LANES = 128
SHARDS = 128
ROLES = 2
CORES = 2
TILES = 2
SHARE = 12
PACKED = 16
VMEM_LIMIT = 40 * 1024 * 1024


def ftrl_weight(linear, squares, shrink):
    return -(linear - jnp.clip(linear, -shrink, shrink)) / (1.0 + jnp.sqrt(squares))


def ftrl_step(linear, squares, gradient, shrink):
    prior = ftrl_weight(linear, squares, shrink)
    fresh_squares = squares + gradient * gradient
    sigma_step = jnp.sqrt(fresh_squares) - jnp.sqrt(squares)
    return (linear + gradient - sigma_step * prior, fresh_squares, prior)


def iota(shape, dim):
    return lax.broadcasted_iota(jnp.int32, shape, dim)


def kernel_call(body, out_shape, flops=0, bytes_accessed=0, vmem=VMEM_LIMIT, **options):
    return pl.pallas_call(
        body,
        out_shape=out_shape,
        compiler_params=pltpu.CompilerParams(vmem_limit_bytes=vmem),
        cost_estimate=pl.CostEstimate(
            flops=flops, bytes_accessed=bytes_accessed, transcendentals=0
        ),
        **options,
    )


VMEM = pl.BlockSpec(memory_space=pltpu.VMEM)
SMEM = pl.BlockSpec(memory_space=pltpu.SMEM)
ANY = pl.BlockSpec(memory_space=pl.ANY)


def position():
    shard = lax.axis_index("shard")
    return lax.axis_index("role"), shard, lax.rem(shard, CORES)


def piece_copies(array_ref, own_ref):
    _, shard, _ = position()
    rows = array_ref.shape[0] // ROLES
    pairs = []
    for half in range(ROLES):
        first = pl.multiple_of(half * rows + shard // 4 * (2 * SHARE), 2 * SHARE)
        for core in range(CORES):
            left = pl.multiple_of((core * TILES + lax.rem(shard, TILES)) * LANES, LANES)
            pairs.append(
                (
                    array_ref.at[pl.ds(first, 2 * SHARE), pl.ds(left, LANES)],
                    own_ref.at[half, core],
                )
            )
    return pairs


def half_copies(grad_ref, send_ref, keep_ref):
    role, _, core = position()
    rows = grad_ref.shape[0] // ROLES
    pairs = []
    for flip, target in ((1, send_ref), (0, keep_ref)):
        for tile in range(TILES):
            left = pl.multiple_of(((core ^ flip) * TILES + tile) * LANES, LANES)
            first = pl.multiple_of(role * rows, rows)
            pairs.append(
                (grad_ref.at[pl.ds(first, rows), pl.ds(left, LANES)], target.at[tile])
            )
    return pairs


def front_body(owner_ref, slot_ref, grad_ref, state_ref, square_ref, place_ref, request_ref, send_ref, keep_ref, own_state_ref, own_square_ref, arrived):
    pairs = (
        half_copies(grad_ref, send_ref, keep_ref)
        + piece_copies(state_ref, own_state_ref)
        + piece_copies(square_ref, own_square_ref)
    )
    copies = [
        pltpu.make_async_copy(source, target, arrived.at[at])
        for at, (source, target) in enumerate(pairs)
    ]
    for copy in copies:
        copy.start()
    fields, examples = owner_ref.shape
    shape = (SHARDS, examples)
    shard_ids = iota(shape, 0)
    member = jnp.zeros(shape, jnp.float32)
    wanted = jnp.zeros(shape, jnp.float32)
    for field in range(fields):
        named = owner_ref[field : field + 1, :] == shard_ids
        member = jnp.where(named, 1.0, member)
        wanted = jnp.where(named, slot_ref[field : field + 1, :].astype(jnp.float32), wanted)
    earlier = jnp.where(iota((examples, examples), 0) < iota((examples, examples), 1), 1.0, 0.0)
    ranks = jnp.dot(
        member.astype(jnp.bfloat16),
        earlier.astype(jnp.bfloat16),
        preferred_element_type=jnp.float32,
    )
    places = []
    for field in range(fields):
        owners = owner_ref[field : field + 1, :]
        rank = jnp.sum(jnp.where(owners == shard_ids, ranks, 0.0), axis=0, keepdims=True)
        places.append(owners * CAP + rank.astype(jnp.int32))
    place_ref[...] = jnp.concatenate(
        places + [jnp.zeros((8 - fields, examples), jnp.int32)], axis=0
    )
    ranks = jnp.where(member > 0.5, ranks, -1.0)
    requests = jnp.zeros((SHARDS, LANES), jnp.float32)
    lanes = iota((SHARDS, LANES), 1)
    for rank in range(CAP):
        column = jnp.sum(
            jnp.where(ranks == float(rank), wanted, 0.0), axis=1, keepdims=True
        )
        requests = jnp.where(lanes == rank, column, requests)
    asked = requests[:, :CAP].astype(jnp.int32)
    request_ref[...] = jnp.concatenate(
        [asked >> 4, asked & 15, jnp.zeros((SHARDS, LANES - 2 * CAP), jnp.int32)], axis=1
    ).astype(jnp.float32)
    for copy in copies:
        copy.wait()


def front(owners, slots, grads, state, squares):
    fields, examples = owners.shape
    halves = jax.ShapeDtypeStruct((TILES, grads.shape[0] // ROLES, LANES), jnp.float32)
    own = jax.ShapeDtypeStruct((ROLES, CORES, 2 * SHARE, LANES), jnp.float32)
    return kernel_call(
        front_body,
        (
            jax.ShapeDtypeStruct((8, examples), jnp.int32),
            jax.ShapeDtypeStruct((SHARDS, LANES), jnp.float32),
            halves,
            halves,
            own,
            own,
        ),
        flops=10_000_000,
        bytes_accessed=4_000_000,
        vmem=60 * 1024 * 1024,
        in_specs=[VMEM, VMEM, ANY, ANY, ANY],
        out_specs=(VMEM,) * 6,
        scratch_shapes=[pltpu.SemaphoreType.DMA((2 * TILES + 4 * ROLES,))],
    )(owners, slots, grads, state, squares)


def pack_body(keep_ref, arrived_ref, request_ref, packed_ref):
    for block in range(SHARDS // 4):
        rows = slice(block * 2 * SHARE, (block + 1) * 2 * SHARE)
        for tile in range(TILES):
            terms = keep_ref[tile, rows, :] + arrived_ref[tile, rows, :]
            for part in range(2):
                shard = block * 4 + part * TILES + tile
                packed_ref[shard] = jnp.concatenate(
                    [
                        terms[part * SHARE : (part + 1) * SHARE, :],
                        request_ref[shard : shard + 1, :],
                        jnp.zeros((PACKED - SHARE - 1, LANES), jnp.float32),
                    ],
                    axis=0,
                ).astype(jnp.bfloat16)


def pack(keep, arrived, requests):
    return kernel_call(
        pack_body,
        jax.ShapeDtypeStruct((SHARDS, PACKED, LANES), jnp.bfloat16),
        in_specs=[VMEM] * 3,
        out_specs=VMEM,
    )(keep, arrived, requests)


def unpack_body(packed_ref, sum_ref, asked_ref):
    for core in range(CORES):
        total = jnp.zeros((PACKED, LANES), jnp.float32)
        for shard in range(core, SHARDS, CORES):
            packed = packed_ref[shard].astype(jnp.float32)
            total = total + packed
            asked_ref[shard : shard + 1, :] = packed[SHARE : SHARE + 1, :]
        sum_ref[core] = total


def unpack(packed):
    return kernel_call(
        unpack_body,
        (
            jax.ShapeDtypeStruct((CORES, PACKED, LANES), jnp.float32),
            jax.ShapeDtypeStruct((SHARDS, LANES), jnp.float32),
        ),
        in_specs=[VMEM],
        out_specs=(VMEM, VMEM),
    )(packed)


def used_slots(slot_ref, count):
    slots = slot_ref[...]
    return jnp.where(iota(slots.shape, 1) < count, slots, -1)


def rows_of_block(slots, first, rows):
    hit = slots == iota((rows, slots.shape[1]), 0) + first
    return jnp.where(hit, 1.0, 0.0).astype(jnp.bfloat16)


def train_body(count_ref, slot_ref, held_ref, square_ref, grad_ref, state_ref, new_ref, weight_ref, fresh_ref, parts, total):
    step = pl.program_id(0)
    rows = held_ref.shape[0]

    @pl.when(step == 0)
    def _():
        grads = grad_ref[...]
        high = grads.astype(jnp.bfloat16)
        rest = grads - high.astype(jnp.float32)
        middle = rest.astype(jnp.bfloat16)
        low = (rest - middle.astype(jnp.float32)).astype(jnp.bfloat16)
        parts[...] = jnp.concatenate([high, middle, low], axis=1)
        total[...] = jnp.zeros_like(total)

    spread = rows_of_block(used_slots(slot_ref, count_ref[0]), step * rows, rows)
    sums = jnp.dot(spread, parts[...], preferred_element_type=jnp.float32)
    gradient = (sums[:, :LANES] + sums[:, LANES : 2 * LANES]) + sums[:, 2 * LANES :]
    linear, squares, _ = ftrl_step(held_ref[...], square_ref[...], gradient, ROW_SHRINK)
    new_ref[...] = linear
    weights = ftrl_weight(linear, squares, ROW_SHRINK).astype(jnp.bfloat16)
    weight_ref[...] = weights
    total[...] += lax.dot_general(
        spread, weights, (((0,), (0,)), ((), ())), preferred_element_type=jnp.float32
    )

    @pl.when(step == pl.num_programs(0) - 1)
    def _():
        updates = total.shape[0]
        fresh_ref[:updates, :] = total[...]
        fresh_ref[updates:, :] = state_ref[...]


def train_rows(count, slots, held, squares, grads, state):
    rows, width = held.shape
    updates = grads.shape[0]
    block = 512
    by_rows = pl.BlockSpec((block, width), lambda i: (i, 0))
    return kernel_call(
        train_body,
        (
            jax.ShapeDtypeStruct((rows, width), jnp.float32),
            jax.ShapeDtypeStruct((rows, width), jnp.bfloat16),
            jax.ShapeDtypeStruct((updates + state.shape[0], width), jnp.float32),
        ),
        grid=(rows // block,),
        in_specs=[
            SMEM,
            pl.BlockSpec((1, updates), lambda i: (0, 0)),
            by_rows,
            by_rows,
            pl.BlockSpec((updates, width), lambda i: (0, 0)),
            pl.BlockSpec(state.shape, lambda i: (0, 0)),
        ],
        out_specs=(
            by_rows,
            by_rows,
            pl.BlockSpec((updates + state.shape[0], width), lambda i: (0, 0)),
        ),
        scratch_shapes=[
            pltpu.VMEM((updates, 3 * width), jnp.bfloat16),
            pltpu.VMEM((updates, width), jnp.float32),
        ],
    )(count, slots, held, squares, grads, state)


def serve_body(count_ref, slot_ref, arrived_ref, held_ref, new_ref, weight_ref, table_ref, lookup_ref):
    step = pl.program_id(0)
    rows = held_ref.shape[0]
    role = lax.axis_index("role")

    @pl.when(role == 0)
    def _():
        table_ref[...] = new_ref[...]
        lookup_ref[...] = weight_ref[...]

    @pl.when(role != 0)
    def _():
        spread = rows_of_block(used_slots(slot_ref, count_ref[0]), step * rows, rows)
        arrived = arrived_ref[: slot_ref.shape[1], :].astype(jnp.bfloat16)
        sums = jnp.dot(
            spread,
            jnp.concatenate([arrived, jnp.ones_like(arrived)], axis=1),
            preferred_element_type=jnp.float32,
        )
        table = jnp.where(sums[:, LANES:] > 0.5, sums[:, :LANES], held_ref[...])
        table_ref[...] = table
        lookup_ref[...] = table.astype(jnp.bfloat16)


def serve_rows(count, slots, arrived, held, new_linear, weights):
    rows, width = held.shape
    updates = slots.shape[1]
    block = 1024
    by_rows = pl.BlockSpec((block, width), lambda i: (i, 0))
    return kernel_call(
        serve_body,
        (
            jax.ShapeDtypeStruct((rows, width), jnp.float32),
            jax.ShapeDtypeStruct((rows, width), jnp.bfloat16),
        ),
        grid=(rows // block,),
        in_specs=[
            SMEM,
            pl.BlockSpec((1, updates), lambda i: (0, 0)),
            pl.BlockSpec((updates, width), lambda i: (0, 0)),
            by_rows,
            by_rows,
            by_rows,
        ],
        out_specs=(by_rows, by_rows),
    )(count, slots, arrived, held, new_linear, weights)


def looked_up(column, folded):
    rows, height = column.shape[0], folded.shape[0]
    spread = jnp.broadcast_to(column, (rows, LANES))
    within = jnp.where((spread & (LANES - 1)) == iota((rows, LANES), 1), 1.0, 0.0).astype(
        jnp.bfloat16
    )
    block = ((spread & (height - 1)) >> 7).astype(jnp.float32).astype(jnp.bfloat16)
    none = jnp.zeros_like(within)
    hot = jnp.concatenate(
        [jnp.where(block == jnp.bfloat16(at), within, none) for at in range(height // LANES)],
        axis=1,
    )
    both = jnp.dot(hot, folded, preferred_element_type=jnp.float32)
    return jnp.where(spread < height, both[:, :LANES], both[:, LANES:]).astype(jnp.bfloat16)


def fold(source_ref, target_ref):
    height = target_ref.shape[0]
    target_ref[:, :LANES] = source_ref[:height, :]
    target_ref[:, LANES:] = source_ref[height:, :]


def piece_weights(sum_ref, other_ref, state_ref, trained_ref, square_ref):
    role, shard, _ = position()
    later = lax.rem(shard // TILES, 2) == 1

    def own(values):
        return jnp.where(later, values[SHARE : 2 * SHARE, :], values[:SHARE, :])

    halves = []
    for half in range(ROLES):
        parts = []
        for core in range(CORES):
            gradient = jnp.where(role == half, sum_ref[core], other_ref[core])[:SHARE, :]
            first = (half * CORES + core) * 2 * SHARE
            state = own(state_ref[half, core])
            trained = own(trained_ref[first : first + 2 * SHARE, :])
            linear = jnp.where(role == 0, state, trained)
            dense_linear, dense_sumsq, prior = ftrl_step(
                linear, own(square_ref[half, core]), gradient, DENSE_SHRINK
            )
            fresh = ftrl_weight(dense_linear, dense_sumsq, DENSE_SHRINK)
            parts.append(jnp.where(role == 0, fresh, state + (fresh - prior)))
        halves.append(jnp.concatenate(parts, axis=0).astype(jnp.bfloat16))
    return halves


def answer_body(asked_ref, table_ref, sum_ref, other_ref, state_ref, trained_ref, square_ref, answer_ref, columns, folded):
    digits = asked_ref[...]
    wide = jnp.concatenate(
        [
            digits[:, :CAP] * 16.0 + digits[:, CAP : 2 * CAP],
            jnp.zeros((SHARDS, LANES - CAP), jnp.float32),
        ],
        axis=1,
    )
    columns[...] = jnp.transpose(wide)[:CAP, :].astype(jnp.int32)
    fold(table_ref, folded)
    halves = piece_weights(sum_ref, other_ref, state_ref, trained_ref, square_ref)
    group = 8
    for at in range(0, SHARDS, group):
        asked = jnp.concatenate(
            [columns[:, shard : shard + 1] for shard in range(at, at + group)], axis=0
        )
        found = looked_up(asked, folded[...])
        for part in range(group):
            answer_ref[at + part] = jnp.concatenate(
                [found[part * CAP : (part + 1) * CAP, :], halves[(at + part) % CORES]], axis=0
            )


def answer_rows(asked, table, sums, other_sums, state, trained, squares):
    rows, width = table.shape
    return kernel_call(
        answer_body,
        jax.ShapeDtypeStruct((SHARDS, CAP + CORES * SHARE, width), jnp.bfloat16),
        flops=2 * SHARDS * CAP * rows * width,
        bytes_accessed=2_000_000,
        in_specs=[VMEM] * 7,
        out_specs=VMEM,
        scratch_shapes=[
            pltpu.VMEM((CAP, SHARDS), jnp.int32),
            pltpu.VMEM((rows // 2, 2 * width), jnp.bfloat16),
        ],
    )(asked, table, sums, other_sums, state, trained, squares)


def collect_body(answer_ref, half_ref):
    for block in range(SHARDS // 8):
        for core in range(CORES):
            for tile in range(TILES):
                first = CAP + core * SHARE
                parts = [
                    answer_ref[block * 8 + part * TILES + tile].astype(jnp.float32)[
                        first : first + SHARE, :
                    ]
                    for part in range(4)
                ]
                left = (core * TILES + tile) * LANES
                half_ref[block * 4 * SHARE : (block + 1) * 4 * SHARE, left : left + LANES] = (
                    jnp.concatenate(parts, axis=0).astype(jnp.bfloat16)
                )


def collect(answers):
    return kernel_call(
        collect_body,
        jax.ShapeDtypeStruct(
            (SHARDS // 2 * SHARE, CORES * TILES * LANES), jnp.bfloat16
        ),
        in_specs=[VMEM],
        out_specs=VMEM,
    )(answers)


def arrange_body(place_ref, answer_ref, base_ref, columns, folded):
    columns[...] = jnp.transpose(place_ref[...])
    for shard in range(SHARDS):
        side, at = divmod(shard, SHARDS // 2)
        folded[at * CAP : (at + 1) * CAP, side * LANES : (side + 1) * LANES] = answer_ref[shard][
            :CAP, :
        ]
    examples = columns.shape[0]
    block = 256
    for field in range(base_ref.shape[1] // LANES):
        for at in range(0, examples, block):
            base_ref[at : at + block, field * LANES : (field + 1) * LANES] = looked_up(
                columns[at : at + block, field : field + 1], folded[...]
            )


def arrange_rows(places, answers, fields):
    examples = places.shape[1]
    rows, width = SHARDS * CAP, answers.shape[2]
    return kernel_call(
        arrange_body,
        jax.ShapeDtypeStruct((examples, fields * width), jnp.bfloat16),
        flops=2 * examples * fields * rows * width,
        bytes_accessed=2_000_000,
        in_specs=[VMEM, VMEM],
        out_specs=VMEM,
        scratch_shapes=[
            pltpu.VMEM((examples, 8), jnp.int32),
            pltpu.VMEM((rows // 2, 2 * width), jnp.bfloat16),
        ],
    )(places, answers)


def cross_body(base_ref, bias_ref, out_ref, own_ref, other_ref, score_ref, weights):
    _, _, core = position()
    rows = own_ref.shape[0]
    weights[pl.ds(pl.multiple_of(core * rows, rows), rows), :] = own_ref[...]
    weights[pl.ds(pl.multiple_of((1 - core) * rows, rows), rows), :] = other_ref[...]
    width = base_ref.shape[1]
    base = base_ref[...].astype(jnp.float32)
    crossed = base
    for layer in range(bias_ref.shape[0]):
        mixed = jnp.dot(
            crossed.astype(jnp.bfloat16),
            weights[layer * width : (layer + 1) * width, :],
            preferred_element_type=jnp.float32,
        )
        crossed = base * (mixed + bias_ref[layer : layer + 1, :]) + crossed
    scores = jnp.sum(crossed * out_ref[...], axis=1, keepdims=True)
    score_ref[...] = jnp.transpose(jnp.broadcast_to(scores, (scores.shape[0], LANES)))[:1, :]


def cross_scores(base, bias, out_weight, own, other):
    examples, width = base.shape
    layers = bias.shape[0]
    return kernel_call(
        cross_body,
        jax.ShapeDtypeStruct((1, examples), jnp.float32),
        flops=2 * examples * width * width * layers,
        bytes_accessed=3_000_000,
        in_specs=[VMEM] * 5,
        out_specs=VMEM,
        scratch_shapes=[pltpu.VMEM((layers * width, width), jnp.bfloat16)],
    )(base, bias, out_weight, own, other)


BOTH = ("role", "shard")
CORE_BIT, ROLE_BIT = 1, 128


def swapped(value, bits):
    count = ROLES * SHARDS
    return lax.ppermute(value, BOTH, [(source, source ^ bits) for source in range(count)])


def exchange(value):
    return lax.all_to_all(value, "shard", split_axis=0, concat_axis=0, tiled=True)


def on_device(
    tables,
    row_squares,
    update_slots,
    update_counts,
    row_grads,
    dense_state,
    dense_squares,
    dense_grads,
    cross_bias,
    out_weight,
    cand_owner,
    cand_slot,
):
    fields = cand_owner.shape[2]
    rows = dense_squares.shape[0] * dense_squares.shape[1]
    places, requests, send, keep, own_state, own_squares = front(
        cand_owner[0].T,
        cand_slot[0].T,
        dense_grads[0].reshape(rows, -1),
        dense_state[0].reshape(rows, -1),
        dense_squares.reshape(rows, -1),
    )
    sums, asked = unpack(exchange(pack(keep, swapped(send, CORE_BIT), requests)))
    slots = update_slots.reshape(1, -1)
    new_linear, weights, fresh = train_rows(
        update_counts, slots, tables[0], row_squares, row_grads, own_state.reshape(-1, LANES)
    )
    arrived = lax.ppermute(fresh, "role", [(0, 1)])
    table_result, lookup = serve_rows(
        update_counts, slots, arrived, tables[0], new_linear, weights
    )
    answers = exchange(
        answer_rows(
            asked,
            lookup,
            sums,
            swapped(sums, ROLE_BIT),
            own_state,
            arrived[slots.shape[1] :],
            own_squares,
        )
    )
    half = collect(answers)
    base = arrange_rows(places, answers, fields)
    scores = cross_scores(
        base, cross_bias, out_weight.reshape(1, -1), half, swapped(half, CORE_BIT)
    )
    return (table_result[None], scores)


def solution(mesh):
    return jax.shard_map(
        on_device,
        mesh=mesh,
        in_specs=(
            P("role", "shard", None),
            P("shard", None),
            P("shard"),
            P("shard"),
            P("shard", None),
            P("role", None, None, None),
            P(),
            P("shard", None, None, None),
            P(),
            P(),
            P("role", "shard", None),
            P("role", "shard", None),
        ),
        out_specs=(P("role", "shard", None), P("role", "shard")),
        check_vma=False,
    )
```

time: 143 us -> 117 us (0.82)
  blocking collectives: 0 us -> 56.4 us
  starting transfers between devices: 74.4 us -> 18.1 us
  waiting for transfers between devices: 43.4 us -> 16.5 us
  local copies, waits for them, and re-layouts: 2.11 us -> 4.21 us
    ppermute x29 -> x3, starting transfers between devices: 59.7 us -> 1.88 us  [swapped(): lax.ppermute(value, BOTH, [(source, source ^ bits) for source in range(co...]
    all_to_all x0 -> x1, blocking collectives: none -> 56.4 us  [exchange(): lax.all_to_all(value, 'shard', split_axis=0, concat_axis=0, tiled=True)]
    ppermute x29 -> x3, waiting for transfers between devices: 43.4 us -> 2.49 us  [swapped(): lax.ppermute(value, BOTH, [(source, source ^ bits) for source in range(co...]
    all_to_all x1, waiting for transfers between devices: 0.01 us -> 14 us  [exchange(): lax.all_to_all(value, 'shard', split_axis=0, concat_axis=0, tiled=True)]
    unnamed x22 -> x26, local copies, waits for them, and re-layouts: 2.09 us -> 4.21 us
    all_to_all x1, starting transfers between devices: 13.4 us -> 14.9 us  [exchange(): lax.all_to_all(value, 'shard', split_axis=0, concat_axis=0, tiled=True)]
    pallas_call x5 -> x4, Pallas kernels: 4.29 us -> 4.06 us  [the longest x1 2.87 us: answer_rows(): kernel_call(answer_body, jax.ShapeDtypeStruct((SHARDS, CAP + CORES * SHAR...]
  transfers between devices with their start and end apart: 31 -> 5, of which waited for: 11 -> 2; matrix products, arithmetic and copies ran while one was open for 0% -> 0% of each run, Pallas kernels for 6% -> 8%
where the time goes in v3:
time: 117 us; the launch traced here: 116 us
  blocking collectives  56.4 us (48%)
  Pallas kernels  19.5 us (17%)
  starting transfers between devices  18.1 us (15%)
  waiting for transfers between devices  16.5 us (14%)
  local copies, waits for them, and re-layouts  4.21 us (4%)
  between operations  1.5 us (1%)
    all_to_all x1, blocking collectives, exchange(): lax.all_to_all(value, 'shard', split_axis=0, concat_axis=0, tiled=True)  56.4 us
    all_to_all x1, starting transfers between devices, exchange(): lax.all_to_all(value, 'shard', split_axis=0, concat_axis=0, tiled=True)  14.9 us
    all_to_all x1, waiting for transfers between devices, exchange(): lax.all_to_all(value, 'shard', split_axis=0, concat_axis=0, tiled=True)  14 us
    pallas_call x1, Pallas kernels, front(): kernel_call(front_body, (jax.ShapeDtypeStruct((8, examples), jnp.int32),...  4.73 us
    pallas_call x1, Pallas kernels, train_rows(): kernel_call(train_body, (jax.ShapeDtypeStruct((rows, width), jnp.float32)...  4.52 us
    unnamed x26, local copies, waits for them, and re-layouts  4.21 us
    pallas_call x1, Pallas kernels, answer_rows(): kernel_call(answer_body, jax.ShapeDtypeStruct((SHARDS, CAP + CORES * SHAR...  2.87 us
    pallas_call x1, Pallas kernels, arrange_rows(): kernel_call(arrange_body, jax.ShapeDtypeStruct((examples, fields * width)...  2.59 us
  transfers between devices with their start and end apart: 5, of which 2 were waited for; matrix products, arithmetic and copies ran while one was open for 0% of the time, Pallas kernels for 8%

profile of v3, /device:TPU:2, one launch (start us, length us, event | category | flops | bytes accessed | tf_op | source)
XLA Modules:
  0.0 116.2 jit_solution(4281809004034495951)
XLA Ops:
  0.7 4.7 %shard_map.131 = (s32[8,512]{1,0:T(8,128)}, f32[128,128]{1,0:T(8,128)}, f32[2,768,128]{2,1,0:T(8,128)}, f32[2,768,128]{2,1,0:T(8,128)}, f32[2,2,24,128]{3,2,1,0:T(8,128)}, /*index=5*/f32[2,2,24,128]{3,2,1,0:T(8,128)}) custom-call(s32[4,512]{1,0:T(4,128)} %bitcast.23, s32[4,512]{1,0:T(4,128)} %bitcast.24, f32[1536,512]{1,0:T(8,128)} %bitcast.20, ...), custom_call_target="tpu_custom_call" | custom-call | flops 10000000 | bytes 4000000 | tf_op jit(solution)/shard_map/pallas_call | solution.py:144
  5.4 0.0 copy-start
  5.4 0.0 copy-start.1
  5.4 0.1 collective-permute-start.1
  5.5 2.5 %collective-permute-done.1.arrived_ref = f32[2,768,128]{2,1,0:T(8,128)S(1)} collective-permute-done((f32[2,768,128]{2,1,0:T(8,128)}, f32[2,768,128]{2,1,0:T(8,128)S(1)}, u32[]{:S(2)}, u32[]{:S(2)}) %collective-permute-start.1) | collective-permute-done | bytes 786464 | tf_op jit(solution)/shard_map/ppermute | solution.py:521
  8.0 1.1 copy-done.4
  9.1 0.8 copy-done.6
  10.0 0.9 shard_map.134
  10.9 14.9 %all-to-all-start = ((bf16[128,16,128]{2,1,0:T(8,128)(2,1)}), bf16[128,16,128]{2,1,0:T(8,128)(2,1)S(1)}, u32[]{:S(2)}, u32[]{:S(2)}) async-start(bf16[128,16,128]{2,1,0:T(8,128)(2,1)} %shard_map.134), calls=%async_computation | async-start | bytes 1048576 | tf_op jit(solution)/shard_map/all_to_all | solution.py:525
  26.5 4.5 %shard_map.132 = (f32[2048,128]{1,0:T(8,128)S(1)}, bf16[2048,128]{1,0:T(8,128)(2,1)S(1)}, f32[608,128]{1,0:T(8,128)}) custom-call(s32[1]{0:T(128)S(6)} %copy.14.count_ref, s32[1,512]{1,0:T(1,128)S(1)} %bitcast.17, f32[2048,128]{1,0:T(8,128)S(1)} %bitcast.14, f32[2048,128]{1,0:T(8,128)S(1)} %copy-done.1, f32[512,128]{1,0:T(8,128)S(1)} %copy-done.5, ...), custom_call_target="tpu_custom_call" | custom-call | tf_op jit(solution)/shard_map/pallas_call | solution.py:258
  31.0 1.0 copy-done.2
  32.0 1.3 %collective-permute-start = (f32[608,128]{1,0:T(8,128)}, f32[608,128]{1,0:T(8,128)S(1)}, u32[]{:S(2)}, u32[]{:S(2)}) collective-permute-start(f32[608,128]{1,0:T(8,128)} %get-tuple-element.16), channel_id=1, source_target_pairs={{0,128},{1,129},{2,130},{3,131},{4,132},{5,133},{6,134},{7,135},{8... | collective-permute-start | bytes 933896 | tf_op jit(solution)/shard_map/ppermute | solution.py:556
  33.3 14.0 %all-to-all-done.packed_ref = bf16[128,16,128]{2,1,0:T(8,128)(2,1)S(1)} async-done(((bf16[128,16,128]{2,1,0:T(8,128)(2,1)}), bf16[128,16,128]{2,1,0:T(8,128)(2,1)S(1)}, u32[]{:S(2)}, u32[]{:S(2)}) %all-to-all-start) | async-done | bytes 524320 | tf_op jit(solution)/shard_map/all_to_all | solution.py:525
  47.3 0.1 shard_map.135
  47.4 1.5 %collective-permute-start.2 = (f32[2,16,128]{2,1,0:T(8,128)S(1)}, f32[2,16,128]{2,1,0:T(8,128)S(1)}, u32[]{:S(2)}, u32[]{:S(2)}) collective-permute-start(f32[2,16,128]{2,1,0:T(8,128)S(1)} %get-tuple-element.26.sum_ref), channel_id=1, source_target_pairs={{0,128},{1,129},{2,130},{3,131},{4,132},{5,133},{6,134},{7,135},{8... | collective-permute-start | bytes 49160 | tf_op jit(solution)/shard_map/ppermute | solution.py:521
  49.0 1.2 %copy-done.3 = f32[2048,128]{1,0:T(8,128)S(1)} copy-done((f32[2048,128]{1,0:T(8,128)S(1)}, f32[2048,128]{1,0:T(8,128)}, u32[]{:S(2)}) %copy-start.3) | copy-done | bytes 1048600
  50.2 1.7 %shard_map.133 = (f32[2048,128]{1,0:T(8,128)}, bf16[2048,128]{1,0:T(8,128)(2,1)S(1)}) custom-call(s32[1]{0:T(128)S(6)} %copy.14.count_ref, s32[1,512]{1,0:T(1,128)S(1)} %bitcast.18, f32[608,128]{1,0:T(8,128)S(1)} %collective-permute-done.arrived_ref, f32[2048,128]{1,0:T(8,128)S(1)} %bitcast.15, f32[2048,128]{1,0:T(8,128)S(1)} %copy-done.3, ...), custom_call_target="tpu_custom_call" | custom-call | tf_op jit(solution)/shard_map/pallas_call | solution.py:315
  51.9 2.9 %shard_map.136 = bf16[128,56,128]{2,1,0:T(8,128)(2,1)S(1)} custom-call(f32[128,128]{1,0:T(8,128)S(1)} %get-tuple-element.24.asked_ref, bf16[2048,128]{1,0:T(8,128)(2,1)S(1)} %get-tuple-element.25.table_ref, f32[2,16,128]{2,1,0:T(8,128)S(1)} %get-tuple-element.26.sum_ref, f32[2,16,128]{2,1,0:T(8,128)S(1)} %collective-permute-done.2.other_ref, ...), custom_call_target="tpu_custom_call" | custom-call | flops 2147483648 | bytes 2000000 | tf_op jit(solution)/shard_map/pallas_call | solution.py:407
  54.8 56.4 %all_to_all.10.answer_ref = bf16[128,56,128]{2,1,0:T(8,128)(2,1)S(1)} all-to-all(bf16[128,56,128]{2,1,0:T(8,128)(2,1)S(1)} %shard_map.136), channel_id=1, replica_groups=mesh['role'=2,'shard'=128] {'shard'}, dimensions={0} | all-to-all | bytes 3670016 | tf_op jit(solution)/shard_map/all_to_all | solution.py:525
  111.2 0.2 shard_map.138.own_ref
  111.4 0.3 collective-permute-start.3
  111.7 0.0 copy-start.12
  111.7 2.6 %shard_map.137.base_ref = bf16[512,512]{1,0:T(8,128)(2,1)S(1)} custom-call(s32[8,512]{1,0:T(8,128)S(1)} %copy-done.10, bf16[128,56,128]{2,1,0:T(8,128)(2,1)S(1)} %all_to_all.10.answer_ref), custom_call_target="tpu_custom_call" | custom-call | flops 2147483648 | bytes 2000000 | tf_op jit(solution)/shard_map/pallas_call | solution.py:468
  114.3 1.9 %shard_map.139 = f32[1,512]{1,0:T(1,128)} custom-call(bf16[512,512]{1,0:T(8,128)(2,1)S(1)} %shard_map.137.base_ref, f32[3,512]{1,0:T(4,128)S(1)} %copy-done.11, f32[1,512]{1,0:T(1,128)S(1)} %bitcast.19, bf16[768,512]{1,0:T(8,128)(2,1)S(1)} %shard_map.138.own_ref, bf16[768,512]{1,0:T(8,128)(2,1)S(1)} %collective-permute-done.3.other_ref), custom_call_target="tpu_custom_call" | custom-call | flops 805306368 | bytes 3000000 | tf_op jit(solution)/shard_map/pallas_call | solution.py:504
  (23 shorter events, 0.1 us)
Async XLA Ops:
  0.6 25.8 %copy-start.5 = (f32[512,128]{1,0:T(8,128)S(1)}, f32[512,128]{1,0:T(8,128)}, u32[]{:S(2)}) copy-start(f32[512,128]{1,0:T(8,128)} %grad_ref.1) | copy-start | bytes 786436
  0.6 25.8 %copy-start.8 = (s32[512]{0:T(512)S(1)}, s32[512]{0:T(512)}, u32[]{:S(2)}) copy-start(s32[512]{0:T(512)} %param.14) | copy-start | bytes 6148
  5.4 21.1 %copy-start = (f32[1,2048,128]{2,1,0:T(8,128)S(1)}, f32[1,2048,128]{2,1,0:T(8,128)}, u32[]{:S(2)}) copy-start(f32[1,2048,128]{2,1,0:T(8,128)} %param.12) | copy-start | bytes 3145732
  5.4 21.1 %copy-start.1 = (f32[2048,128]{1,0:T(8,128)S(1)}, f32[2048,128]{1,0:T(8,128)}, u32[]{:S(2)}) copy-start(f32[2048,128]{1,0:T(8,128)} %square_ref.1) | copy-start | bytes 3145732
  5.4 2.6 %collective-permute-start.1 = (f32[2,768,128]{2,1,0:T(8,128)}, f32[2,768,128]{2,1,0:T(8,128)S(1)}, u32[]{:S(2)}, u32[]{:S(2)}) collective-permute-start(f32[2,768,128]{2,1,0:T(8,128)} %get-tuple-element.22), channel_id=1, source_target_pairs={{0,1},{1,0},{2,3},{3,2},{4,5},{5,4},{6,7},{7,6},{8,9},{9,8},{10,11... | collective-permute-start | bytes 2359304 | tf_op jit(solution)/shard_map/ppermute | solution.py:521
  8.0 1.1 copy-start.4
  9.1 0.8 copy-start.6
  10.0 16.5 %copy-start.7 = (f32[2,2,24,128]{3,2,1,0:T(8,128)S(1)}, f32[2,2,24,128]{3,2,1,0:T(8,128)}, u32[]{:S(2)}) copy-start(f32[2,2,24,128]{3,2,1,0:T(8,128)} %get-tuple-element.15.state_ref) | copy-start | bytes 147460
  10.9 36.4 %all-to-all-start = ((bf16[128,16,128]{2,1,0:T(8,128)(2,1)}), bf16[128,16,128]{2,1,0:T(8,128)(2,1)S(1)}, u32[]{:S(2)}, u32[]{:S(2)}) async-start(bf16[128,16,128]{2,1,0:T(8,128)(2,1)} %shard_map.134), calls=%async_computation | async-start | bytes 1048576 | tf_op jit(solution)/shard_map/all_to_all | solution.py:525
  25.8 26.1 %copy-start.9 = (f32[2,2,24,128]{3,2,1,0:T(8,128)S(1)}, f32[2,2,24,128]{3,2,1,0:T(8,128)}, u32[]{:S(2)}) copy-start(f32[2,2,24,128]{3,2,1,0:T(8,128)} %get-tuple-element.27.square_ref) | copy-start | bytes 147460
  31.0 1.0 copy-start.2
  32.0 16.9 %collective-permute-start = (f32[608,128]{1,0:T(8,128)}, f32[608,128]{1,0:T(8,128)S(1)}, u32[]{:S(2)}, u32[]{:S(2)}) collective-permute-start(f32[608,128]{1,0:T(8,128)} %get-tuple-element.16), channel_id=1, source_target_pairs={{0,128},{1,129},{2,130},{3,131},{4,132},{5,133},{6,134},{7,135},{8... | collective-permute-start | bytes 933896 | tf_op jit(solution)/shard_map/ppermute | solution.py:556
  47.4 4.5 %collective-permute-start.2 = (f32[2,16,128]{2,1,0:T(8,128)S(1)}, f32[2,16,128]{2,1,0:T(8,128)S(1)}, u32[]{:S(2)}, u32[]{:S(2)}) collective-permute-start(f32[2,16,128]{2,1,0:T(8,128)S(1)} %get-tuple-element.26.sum_ref), channel_id=1, source_target_pairs={{0,128},{1,129},{2,130},{3,131},{4,132},{5,133},{6,134},{7,135},{8... | collective-permute-start | bytes 49160 | tf_op jit(solution)/shard_map/ppermute | solution.py:521
  49.0 1.2 %copy-start.3 = (f32[2048,128]{1,0:T(8,128)S(1)}, f32[2048,128]{1,0:T(8,128)}, u32[]{:S(2)}) copy-start(f32[2048,128]{1,0:T(8,128)} %copy-done.2) | copy-start | bytes 3145732
  54.8 56.9 %copy-start.10 = (s32[8,512]{1,0:T(8,128)S(1)}, s32[8,512]{1,0:T(8,128)}, u32[]{:S(2)}) copy-start(s32[8,512]{1,0:T(8,128)} %get-tuple-element.20.place_ref) | copy-start | bytes 49156
  111.4 2.9 %collective-permute-start.3 = (bf16[768,512]{1,0:T(8,128)(2,1)S(1)}, bf16[768,512]{1,0:T(8,128)(2,1)S(1)}, u32[]{:S(2)}, u32[]{:S(2)}) collective-permute-start(bf16[768,512]{1,0:T(8,128)(2,1)S(1)} %shard_map.138.own_ref), channel_id=1, source_target_pairs={{0,1},{1,0},{2,3},{3,2},{4,5},{5,4},{6,7},{7,6},{8,9},{9,8},{10,11... | collective-permute-start | bytes 2359304 | tf_op jit(solution)/shard_map/ppermute | solution.py:521
  111.7 2.6 %copy-start.11 = (f32[3,512]{1,0:T(4,128)S(1)}, f32[3,512]{1,0:T(4,128)}, u32[]{:S(2)}) copy-start(f32[3,512]{1,0:T(4,128)} %bias_ref.1) | copy-start | bytes 18436
  111.7 2.6 %copy-start.12 = (f32[512]{0:T(512)S(1)}, f32[512]{0:T(512)}, u32[]{:S(2)}) copy-start(f32[512]{0:T(512)} %param.21) | copy-start | bytes 6148

commit v4 on v3

--- a/solution.py
+++ b/solution.py
@@ -11,11 +11,13 @@
 LANES = 128
 SHARDS = 128
 ROLES = 2
-CORES = 2
+Z_SIZE, Y_SIZE, X_SIZE, CORES = 8, 4, 2, 2
+BLOCKS = Z_SIZE * Y_SIZE
+Z_ORDER = (0, 1, 7, 3, 4, 2, 5, 6)
 TILES = 2
 SHARE = 12
 PACKED = 16
-VMEM_LIMIT = 40 * 1024 * 1024
+VMEM_LIMIT = 24 * 1024 * 1024
 
 
 def ftrl_weight(linear, squares, shrink):
@@ -48,6 +50,7 @@
 VMEM = pl.BlockSpec(memory_space=pltpu.VMEM)
 SMEM = pl.BlockSpec(memory_space=pltpu.SMEM)
 ANY = pl.BlockSpec(memory_space=pl.ANY)
+HBM = pl.BlockSpec(memory_space=pltpu.HBM)
 
 
 def position():
@@ -55,49 +58,55 @@
     return lax.axis_index("role"), shard, lax.rem(shard, CORES)
 
 
-def piece_copies(array_ref, own_ref):
-    _, shard, _ = position()
-    rows = array_ref.shape[0] // ROLES
-    pairs = []
-    for half in range(ROLES):
-        first = pl.multiple_of(half * rows + shard // 4 * (2 * SHARE), 2 * SHARE)
-        for core in range(CORES):
-            left = pl.multiple_of((core * TILES + lax.rem(shard, TILES)) * LANES, LANES)
-            pairs.append(
-                (
-                    array_ref.at[pl.ds(first, 2 * SHARE), pl.ds(left, LANES)],
-                    own_ref.at[half, core],
+def half_copies(grad_ref, target_ref, flip, arrived):
+    role, _, core = position()
+    copies = []
+    for tile in range(TILES):
+        left = pl.multiple_of(((core ^ flip) * TILES + tile) * LANES, LANES)
+        copies.append(
+            pltpu.make_async_copy(
+                grad_ref.at[:, role, :, pl.ds(left, LANES)], target_ref.at[tile], arrived.at[tile]
+            )
+        )
+    return copies
+
+
+def fetch_body(grad_ref, state_ref, square_ref, send_ref, keep_ref, own_state_ref, own_square_ref, arrived):
+    _, shard, core = position()
+    copies = half_copies(grad_ref, send_ref, 1, arrived.at[:TILES])
+    copies += half_copies(grad_ref, keep_ref, 0, arrived.at[TILES : 2 * TILES])
+    block = shard // (X_SIZE * CORES)
+    for source, target in ((state_ref, own_state_ref), (square_ref, own_square_ref)):
+        for column in range(CORES):
+            left = pl.multiple_of((column * TILES + core) * LANES, LANES)
+            copies.append(
+                pltpu.make_async_copy(
+                    source.at[block, :, :, pl.ds(left, LANES)],
+                    target.at[column],
+                    arrived.at[len(copies)],
                 )
             )
-    return pairs
-
-
-def half_copies(grad_ref, send_ref, keep_ref):
-    role, _, core = position()
-    rows = grad_ref.shape[0] // ROLES
-    pairs = []
-    for flip, target in ((1, send_ref), (0, keep_ref)):
-        for tile in range(TILES):
-            left = pl.multiple_of(((core ^ flip) * TILES + tile) * LANES, LANES)
-            first = pl.multiple_of(role * rows, rows)
-            pairs.append(
-                (grad_ref.at[pl.ds(first, rows), pl.ds(left, LANES)], target.at[tile])
-            )
-    return pairs
-
-
-def front_body(owner_ref, slot_ref, grad_ref, state_ref, square_ref, place_ref, request_ref, send_ref, keep_ref, own_state_ref, own_square_ref, arrived):
-    pairs = (
-        half_copies(grad_ref, send_ref, keep_ref)
-        + piece_copies(state_ref, own_state_ref)
-        + piece_copies(square_ref, own_square_ref)
-    )
-    copies = [
-        pltpu.make_async_copy(source, target, arrived.at[at])
-        for at, (source, target) in enumerate(pairs)
-    ]
     for copy in copies:
         copy.start()
+    for copy in copies:
+        copy.wait()
+
+
+def fetch(grads, state, squares):
+    halves = jax.ShapeDtypeStruct((TILES, BLOCKS, 2 * SHARE, LANES), jnp.float32)
+    own = jax.ShapeDtypeStruct((CORES, ROLES, 2 * SHARE, LANES), jnp.float32)
+    return kernel_call(
+        fetch_body,
+        (halves, halves, own, own),
+        bytes_accessed=4_000_000,
+        vmem=52 * 1024 * 1024,
+        in_specs=[HBM] * 3,
+        out_specs=(VMEM,) * 4,
+        scratch_shapes=[pltpu.SemaphoreType.DMA((2 * TILES + 2 * CORES,))],
+    )(grads, state, squares)
+
+
+def route_body(owner_ref, slot_ref, place_ref, request_ref):
     fields, examples = owner_ref.shape
     shape = (SHARDS, examples)
     shard_ids = iota(shape, 0)
@@ -133,40 +142,27 @@
     request_ref[...] = jnp.concatenate(
         [asked >> 4, asked & 15, jnp.zeros((SHARDS, LANES - 2 * CAP), jnp.int32)], axis=1
     ).astype(jnp.float32)
-    for copy in copies:
-        copy.wait()
-
-
-def front(owners, slots, grads, state, squares):
-    fields, examples = owners.shape
-    halves = jax.ShapeDtypeStruct((TILES, grads.shape[0] // ROLES, LANES), jnp.float32)
-    own = jax.ShapeDtypeStruct((ROLES, CORES, 2 * SHARE, LANES), jnp.float32)
-    return kernel_call(
-        front_body,
+
+
+def route(owners, slots):
+    examples = owners.shape[1]
+    return kernel_call(
+        route_body,
         (
             jax.ShapeDtypeStruct((8, examples), jnp.int32),
             jax.ShapeDtypeStruct((SHARDS, LANES), jnp.float32),
-            halves,
-            halves,
-            own,
-            own,
         ),
-        flops=10_000_000,
-        bytes_accessed=4_000_000,
-        vmem=60 * 1024 * 1024,
-        in_specs=[VMEM, VMEM, ANY, ANY, ANY],
-        out_specs=(VMEM,) * 6,
-        scratch_shapes=[pltpu.SemaphoreType.DMA((2 * TILES + 4 * ROLES,))],
-    )(owners, slots, grads, state, squares)
+        in_specs=[VMEM, VMEM],
+        out_specs=(VMEM, VMEM),
+    )(owners, slots)
 
 
 def pack_body(keep_ref, arrived_ref, request_ref, packed_ref):
-    for block in range(SHARDS // 4):
-        rows = slice(block * 2 * SHARE, (block + 1) * 2 * SHARE)
+    for block in range(BLOCKS):
         for tile in range(TILES):
-            terms = keep_ref[tile, rows, :] + arrived_ref[tile, rows, :]
-            for part in range(2):
-                shard = block * 4 + part * TILES + tile
+            terms = keep_ref[tile, block] + arrived_ref[tile, block]
+            for part in range(X_SIZE):
+                shard = (block * X_SIZE + part) * CORES + tile
                 packed_ref[shard] = jnp.concatenate(
                     [
                         terms[part * SHARE : (part + 1) * SHARE, :],
@@ -186,7 +182,7 @@
     )(keep, arrived, requests)
 
 
-def unpack_body(packed_ref, sum_ref, asked_ref):
+def unpack_body(packed_ref, lookup_ref, sum_ref, asked_ref):
     for core in range(CORES):
         total = jnp.zeros((PACKED, LANES), jnp.float32)
         for shard in range(core, SHARDS, CORES):
@@ -196,16 +192,16 @@
         sum_ref[core] = total
 
 
-def unpack(packed):
+def unpack(packed, lookup):
     return kernel_call(
         unpack_body,
         (
             jax.ShapeDtypeStruct((CORES, PACKED, LANES), jnp.float32),
             jax.ShapeDtypeStruct((SHARDS, LANES), jnp.float32),
         ),
-        in_specs=[VMEM],
+        in_specs=[VMEM, ANY],
         out_specs=(VMEM, VMEM),
-    )(packed)
+    )(packed, lookup)
 
 
 def used_slots(slot_ref, count):
@@ -218,7 +214,7 @@
     return jnp.where(hit, 1.0, 0.0).astype(jnp.bfloat16)
 
 
-def train_body(count_ref, slot_ref, held_ref, square_ref, grad_ref, state_ref, new_ref, weight_ref, fresh_ref, parts, total):
+def train_body(count_ref, slot_ref, held_ref, square_ref, grad_ref, new_ref, weight_ref, fresh_ref, parts, total):
     step = pl.program_id(0)
     rows = held_ref.shape[0]
 
@@ -245,12 +241,10 @@
 
     @pl.when(step == pl.num_programs(0) - 1)
     def _():
-        updates = total.shape[0]
-        fresh_ref[:updates, :] = total[...]
-        fresh_ref[updates:, :] = state_ref[...]
-
-
-def train_rows(count, slots, held, squares, grads, state):
+        fresh_ref[...] = total[...].astype(jnp.bfloat16)
+
+
+def train_rows(count, slots, held, squares, grads):
     rows, width = held.shape
     updates = grads.shape[0]
     block = 512
@@ -260,7 +254,7 @@
         (
             jax.ShapeDtypeStruct((rows, width), jnp.float32),
             jax.ShapeDtypeStruct((rows, width), jnp.bfloat16),
-            jax.ShapeDtypeStruct((updates + state.shape[0], width), jnp.float32),
+            jax.ShapeDtypeStruct((updates, width), jnp.bfloat16),
         ),
         grid=(rows // block,),
         in_specs=[
@@ -269,18 +263,17 @@
             by_rows,
             by_rows,
             pl.BlockSpec((updates, width), lambda i: (0, 0)),
-            pl.BlockSpec(state.shape, lambda i: (0, 0)),
         ],
         out_specs=(
             by_rows,
             by_rows,
-            pl.BlockSpec((updates + state.shape[0], width), lambda i: (0, 0)),
+            pl.BlockSpec((updates, width), lambda i: (0, 0)),
         ),
         scratch_shapes=[
             pltpu.VMEM((updates, 3 * width), jnp.bfloat16),
             pltpu.VMEM((updates, width), jnp.float32),
         ],
-    )(count, slots, held, squares, grads, state)
+    )(count, slots, held, squares, grads)
 
 
 def serve_body(count_ref, slot_ref, arrived_ref, held_ref, new_ref, weight_ref, table_ref, lookup_ref):
@@ -296,7 +289,7 @@
     @pl.when(role != 0)
     def _():
         spread = rows_of_block(used_slots(slot_ref, count_ref[0]), step * rows, rows)
-        arrived = arrived_ref[: slot_ref.shape[1], :].astype(jnp.bfloat16)
+        arrived = arrived_ref[...]
         sums = jnp.dot(
             spread,
             jnp.concatenate([arrived, jnp.ones_like(arrived)], axis=1),
@@ -353,32 +346,38 @@
     target_ref[:, LANES:] = source_ref[height:, :]
 
 
-def piece_weights(sum_ref, other_ref, state_ref, trained_ref, square_ref):
+def piece_body(sum_ref, other_ref, state_ref, trained_ref, square_ref, answer_ref, piece_ref):
     role, shard, _ = position()
-    later = lax.rem(shard // TILES, 2) == 1
+    later = lax.rem(shard // CORES, X_SIZE) == 1
 
     def own(values):
         return jnp.where(later, values[SHARE : 2 * SHARE, :], values[:SHARE, :])
 
-    halves = []
+    parts = []
     for half in range(ROLES):
-        parts = []
-        for core in range(CORES):
-            gradient = jnp.where(role == half, sum_ref[core], other_ref[core])[:SHARE, :]
-            first = (half * CORES + core) * 2 * SHARE
-            state = own(state_ref[half, core])
-            trained = own(trained_ref[first : first + 2 * SHARE, :])
+        for column in range(CORES):
+            gradient = jnp.where(role == half, sum_ref[column], other_ref[column])[:SHARE, :]
+            state = own(state_ref[column, half])
+            trained = own(trained_ref[column, half])
             linear = jnp.where(role == 0, state, trained)
             dense_linear, dense_sumsq, prior = ftrl_step(
-                linear, own(square_ref[half, core]), gradient, DENSE_SHRINK
+                linear, own(square_ref[column, half]), gradient, DENSE_SHRINK
             )
             fresh = ftrl_weight(dense_linear, dense_sumsq, DENSE_SHRINK)
             parts.append(jnp.where(role == 0, fresh, state + (fresh - prior)))
-        halves.append(jnp.concatenate(parts, axis=0).astype(jnp.bfloat16))
-    return halves
-
-
-def answer_body(asked_ref, table_ref, sum_ref, other_ref, state_ref, trained_ref, square_ref, answer_ref, columns, folded):
+    piece_ref[...] = jnp.concatenate(parts, axis=0).astype(jnp.bfloat16)
+
+
+def piece_weights(sums, other, state, trained, squares, answers):
+    return kernel_call(
+        piece_body,
+        jax.ShapeDtypeStruct((ROLES * CORES * SHARE, LANES), jnp.bfloat16),
+        in_specs=[VMEM] * 5 + [ANY],
+        out_specs=VMEM,
+    )(sums, other, state, trained, squares, answers)
+
+
+def answer_body(asked_ref, table_ref, answer_ref, columns, folded):
     digits = asked_ref[...]
     wide = jnp.concatenate(
         [
@@ -389,70 +388,77 @@
     )
     columns[...] = jnp.transpose(wide)[:CAP, :].astype(jnp.int32)
     fold(table_ref, folded)
-    halves = piece_weights(sum_ref, other_ref, state_ref, trained_ref, square_ref)
     group = 8
     for at in range(0, SHARDS, group):
         asked = jnp.concatenate(
             [columns[:, shard : shard + 1] for shard in range(at, at + group)], axis=0
         )
-        found = looked_up(asked, folded[...])
-        for part in range(group):
-            answer_ref[at + part] = jnp.concatenate(
-                [found[part * CAP : (part + 1) * CAP, :], halves[(at + part) % CORES]], axis=0
-            )
-
-
-def answer_rows(asked, table, sums, other_sums, state, trained, squares):
+        answer_ref[at * CAP : (at + group) * CAP, :] = looked_up(asked, folded[...])
+
+
+def answer_rows(asked, table):
     rows, width = table.shape
     return kernel_call(
         answer_body,
-        jax.ShapeDtypeStruct((SHARDS, CAP + CORES * SHARE, width), jnp.bfloat16),
-        flops=2 * SHARDS * CAP * rows * width,
-        bytes_accessed=2_000_000,
-        in_specs=[VMEM] * 7,
+        jax.ShapeDtypeStruct((SHARDS * CAP, width), jnp.bfloat16),
+        in_specs=[VMEM] * 2,
         out_specs=VMEM,
         scratch_shapes=[
             pltpu.VMEM((CAP, SHARDS), jnp.int32),
             pltpu.VMEM((rows // 2, 2 * width), jnp.bfloat16),
         ],
-    )(asked, table, sums, other_sums, state, trained, squares)
-
-
-def collect_body(answer_ref, half_ref):
-    for block in range(SHARDS // 8):
-        for core in range(CORES):
-            for tile in range(TILES):
-                first = CAP + core * SHARE
-                parts = [
-                    answer_ref[block * 8 + part * TILES + tile].astype(jnp.float32)[
-                        first : first + SHARE, :
-                    ]
-                    for part in range(4)
-                ]
-                left = (core * TILES + tile) * LANES
-                half_ref[block * 4 * SHARE : (block + 1) * 4 * SHARE, left : left + LANES] = (
-                    jnp.concatenate(parts, axis=0).astype(jnp.bfloat16)
-                )
-
-
-def collect(answers):
+    )(asked, table)
+
+
+def after_body(value_ref, other_ref, out_ref):
+    del value_ref, other_ref, out_ref
+
+
+def after(value, other):
+    return kernel_call(
+        after_body,
+        jax.ShapeDtypeStruct(value.shape, value.dtype),
+        in_specs=[ANY, ANY],
+        out_specs=ANY,
+        input_output_aliases={0: 0},
+    )(value, other)
+
+
+def collect_body(*refs):
+    piece_refs, tile_ref = refs[:Y_SIZE], refs[Y_SIZE]
+    _, shard, _ = position()
+    x = lax.rem(shard // CORES, X_SIZE)
+    y = lax.rem(shard // (X_SIZE * CORES), Y_SIZE)
+    z = shard // (Y_SIZE * X_SIZE * CORES)
+    piece = ROLES * CORES * SHARE
+    for y_flip, ref in enumerate(piece_refs):
+        for at, steps in enumerate(Z_ORDER):
+            near = ref[at * piece : (at + 1) * piece, :].astype(jnp.float32)
+            far = ref[(Z_SIZE + at) * piece : (Z_SIZE + at + 1) * piece, :].astype(jnp.float32)
+            first, second = jnp.where(x == 0, near, far), jnp.where(x == 0, far, near)
+            block = lax.rem(z + steps, Z_SIZE) * Y_SIZE + (y ^ y_flip)
+            rows = pl.ds(pl.multiple_of(block * piece, piece), piece)
+            for column in range(CORES):
+                parts = []
+                for half in range(ROLES):
+                    start = (half * CORES + column) * SHARE
+                    parts += [values[start : start + SHARE, :] for values in (first, second)]
+                tile_ref[column, rows, :] = jnp.concatenate(parts, axis=0).astype(jnp.bfloat16)
+
+
+def collect(pieces):
+    rows = BLOCKS * ROLES * X_SIZE * SHARE
     return kernel_call(
         collect_body,
-        jax.ShapeDtypeStruct(
-            (SHARDS // 2 * SHARE, CORES * TILES * LANES), jnp.bfloat16
-        ),
-        in_specs=[VMEM],
+        jax.ShapeDtypeStruct((CORES, rows, LANES), jnp.bfloat16),
+        in_specs=[VMEM] * Y_SIZE,
         out_specs=VMEM,
-    )(answers)
+    )(*pieces)
 
 
 def arrange_body(place_ref, answer_ref, base_ref, columns, folded):
     columns[...] = jnp.transpose(place_ref[...])
-    for shard in range(SHARDS):
-        side, at = divmod(shard, SHARDS // 2)
-        folded[at * CAP : (at + 1) * CAP, side * LANES : (side + 1) * LANES] = answer_ref[shard][
-            :CAP, :
-        ]
+    fold(answer_ref, folded)
     examples = columns.shape[0]
     block = 256
     for field in range(base_ref.shape[1] // LANES):
@@ -464,7 +470,7 @@
 
 def arrange_rows(places, answers, fields):
     examples = places.shape[1]
-    rows, width = SHARDS * CAP, answers.shape[2]
+    rows, width = answers.shape
     return kernel_call(
         arrange_body,
         jax.ShapeDtypeStruct((examples, fields * width), jnp.bfloat16),
@@ -481,9 +487,10 @@
 
 def cross_body(base_ref, bias_ref, out_ref, own_ref, other_ref, score_ref, weights):
     _, _, core = position()
-    rows = own_ref.shape[0]
-    weights[pl.ds(pl.multiple_of(core * rows, rows), rows), :] = own_ref[...]
-    weights[pl.ds(pl.multiple_of((1 - core) * rows, rows), rows), :] = other_ref[...]
+    for column in range(CORES):
+        for flip, tile_ref in ((0, own_ref), (1, other_ref)):
+            left = pl.multiple_of((column * TILES + (core ^ flip)) * LANES, LANES)
+            weights[:, pl.ds(left, LANES)] = tile_ref[column]
     width = base_ref.shape[1]
     base = base_ref[...].astype(jnp.float32)
     crossed = base
@@ -513,12 +520,21 @@
 
 
 BOTH = ("role", "shard")
-CORE_BIT, ROLE_BIT = 1, 128
+CORE_BIT, X_BIT, Y_BIT, ROLE_BIT = 1, 2, 4, 128
 
 
 def swapped(value, bits):
     count = ROLES * SHARDS
     return lax.ppermute(value, BOTH, [(source, source ^ bits) for source in range(count)])
+
+
+def from_ahead(value, steps):
+    span = SHARDS // Z_SIZE
+    return lax.ppermute(
+        value,
+        "shard",
+        [((source + steps * span) % SHARDS, source) for source in range(SHARDS)],
+    )
 
 
 def exchange(value):
@@ -540,38 +556,42 @@
     cand_slot,
 ):
     fields = cand_owner.shape[2]
-    rows = dense_squares.shape[0] * dense_squares.shape[1]
-    places, requests, send, keep, own_state, own_squares = front(
-        cand_owner[0].T,
-        cand_slot[0].T,
-        dense_grads[0].reshape(rows, -1),
-        dense_state[0].reshape(rows, -1),
-        dense_squares.reshape(rows, -1),
-    )
-    sums, asked = unpack(exchange(pack(keep, swapped(send, CORE_BIT), requests)))
+    blocks = (BLOCKS, ROLES, 2 * SHARE, dense_squares.shape[2])
+    grads = dense_grads.reshape(blocks)
+    send, keep, own_state, own_squares = fetch(
+        grads, dense_state.reshape(blocks), dense_squares.reshape(blocks)
+    )
+    paired = swapped(send, CORE_BIT)
+    trained = lax.ppermute(own_state, "role", [(0, 1)])
+    places, requests = route(cand_owner[0].T, cand_slot[0].T)
+    packed = exchange(pack(keep, paired, requests))
     slots = update_slots.reshape(1, -1)
     new_linear, weights, fresh = train_rows(
-        update_counts, slots, tables[0], row_squares, row_grads, own_state.reshape(-1, LANES)
+        update_counts, slots, tables[0], row_squares, row_grads
     )
     arrived = lax.ppermute(fresh, "role", [(0, 1)])
     table_result, lookup = serve_rows(
         update_counts, slots, arrived, tables[0], new_linear, weights
     )
-    answers = exchange(
-        answer_rows(
-            asked,
-            lookup,
-            sums,
-            swapped(sums, ROLE_BIT),
-            own_state,
-            arrived[slots.shape[1] :],
-            own_squares,
-        )
-    )
-    half = collect(answers)
-    base = arrange_rows(places, answers, fields)
+    sums, asked = unpack(packed, lookup)
+    answers = answer_rows(asked, lookup)
+    piece = piece_weights(
+        sums, swapped(sums, ROLE_BIT), own_state, trained, own_squares, answers
+    )
+    near = [piece, from_ahead(piece, 1), from_ahead(piece, -1)]
+    three = jnp.concatenate(near, axis=0)
+    pieces = jnp.concatenate(
+        [three, from_ahead(three, 3), from_ahead(three[: 2 * piece.shape[0]], -3)], axis=0
+    )
+    answers = after(answers, pieces)
+    answered = exchange(answers.reshape(SHARDS, CAP, LANES))
+    pieces = jnp.concatenate([pieces, swapped(pieces, X_BIT)], axis=0)
+    tiles = collect(
+        [pieces] + [swapped(pieces, flip * Y_BIT) for flip in range(1, Y_SIZE)]
+    )
+    base = arrange_rows(places, answered.reshape(SHARDS * CAP, LANES), fields)
     scores = cross_scores(
-        base, cross_bias, out_weight.reshape(1, -1), half, swapped(half, CORE_BIT)
+        base, cross_bias, out_weight.reshape(1, -1), tiles, swapped(tiles, CORE_BIT)
     )
     return (table_result[None], scores)
 

time: 117 us -> 106 us (0.906)
  blocking collectives: 56.4 us -> 0 us
  starting transfers between devices: 18.1 us -> 44.3 us
  waiting for transfers between devices: 16.5 us -> 41.3 us
  local copies, waits for them, and re-layouts: 4.21 us -> 0.1 us
  Pallas kernels: 19.5 us -> 18.3 us
    all_to_all x1 -> x0, blocking collectives: 56.4 us -> none  [exchange(): lax.all_to_all(value, 'shard', split_axis=0, concat_axis=0, tiled=True)]
    ppermute x3 -> x7, waiting for transfers between devices: 2.49 us -> 21.6 us  [swapped(): lax.ppermute(value, BOTH, [(source, source ^ bits) for source in range(co...]
    all_to_all x1 -> x2, starting transfers between devices: 14.9 us -> 24.7 us  [exchange(): lax.all_to_all(value, 'shard', split_axis=0, concat_axis=0, tiled=True)]
    ppermute x0 -> x5, starting transfers between devices: none -> 9.64 us  [the longest x4 8.35 us: from_ahead(): lax.ppermute(value, 'shard', [((source + steps * span) % SHARDS, source)...]
    ppermute x1, waiting for transfers between devices: 0.01 us -> 7.22 us  [on_device(): arrived = lax.ppermute(fresh, 'role', [(0, 1)])]
    ppermute x3 -> x7, starting transfers between devices: 1.88 us -> 8.67 us  [swapped(): lax.ppermute(value, BOTH, [(source, source ^ bits) for source in range(co...]
    all_to_all x1 -> x2, waiting for transfers between devices: 14 us -> 9.22 us  [exchange(): lax.all_to_all(value, 'shard', split_axis=0, concat_axis=0, tiled=True)]
    unnamed x26 -> x21, local copies, waits for them, and re-layouts: 4.21 us -> 0.09 us
  transfers between devices with their start and end apart: 5 -> 15, of which waited for: 2 -> 10; matrix products, arithmetic and copies ran while one was open for 0% -> 0% of each run, Pallas kernels for 8% -> 13%
where the time goes in v4:
time: 106 us; the launch traced here: 105 us
  starting transfers between devices  44.3 us (42%)
  waiting for transfers between devices  41.3 us (39%)
  Pallas kernels  18.3 us (17%)
  between operations  1.52 us (1%)
    all_to_all x2, starting transfers between devices, exchange(): lax.all_to_all(value, 'shard', split_axis=0, concat_axis=0, tiled=True)  24.7 us
    ppermute x7, waiting for transfers between devices, swapped(): lax.ppermute(value, BOTH, [(source, source ^ bits) for source in range(co...  21.6 us
    all_to_all x2, waiting for transfers between devices, exchange(): lax.all_to_all(value, 'shard', split_axis=0, concat_axis=0, tiled=True)  9.22 us
    ppermute x7, starting transfers between devices, swapped(): lax.ppermute(value, BOTH, [(source, source ^ bits) for source in range(co...  8.67 us
    ppermute x4, starting transfers between devices, from_ahead(): lax.ppermute(value, 'shard', [((source + steps * span) % SHARDS, source)...  8.35 us
    ppermute x1, waiting for transfers between devices, on_device(): arrived = lax.ppermute(fresh, 'role', [(0, 1)])  7.22 us
    pallas_call x1, Pallas kernels, answer_rows(): kernel_call(answer_body, jax.ShapeDtypeStruct((SHARDS * CAP, width), jnp....  3.84 us
    pallas_call x1, Pallas kernels, train_rows(): kernel_call(train_body, (jax.ShapeDtypeStruct((rows, width), jnp.float32)...  3.77 us
  transfers between devices with their start and end apart: 15, of which 10 were waited for; matrix products, arithmetic and copies ran while one was open for 0% of the time, Pallas kernels for 13%

profile of v4, /device:TPU:2, one launch (start us, length us, event | category | flops | bytes accessed | tf_op | source)
XLA Modules:
  0.0 105.4 jit_solution(10389619429819851605)
XLA Ops:
  0.7 1.5 %shard_map.134 = (f32[2,32,24,128]{3,2,1,0:T(8,128)S(1)}, f32[2,32,24,128]{3,2,1,0:T(8,128)S(1)}, f32[2,2,24,128]{3,2,1,0:T(8,128)S(1)}, f32[2,2,24,128]{3,2,1,0:T(8,128)S(1)}) custom-call(f32[32,2,24,512]{3,2,1,0:T(8,128)} %bitcast.23, f32[32,2,24,512]{3,2,1,0:T(8,128)} %bitcast.24, f32[32,2,24,512]{3,2,1,0:T(8,128)} %bitcast.25), custom_call_target="tpu_custom_call" | custom-call | bytes 4000000 | tf_op jit(solution)/shard_map/pallas_call | solution.py:98
  2.3 1.4 %shard_map.133 = (s32[8,512]{1,0:T(8,128)S(1)}, f32[128,128]{1,0:T(8,128)S(1)}) custom-call(s32[4,512]{1,0:T(4,128)S(1)} %bitcast.18, s32[4,512]{1,0:T(4,128)S(1)} %bitcast.19), custom_call_target="tpu_custom_call" | custom-call | tf_op jit(solution)/shard_map/pallas_call | solution.py:149
  5.5 14.9 %all-to-all-start = ((bf16[128,16,128]{2,1,0:T(8,128)(2,1)}), bf16[128,16,128]{2,1,0:T(8,128)(2,1)S(1)}, u32[]{:S(2)}, u32[]{:S(2)}) async-start(bf16[128,16,128]{2,1,0:T(8,128)(2,1)} %shard_map.135), calls=%async_computation | async-start | bytes 1048576 | tf_op jit(solution)/shard_map/all_to_all | solution.py:541
  21.1 3.8 %shard_map.131 = (f32[2048,128]{1,0:T(8,128)S(1)}, bf16[2048,128]{1,0:T(8,128)(2,1)S(1)}, bf16[512,128]{1,0:T(8,128)(2,1)S(1)}) custom-call(s32[1]{0:T(128)S(6)} %copy.25.count_ref, s32[1,512]{1,0:T(1,128)S(1)} %bitcast.20, f32[2048,128]{1,0:T(8,128)S(1)} %bitcast.15, f32[2048,128]{1,0:T(8,128)S(1)} %copy-done.1, f32[512,128]{1,0:T(8,128)S(1)} %copy-done.2), custom_call_target="tpu_custom_call" | custom-call | tf_op jit(solution)/shard_map/pallas_call | solution.py:252
  24.8 1.3 %collective-permute-start = (bf16[512,128]{1,0:T(8,128)(2,1)S(1)}, bf16[512,128]{1,0:T(8,128)(2,1)S(1)}, u32[]{:S(2)}, u32[]{:S(2)}) collective-permute-start(bf16[512,128]{1,0:T(8,128)(2,1)S(1)} %get-tuple-element.15), channel_id=1, source_target_pairs={{0,128},{1,129},{2,130},{3,131},{4,132},{5,133},{6,134},{7,135},{8... | collective-permute-start | bytes 393224 | tf_op jit(solution)/shard_map/ppermute | solution.py:572
  26.1 1.3 %collective-permute-start.3 = (f32[2,2,24,128]{3,2,1,0:T(8,128)S(1)}, f32[2,2,24,128]{3,2,1,0:T(8,128)S(1)}, u32[]{:S(2)}, u32[]{:S(2)}) collective-permute-start(f32[2,2,24,128]{3,2,1,0:T(8,128)S(1)} %get-tuple-element.26.state_ref), channel_id=1, source_target_pairs={{0,128},{1,129},{2,130},{3,131},{4,132},{5,133},{6,134},{7,135},{8... | collective-permute-start | bytes 147464 | tf_op jit(solution)/shard_map/ppermute | solution.py:565
  27.4 7.2 %collective-permute-done.arrived_ref = bf16[512,128]{1,0:T(8,128)(2,1)S(1)} collective-permute-done((bf16[512,128]{1,0:T(8,128)(2,1)S(1)}, bf16[512,128]{1,0:T(8,128)(2,1)S(1)}, u32[]{:S(2)}, u32[]{:S(2)}) %collective-permute-start) | collective-permute-done | bytes 131104 | tf_op jit(solution)/shard_map/ppermute | solution.py:572
  34.7 1.7 %shard_map.132 = (f32[2048,128]{1,0:T(8,128)}, bf16[2048,128]{1,0:T(8,128)(2,1)S(1)}) custom-call(s32[1]{0:T(128)S(6)} %copy.25.count_ref, s32[1,512]{1,0:T(1,128)S(1)} %bitcast.21, bf16[512,128]{1,0:T(8,128)(2,1)S(1)} %collective-permute-done.arrived_ref, f32[2048,128]{1,0:T(8,128)S(1)} %bitcast.16, f32[2048,128]{1,0:T(8,128)S(1)} %get-tuple-element.16.new_ref, ...), custom_call_target="tpu_custom_call" | custom-call | tf_op jit(solution)/shard_map/pallas_call | solution.py:308
  36.4 5.5 %all-to-all-done.packed_ref = bf16[128,16,128]{2,1,0:T(8,128)(2,1)S(1)} async-done(((bf16[128,16,128]{2,1,0:T(8,128)(2,1)}), bf16[128,16,128]{2,1,0:T(8,128)(2,1)S(1)}, u32[]{:S(2)}, u32[]{:S(2)}) %all-to-all-start) | async-done | bytes 524320 | tf_op jit(solution)/shard_map/all_to_all | solution.py:541
  42.0 1.5 %collective-permute-start.2 = (f32[2,16,128]{2,1,0:T(8,128)S(1)}, f32[2,16,128]{2,1,0:T(8,128)S(1)}, u32[]{:S(2)}, u32[]{:S(2)}) collective-permute-start(f32[2,16,128]{2,1,0:T(8,128)S(1)} %get-tuple-element.25.sum_ref), channel_id=1, source_target_pairs={{0,128},{1,129},{2,130},{3,131},{4,132},{5,133},{6,134},{7,135},{8... | collective-permute-start | bytes 49160 | tf_op jit(solution)/shard_map/ppermute | solution.py:528
  43.5 3.8 %shard_map.137.answer_ref.value_ref = bf16[4096,128]{1,0:T(8,128)(2,1)} custom-call(f32[128,128]{1,0:T(8,128)S(1)} %get-tuple-element.24.asked_ref, bf16[2048,128]{1,0:T(8,128)(2,1)S(1)} %get-tuple-element.23.lookup_ref.table_ref), custom_call_target="tpu_custom_call" | custom-call | tf_op jit(solution)/shard_map/pallas_call | solution.py:401
  48.3 2.4 %collective-permute-start.4 = (bf16[48,128]{1,0:T(8,128)(2,1)S(1)}, bf16[48,128]{1,0:T(8,128)(2,1)S(1)}, u32[]{:S(2)}, u32[]{:S(2)}) collective-permute-start(bf16[48,128]{1,0:T(8,128)(2,1)S(1)} %shard_map.138), channel_id=1, source_target_pairs={{16,0},{17,1},{18,2},{19,3},{20,4},{21,5},{22,6},{23,7},{24,8},{25... | collective-permute-start | bytes 36872 | tf_op jit(solution)/shard_map/ppermute | solution.py:533
  50.8 1.4 %collective-permute-done.4 = bf16[48,128]{1,0:T(8,128)(2,1)S(1)} collective-permute-done((bf16[48,128]{1,0:T(8,128)(2,1)S(1)}, bf16[48,128]{1,0:T(8,128)(2,1)S(1)}, u32[]{:S(2)}, u32[]{:S(2)}) %collective-permute-start.4) | collective-permute-done | bytes 12320 | tf_op jit(solution)/shard_map/ppermute | solution.py:533
  52.8 4.4 %collective-permute-start.6 = (bf16[144,128]{1,0:T(8,128)(2,1)S(1)}, bf16[144,128]{1,0:T(8,128)(2,1)S(1)}, u32[]{:S(2)}, u32[]{:S(2)}) collective-permute-start(bf16[144,128]{1,0:T(8,128)(2,1)S(1)} %pad_maximum_fusion), channel_id=1, source_target_pairs={{48,0},{49,1},{50,2},{51,3},{52,4},{53,5},{54,6},{55,7},{56,8},{57... | collective-permute-start | bytes 110600 | tf_op jit(solution)/shard_map/ppermute | solution.py:533
  57.2 1.6 %collective-permute-done.6 = bf16[144,128]{1,0:T(8,128)(2,1)S(1)} collective-permute-done((bf16[144,128]{1,0:T(8,128)(2,1)S(1)}, bf16[144,128]{1,0:T(8,128)(2,1)S(1)}, u32[]{:S(2)}, u32[]{:S(2)}) %collective-permute-start.6) | collective-permute-done | bytes 36896 | tf_op jit(solution)/shard_map/ppermute | solution.py:533
  59.0 9.8 %all-to-all-start.1 = ((bf16[128,32,128]{2,1,0:T(8,128)(2,1)}), bf16[128,32,128]{2,1,0:T(8,128)(2,1)S(1)}, u32[]{:S(2)}, u32[]{:S(2)}) async-start(bf16[128,32,128]{2,1,0:T(8,128)(2,1)} %bitcast.10), calls=%async_computation.1 | async-start | bytes 2097152 | tf_op jit(solution)/shard_map/all_to_all | solution.py:541
  68.8 2.7 %collective-permute-start.8 = (bf16[384,128]{1,0:T(8,128)(2,1)S(1)}, bf16[384,128]{1,0:T(8,128)(2,1)S(1)}, u32[]{:S(2)}, u32[]{:S(2)}) collective-permute-start(bf16[384,128]{1,0:T(8,128)(2,1)S(1)} %get-tuple-element.31.other_ref), channel_id=1, source_target_pairs={{0,2},{1,3},{2,0},{3,1},{4,6},{5,7},{6,4},{7,5},{8,10},{9,11},{10,... | collective-permute-start | bytes 294920 | tf_op jit(solution)/shard_map/ppermute | solution.py:528
  71.6 4.9 %collective-permute-done.8 = bf16[384,128]{1,0:T(8,128)(2,1)S(1)} collective-permute-done((bf16[384,128]{1,0:T(8,128)(2,1)S(1)}, bf16[384,128]{1,0:T(8,128)(2,1)S(1)}, u32[]{:S(2)}, u32[]{:S(2)}) %collective-permute-start.8) | collective-permute-done | bytes 98336 | tf_op jit(solution)/shard_map/ppermute | solution.py:528
  76.4 3.3 %collective-permute-start.11 = (bf16[768,128]{1,0:T(8,128)(2,1)S(1)}, bf16[768,128]{1,0:T(8,128)(2,1)S(1)}, u32[]{:S(2)}, u32[]{:S(2)}) collective-permute-start(bf16[768,128]{1,0:T(8,128)(2,1)S(1)} %constant_dynamic-update-slice_fusion.5.refs_0_), channel_id=1, source_target_pairs={{0,12},{1,13},{2,14},{3,15},{4,8},{5,9},{6,10},{7,11},{8,4},{9,5},... | collective-permute-start | bytes 589832 | tf_op jit(solution)/shard_map/ppermute | solution.py:528
  80.7 14.6 %collective-permute-done.11.refs_3_ = bf16[768,128]{1,0:T(8,128)(2,1)S(1)} collective-permute-done((bf16[768,128]{1,0:T(8,128)(2,1)S(1)}, bf16[768,128]{1,0:T(8,128)(2,1)S(1)}, u32[]{:S(2)}, u32[]{:S(2)}) %collective-permute-start.11) | collective-permute-done | bytes 196640 | tf_op jit(solution)/shard_map/ppermute | solution.py:528
  95.3 1.3 %collective-permute-done.9.refs_1_ = bf16[768,128]{1,0:T(8,128)(2,1)S(1)} collective-permute-done((bf16[768,128]{1,0:T(8,128)(2,1)S(1)}, bf16[768,128]{1,0:T(8,128)(2,1)S(1)}, u32[]{:S(2)}, u32[]{:S(2)}) %collective-permute-start.9) | collective-permute-done | bytes 196640 | tf_op jit(solution)/shard_map/ppermute | solution.py:528
  96.9 3.7 %all-to-all-done.1 = bf16[128,32,128]{2,1,0:T(8,128)(2,1)S(1)} async-done(((bf16[128,32,128]{2,1,0:T(8,128)(2,1)}), bf16[128,32,128]{2,1,0:T(8,128)(2,1)S(1)}, u32[]{:S(2)}, u32[]{:S(2)}) %all-to-all-start.1) | async-done | bytes 1048608 | tf_op jit(solution)/shard_map/all_to_all | solution.py:541
  100.6 2.6 %shard_map.140.base_ref = bf16[512,512]{1,0:T(8,128)(2,1)S(1)} custom-call(s32[8,512]{1,0:T(8,128)S(1)} %get-tuple-element.19.place_ref, bf16[4096,128]{1,0:T(8,128)(2,1)S(1)} %bitcast.17), custom_call_target="tpu_custom_call" | custom-call | flops 2147483648 | bytes 2000000 | tf_op jit(solution)/shard_map/pallas_call | solution.py:474
  103.2 2.2 %shard_map.142 = f32[1,512]{1,0:T(1,128)} custom-call(bf16[512,512]{1,0:T(8,128)(2,1)S(1)} %shard_map.140.base_ref, f32[3,512]{1,0:T(4,128)S(1)} %copy-done.6, f32[1,512]{1,0:T(1,128)S(1)} %bitcast.22, bf16[2,1536,128]{2,1,0:T(8,128)(2,1)S(1)} %shard_map.141.own_ref, bf16[2,1536,128]{2,1,0:T(8,128)(2,1)S(1)} %collective-permute-done.12.other_ref), custom_call_target="tpu_custom_call" | custom-call | flops 805306368 | bytes 3000000 | tf_op jit(solution)/shard_map/pallas_call | solution.py:511
  (42 shorter events, 5.1 us)
Async XLA Ops:
  0.6 1.7 %copy-start.3 = (s32[1,512,4]{1,2,0:T(4,128)S(1)}, s32[1,512,4]{1,2,0:T(4,128)}, u32[]{:S(2)}) copy-start(s32[1,512,4]{1,2,0:T(4,128)} %param.22) | copy-start | bytes 24580
  0.6 1.7 %copy-start.4 = (s32[1,512,4]{1,2,0:T(4,128)S(1)}, s32[1,512,4]{1,2,0:T(4,128)}, u32[]{:S(2)}) copy-start(s32[1,512,4]{1,2,0:T(4,128)} %param.23) | copy-start | bytes 24580
  2.1 18.9 %copy-start = (f32[1,2048,128]{2,1,0:T(8,128)S(1)}, f32[1,2048,128]{2,1,0:T(8,128)}, u32[]{:S(2)}) copy-start(f32[1,2048,128]{2,1,0:T(8,128)} %param.12) | copy-start | bytes 3145732
  2.1 18.9 %copy-start.1 = (f32[2048,128]{1,0:T(8,128)S(1)}, f32[2048,128]{1,0:T(8,128)}, u32[]{:S(2)}) copy-start(f32[2048,128]{1,0:T(8,128)} %square_ref.1) | copy-start | bytes 3145732
  2.2 18.9 %copy-start.2 = (f32[512,128]{1,0:T(8,128)S(1)}, f32[512,128]{1,0:T(8,128)}, u32[]{:S(2)}) copy-start(f32[512,128]{1,0:T(8,128)} %grad_ref.1) | copy-start | bytes 786436
  2.2 18.9 %copy-start.5 = (s32[512]{0:T(512)S(1)}, s32[512]{0:T(512)}, u32[]{:S(2)}) copy-start(s32[512]{0:T(512)} %param.14) | copy-start | bytes 6148
  2.2 2.4 %collective-permute-start.1 = (f32[2,32,24,128]{3,2,1,0:T(8,128)S(1)}, f32[2,32,24,128]{3,2,1,0:T(8,128)S(1)}, u32[]{:S(2)}, u32[]{:S(2)}) collective-permute-start(f32[2,32,24,128]{3,2,1,0:T(8,128)S(1)} %get-tuple-element.21), channel_id=1, source_target_pairs={{0,1},{1,0},{2,3},{3,2},{4,5},{5,4},{6,7},{7,6},{8,9},{9,8},{10,11... | collective-permute-start | bytes 2359304 | tf_op jit(solution)/shard_map/ppermute | solution.py:528
  5.5 36.4 %all-to-all-start = ((bf16[128,16,128]{2,1,0:T(8,128)(2,1)}), bf16[128,16,128]{2,1,0:T(8,128)(2,1)S(1)}, u32[]{:S(2)}, u32[]{:S(2)}) async-start(bf16[128,16,128]{2,1,0:T(8,128)(2,1)} %shard_map.135), calls=%async_computation | async-start | bytes 1048576 | tf_op jit(solution)/shard_map/all_to_all | solution.py:541
  24.8 9.8 %collective-permute-start = (bf16[512,128]{1,0:T(8,128)(2,1)S(1)}, bf16[512,128]{1,0:T(8,128)(2,1)S(1)}, u32[]{:S(2)}, u32[]{:S(2)}) collective-permute-start(bf16[512,128]{1,0:T(8,128)(2,1)S(1)} %get-tuple-element.15), channel_id=1, source_target_pairs={{0,128},{1,129},{2,130},{3,131},{4,132},{5,133},{6,134},{7,135},{8... | collective-permute-start | bytes 393224 | tf_op jit(solution)/shard_map/ppermute | solution.py:572
  26.1 21.2 %collective-permute-start.3 = (f32[2,2,24,128]{3,2,1,0:T(8,128)S(1)}, f32[2,2,24,128]{3,2,1,0:T(8,128)S(1)}, u32[]{:S(2)}, u32[]{:S(2)}) collective-permute-start(f32[2,2,24,128]{3,2,1,0:T(8,128)S(1)} %get-tuple-element.26.state_ref), channel_id=1, source_target_pairs={{0,128},{1,129},{2,130},{3,131},{4,132},{5,133},{6,134},{7,135},{8... | collective-permute-start | bytes 147464 | tf_op jit(solution)/shard_map/ppermute | solution.py:565
  42.0 5.4 %collective-permute-start.2 = (f32[2,16,128]{2,1,0:T(8,128)S(1)}, f32[2,16,128]{2,1,0:T(8,128)S(1)}, u32[]{:S(2)}, u32[]{:S(2)}) collective-permute-start(f32[2,16,128]{2,1,0:T(8,128)S(1)} %get-tuple-element.25.sum_ref), channel_id=1, source_target_pairs={{0,128},{1,129},{2,130},{3,131},{4,132},{5,133},{6,134},{7,135},{8... | collective-permute-start | bytes 49160 | tf_op jit(solution)/shard_map/ppermute | solution.py:528
  47.4 5.4 %collective-permute-start.5 = (bf16[48,128]{1,0:T(8,128)(2,1)S(1)}, bf16[48,128]{1,0:T(8,128)(2,1)S(1)}, u32[]{:S(2)}, u32[]{:S(2)}) collective-permute-start(bf16[48,128]{1,0:T(8,128)(2,1)S(1)} %shard_map.138), channel_id=1, source_target_pairs={{112,0},{113,1},{114,2},{115,3},{116,4},{117,5},{118,6},{119,7},{1... | collective-permute-start | bytes 36872 | tf_op jit(solution)/shard_map/ppermute | solution.py:533
  48.3 3.8 %collective-permute-start.4 = (bf16[48,128]{1,0:T(8,128)(2,1)S(1)}, bf16[48,128]{1,0:T(8,128)(2,1)S(1)}, u32[]{:S(2)}, u32[]{:S(2)}) collective-permute-start(bf16[48,128]{1,0:T(8,128)(2,1)S(1)} %shard_map.138), channel_id=1, source_target_pairs={{16,0},{17,1},{18,2},{19,3},{20,4},{21,5},{22,6},{23,7},{24,8},{25... | collective-permute-start | bytes 36872 | tf_op jit(solution)/shard_map/ppermute | solution.py:533
  52.2 6.8 %collective-permute-start.7 = (bf16[96,128]{1,0:T(8,128)(2,1)S(1)}, bf16[96,128]{1,0:T(8,128)(2,1)S(1)}, u32[]{:S(2)}, u32[]{:S(2)}) collective-permute-start(bf16[96,128]{1,0:T(8,128)(2,1)S(1)} %pad_maximum_fusion.1), channel_id=1, source_target_pairs={{80,0},{81,1},{82,2},{83,3},{84,4},{85,5},{86,6},{87,7},{88,8},{89... | collective-permute-start | bytes 73736 | tf_op jit(solution)/shard_map/ppermute | solution.py:533
  52.8 6.0 %collective-permute-start.6 = (bf16[144,128]{1,0:T(8,128)(2,1)S(1)}, bf16[144,128]{1,0:T(8,128)(2,1)S(1)}, u32[]{:S(2)}, u32[]{:S(2)}) collective-permute-start(bf16[144,128]{1,0:T(8,128)(2,1)S(1)} %pad_maximum_fusion), channel_id=1, source_target_pairs={{48,0},{49,1},{50,2},{51,3},{52,4},{53,5},{54,6},{55,7},{56,8},{57... | collective-permute-start | bytes 110600 | tf_op jit(solution)/shard_map/ppermute | solution.py:533
  59.0 41.6 %all-to-all-start.1 = ((bf16[128,32,128]{2,1,0:T(8,128)(2,1)}), bf16[128,32,128]{2,1,0:T(8,128)(2,1)S(1)}, u32[]{:S(2)}, u32[]{:S(2)}) async-start(bf16[128,32,128]{2,1,0:T(8,128)(2,1)} %bitcast.10), calls=%async_computation.1 | async-start | bytes 2097152 | tf_op jit(solution)/shard_map/all_to_all | solution.py:541
  68.8 7.6 %collective-permute-start.8 = (bf16[384,128]{1,0:T(8,128)(2,1)S(1)}, bf16[384,128]{1,0:T(8,128)(2,1)S(1)}, u32[]{:S(2)}, u32[]{:S(2)}) collective-permute-start(bf16[384,128]{1,0:T(8,128)(2,1)S(1)} %get-tuple-element.31.other_ref), channel_id=1, source_target_pairs={{0,2},{1,3},{2,0},{3,1},{4,6},{5,7},{6,4},{7,5},{8,10},{9,11},{10,... | collective-permute-start | bytes 294920 | tf_op jit(solution)/shard_map/ppermute | solution.py:528
  76.4 18.9 %collective-permute-start.11 = (bf16[768,128]{1,0:T(8,128)(2,1)S(1)}, bf16[768,128]{1,0:T(8,128)(2,1)S(1)}, u32[]{:S(2)}, u32[]{:S(2)}) collective-permute-start(bf16[768,128]{1,0:T(8,128)(2,1)S(1)} %constant_dynamic-update-slice_fusion.5.refs_0_), channel_id=1, source_target_pairs={{0,12},{1,13},{2,14},{3,15},{4,8},{5,9},{6,10},{7,11},{8,4},{9,5},... | collective-permute-start | bytes 589832 | tf_op jit(solution)/shard_map/ppermute | solution.py:528
  79.7 15.6 %collective-permute-start.10 = (bf16[768,128]{1,0:T(8,128)(2,1)S(1)}, bf16[768,128]{1,0:T(8,128)(2,1)S(1)}, u32[]{:S(2)}, u32[]{:S(2)}) collective-permute-start(bf16[768,128]{1,0:T(8,128)(2,1)S(1)} %constant_dynamic-update-slice_fusion.5.refs_0_), channel_id=1, source_target_pairs={{0,8},{1,9},{2,10},{3,11},{4,12},{5,13},{6,14},{7,15},{8,0},{9,1},... | collective-permute-start | bytes 589832 | tf_op jit(solution)/shard_map/ppermute | solution.py:528
  80.3 16.3 %collective-permute-start.9 = (bf16[768,128]{1,0:T(8,128)(2,1)S(1)}, bf16[768,128]{1,0:T(8,128)(2,1)S(1)}, u32[]{:S(2)}, u32[]{:S(2)}) collective-permute-start(bf16[768,128]{1,0:T(8,128)(2,1)S(1)} %constant_dynamic-update-slice_fusion.5.refs_0_), channel_id=1, source_target_pairs={{0,4},{1,5},{2,6},{3,7},{4,0},{5,1},{6,2},{7,3},{8,12},{9,13},{10,... | collective-permute-start | bytes 589832 | tf_op jit(solution)/shard_map/ppermute | solution.py:528
  96.8 6.4 %collective-permute-start.12 = (bf16[2,1536,128]{2,1,0:T(8,128)(2,1)S(1)}, bf16[2,1536,128]{2,1,0:T(8,128)(2,1)S(1)}, u32[]{:S(2)}, u32[]{:S(2)}) collective-permute-start(bf16[2,1536,128]{2,1,0:T(8,128)(2,1)S(1)} %shard_map.141.own_ref), channel_id=1, source_target_pairs={{0,1},{1,0},{2,3},{3,2},{4,5},{5,4},{6,7},{7,6},{8,9},{9,8},{10,11... | collective-permute-start | bytes 2359304 | tf_op jit(solution)/shard_map/ppermute | solution.py:528
  100.6 2.6 %copy-start.6 = (f32[3,512]{1,0:T(4,128)S(1)}, f32[3,512]{1,0:T(4,128)}, u32[]{:S(2)}) copy-start(f32[3,512]{1,0:T(4,128)} %bias_ref.1) | copy-start | bytes 18436
  100.6 2.6 %copy-start.7 = (f32[512]{0:T(512)S(1)}, f32[512]{0:T(512)}, u32[]{:S(2)}) copy-start(f32[512]{0:T(512)} %param.21) | copy-start | bytes 6148

commit v5 on v4

--- a/solution.py
+++ b/solution.py
@@ -13,7 +13,7 @@
 ROLES = 2
 Z_SIZE, Y_SIZE, X_SIZE, CORES = 8, 4, 2, 2
 BLOCKS = Z_SIZE * Y_SIZE
-Z_ORDER = (0, 1, 7, 3, 4, 2, 5, 6)
+Z_ORDER = (0, 1, 7, 3, 4, 2, 6, 5)
 TILES = 2
 SHARE = 12
 PACKED = 16
@@ -346,7 +346,7 @@
     target_ref[:, LANES:] = source_ref[height:, :]
 
 
-def piece_body(sum_ref, other_ref, state_ref, trained_ref, square_ref, answer_ref, piece_ref):
+def piece_body(sum_ref, other_ref, state_ref, trained_ref, square_ref, piece_ref):
     role, shard, _ = position()
     later = lax.rem(shard // CORES, X_SIZE) == 1
 
@@ -368,16 +368,16 @@
     piece_ref[...] = jnp.concatenate(parts, axis=0).astype(jnp.bfloat16)
 
 
-def piece_weights(sums, other, state, trained, squares, answers):
+def piece_weights(sums, other, state, trained, squares):
     return kernel_call(
         piece_body,
         jax.ShapeDtypeStruct((ROLES * CORES * SHARE, LANES), jnp.bfloat16),
-        in_specs=[VMEM] * 5 + [ANY],
+        in_specs=[VMEM] * 5,
         out_specs=VMEM,
-    )(sums, other, state, trained, squares, answers)
-
-
-def answer_body(asked_ref, table_ref, answer_ref, columns, folded):
+    )(sums, other, state, trained, squares)
+
+
+def answer_body(asked_ref, table_ref, late_ref, answer_ref, columns, folded):
     digits = asked_ref[...]
     wide = jnp.concatenate(
         [
@@ -396,18 +396,18 @@
         answer_ref[at * CAP : (at + group) * CAP, :] = looked_up(asked, folded[...])
 
 
-def answer_rows(asked, table):
+def answer_rows(asked, table, late):
     rows, width = table.shape
     return kernel_call(
         answer_body,
         jax.ShapeDtypeStruct((SHARDS * CAP, width), jnp.bfloat16),
-        in_specs=[VMEM] * 2,
+        in_specs=[VMEM] * 2 + [ANY],
         out_specs=VMEM,
         scratch_shapes=[
             pltpu.VMEM((CAP, SHARDS), jnp.int32),
             pltpu.VMEM((rows // 2, 2 * width), jnp.bfloat16),
         ],
-    )(asked, table)
+    )(asked, table, late)
 
 
 def after_body(value_ref, other_ref, out_ref):
@@ -443,14 +443,16 @@
                 for half in range(ROLES):
                     start = (half * CORES + column) * SHARE
                     parts += [values[start : start + SHARE, :] for values in (first, second)]
-                tile_ref[column, rows, :] = jnp.concatenate(parts, axis=0).astype(jnp.bfloat16)
+                tile_ref[rows, column * LANES : (column + 1) * LANES] = jnp.concatenate(
+                    parts, axis=0
+                ).astype(jnp.bfloat16)
 
 
 def collect(pieces):
     rows = BLOCKS * ROLES * X_SIZE * SHARE
     return kernel_call(
         collect_body,
-        jax.ShapeDtypeStruct((CORES, rows, LANES), jnp.bfloat16),
+        jax.ShapeDtypeStruct((rows, CORES * LANES), jnp.bfloat16),
         in_specs=[VMEM] * Y_SIZE,
         out_specs=VMEM,
     )(*pieces)
@@ -485,20 +487,26 @@
     )(places, answers)
 
 
-def cross_body(base_ref, bias_ref, out_ref, own_ref, other_ref, score_ref, weights):
+def cross_body(base_ref, bias_ref, out_ref, own_ref, other_ref, score_ref):
     _, _, core = position()
-    for column in range(CORES):
-        for flip, tile_ref in ((0, own_ref), (1, other_ref)):
-            left = pl.multiple_of((column * TILES + (core ^ flip)) * LANES, LANES)
-            weights[:, pl.ds(left, LANES)] = tile_ref[column]
     width = base_ref.shape[1]
     base = base_ref[...].astype(jnp.float32)
     crossed = base
     for layer in range(bias_ref.shape[0]):
-        mixed = jnp.dot(
-            crossed.astype(jnp.bfloat16),
-            weights[layer * width : (layer + 1) * width, :],
-            preferred_element_type=jnp.float32,
+        rows = slice(layer * width, (layer + 1) * width)
+        inputs = crossed.astype(jnp.bfloat16)
+        own, other = (
+            jnp.dot(inputs, tile_ref[rows, :], preferred_element_type=jnp.float32)
+            for tile_ref in (own_ref, other_ref)
+        )
+        even, odd = jnp.where(core == 0, own, other), jnp.where(core == 0, other, own)
+        mixed = jnp.concatenate(
+            [
+                tiles[:, column * LANES : (column + 1) * LANES]
+                for column in range(CORES)
+                for tiles in (even, odd)
+            ],
+            axis=1,
         )
         crossed = base * (mixed + bias_ref[layer : layer + 1, :]) + crossed
     scores = jnp.sum(crossed * out_ref[...], axis=1, keepdims=True)
@@ -507,15 +515,13 @@
 
 def cross_scores(base, bias, out_weight, own, other):
     examples, width = base.shape
-    layers = bias.shape[0]
     return kernel_call(
         cross_body,
         jax.ShapeDtypeStruct((1, examples), jnp.float32),
-        flops=2 * examples * width * width * layers,
+        flops=2 * examples * width * width * bias.shape[0],
         bytes_accessed=3_000_000,
         in_specs=[VMEM] * 5,
         out_specs=VMEM,
-        scratch_shapes=[pltpu.VMEM((layers * width, width), jnp.bfloat16)],
     )(base, bias, out_weight, own, other)
 
 
@@ -574,16 +580,20 @@
         update_counts, slots, arrived, tables[0], new_linear, weights
     )
     sums, asked = unpack(packed, lookup)
-    answers = answer_rows(asked, lookup)
     piece = piece_weights(
-        sums, swapped(sums, ROLE_BIT), own_state, trained, own_squares, answers
-    )
-    near = [piece, from_ahead(piece, 1), from_ahead(piece, -1)]
-    three = jnp.concatenate(near, axis=0)
+        sums, swapped(sums, ROLE_BIT), own_state, trained, own_squares
+    )
+    ahead, behind = from_ahead(piece, 1), from_ahead(piece, -1)
+    three = jnp.concatenate([piece, ahead, behind], axis=0)
     pieces = jnp.concatenate(
-        [three, from_ahead(three, 3), from_ahead(three[: 2 * piece.shape[0]], -3)], axis=0
-    )
-    answers = after(answers, pieces)
+        [
+            three,
+            from_ahead(three, 3),
+            from_ahead(jnp.concatenate([piece, behind], axis=0), -2),
+        ],
+        axis=0,
+    )
+    answers = after(answer_rows(asked, lookup, three), pieces)
     answered = exchange(answers.reshape(SHARDS, CAP, LANES))
     pieces = jnp.concatenate([pieces, swapped(pieces, X_BIT)], axis=0)
     tiles = collect(

time: 106 us -> 103 us (0.972)
  starting transfers between devices: 44.3 us -> 39.9 us
  waiting for transfers between devices: 41.3 us -> 43.1 us
    ppermute x4, starting transfers between devices: 8.35 us -> 5.27 us  [from_ahead(): lax.ppermute(value, 'shard', [((source + steps * span) % SHARDS, source)...]
    ppermute x7, waiting for transfers between devices: 21.6 us -> 23.9 us  [swapped(): lax.ppermute(value, BOTH, [(source, source ^ bits) for source in range(co...]
    all_to_all x2, starting transfers between devices: 24.7 us -> 23.4 us  [exchange(): lax.all_to_all(value, 'shard', split_axis=0, concat_axis=0, tiled=True)]
where the time goes in v5:
time: 103 us
  waiting for transfers between devices  43.1 us (42%)
  starting transfers between devices  39.9 us (39%)
  Pallas kernels  17.9 us (17%)
  between operations  1.54 us (1%)
    ppermute x7, waiting for transfers between devices, swapped(): lax.ppermute(value, BOTH, [(source, source ^ bits) for source in range(co...  23.9 us
    all_to_all x2, starting transfers between devices, exchange(): lax.all_to_all(value, 'shard', split_axis=0, concat_axis=0, tiled=True)  23.4 us
    all_to_all x2, waiting for transfers between devices, exchange(): lax.all_to_all(value, 'shard', split_axis=0, concat_axis=0, tiled=True)  9.19 us
    ppermute x7, starting transfers between devices, swapped(): lax.ppermute(value, BOTH, [(source, source ^ bits) for source in range(co...  8.67 us
    ppermute x1, waiting for transfers between devices, on_device(): arrived = lax.ppermute(fresh, 'role', [(0, 1)])  7.22 us
    ppermute x4, starting transfers between devices, from_ahead(): lax.ppermute(value, 'shard', [((source + steps * span) % SHARDS, source)...  5.27 us
    pallas_call x1, Pallas kernels, answer_rows(): kernel_call(answer_body, jax.ShapeDtypeStruct((SHARDS * CAP, width), jnp....  3.84 us
    pallas_call x1, Pallas kernels, train_rows(): kernel_call(train_body, (jax.ShapeDtypeStruct((rows, width), jnp.float32)...  3.77 us
  transfers between devices with their start and end apart: 15, of which 10 were waited for; matrix products, arithmetic and copies ran while one was open for 0% of the time, Pallas kernels for 13%

profile of v5, /device:TPU:2, one launch (start us, length us, event | category | flops | bytes accessed | tf_op | source)
XLA Modules:
  0.0 102.6 jit_solution(14062694836804577077)
XLA Ops:
  0.7 1.5 %shard_map.134 = (f32[2,32,24,128]{3,2,1,0:T(8,128)S(1)}, f32[2,32,24,128]{3,2,1,0:T(8,128)S(1)}, f32[2,2,24,128]{3,2,1,0:T(8,128)S(1)}, f32[2,2,24,128]{3,2,1,0:T(8,128)S(1)}) custom-call(f32[32,2,24,512]{3,2,1,0:T(8,128)} %bitcast.23, f32[32,2,24,512]{3,2,1,0:T(8,128)} %bitcast.24, f32[32,2,24,512]{3,2,1,0:T(8,128)} %bitcast.25), custom_call_target="tpu_custom_call" | custom-call | bytes 4000000 | tf_op jit(solution)/shard_map/pallas_call | solution.py:98
  2.3 1.4 %shard_map.133 = (s32[8,512]{1,0:T(8,128)S(1)}, f32[128,128]{1,0:T(8,128)S(1)}) custom-call(s32[4,512]{1,0:T(4,128)S(1)} %bitcast.18, s32[4,512]{1,0:T(4,128)S(1)} %bitcast.19), custom_call_target="tpu_custom_call" | custom-call | tf_op jit(solution)/shard_map/pallas_call | solution.py:149
  5.5 14.9 %all-to-all-start = ((bf16[128,16,128]{2,1,0:T(8,128)(2,1)}), bf16[128,16,128]{2,1,0:T(8,128)(2,1)S(1)}, u32[]{:S(2)}, u32[]{:S(2)}) async-start(bf16[128,16,128]{2,1,0:T(8,128)(2,1)} %shard_map.135), calls=%async_computation | async-start | bytes 1048576 | tf_op jit(solution)/shard_map/all_to_all | solution.py:547
  21.1 3.8 %shard_map.131 = (f32[2048,128]{1,0:T(8,128)S(1)}, bf16[2048,128]{1,0:T(8,128)(2,1)S(1)}, bf16[512,128]{1,0:T(8,128)(2,1)S(1)}) custom-call(s32[1]{0:T(128)S(6)} %copy.25.count_ref, s32[1,512]{1,0:T(1,128)S(1)} %bitcast.20, f32[2048,128]{1,0:T(8,128)S(1)} %bitcast.15, f32[2048,128]{1,0:T(8,128)S(1)} %copy-done.1, f32[512,128]{1,0:T(8,128)S(1)} %copy-done.2), custom_call_target="tpu_custom_call" | custom-call | tf_op jit(solution)/shard_map/pallas_call | solution.py:252
  24.8 1.3 %collective-permute-start = (bf16[512,128]{1,0:T(8,128)(2,1)S(1)}, bf16[512,128]{1,0:T(8,128)(2,1)S(1)}, u32[]{:S(2)}, u32[]{:S(2)}) collective-permute-start(bf16[512,128]{1,0:T(8,128)(2,1)S(1)} %get-tuple-element.15), channel_id=1, source_target_pairs={{0,128},{1,129},{2,130},{3,131},{4,132},{5,133},{6,134},{7,135},{8... | collective-permute-start | bytes 393224 | tf_op jit(solution)/shard_map/ppermute | solution.py:578
  26.1 1.3 %collective-permute-start.3 = (f32[2,2,24,128]{3,2,1,0:T(8,128)S(1)}, f32[2,2,24,128]{3,2,1,0:T(8,128)S(1)}, u32[]{:S(2)}, u32[]{:S(2)}) collective-permute-start(f32[2,2,24,128]{3,2,1,0:T(8,128)S(1)} %get-tuple-element.26.state_ref), channel_id=1, source_target_pairs={{0,128},{1,129},{2,130},{3,131},{4,132},{5,133},{6,134},{7,135},{8... | collective-permute-start | bytes 147464 | tf_op jit(solution)/shard_map/ppermute | solution.py:571
  27.4 7.2 %collective-permute-done.arrived_ref = bf16[512,128]{1,0:T(8,128)(2,1)S(1)} collective-permute-done((bf16[512,128]{1,0:T(8,128)(2,1)S(1)}, bf16[512,128]{1,0:T(8,128)(2,1)S(1)}, u32[]{:S(2)}, u32[]{:S(2)}) %collective-permute-start) | collective-permute-done | bytes 131104 | tf_op jit(solution)/shard_map/ppermute | solution.py:578
  34.7 1.7 %shard_map.132 = (f32[2048,128]{1,0:T(8,128)}, bf16[2048,128]{1,0:T(8,128)(2,1)S(1)}) custom-call(s32[1]{0:T(128)S(6)} %copy.25.count_ref, s32[1,512]{1,0:T(1,128)S(1)} %bitcast.21, bf16[512,128]{1,0:T(8,128)(2,1)S(1)} %collective-permute-done.arrived_ref, f32[2048,128]{1,0:T(8,128)S(1)} %bitcast.16, f32[2048,128]{1,0:T(8,128)S(1)} %get-tuple-element.16.new_ref, ...), custom_call_target="tpu_custom_call" | custom-call | tf_op jit(solution)/shard_map/pallas_call | solution.py:308
  36.4 5.5 %all-to-all-done.packed_ref = bf16[128,16,128]{2,1,0:T(8,128)(2,1)S(1)} async-done(((bf16[128,16,128]{2,1,0:T(8,128)(2,1)}), bf16[128,16,128]{2,1,0:T(8,128)(2,1)S(1)}, u32[]{:S(2)}, u32[]{:S(2)}) %all-to-all-start) | async-done | bytes 524320 | tf_op jit(solution)/shard_map/all_to_all | solution.py:547
  42.0 1.5 %collective-permute-start.2 = (f32[2,16,128]{2,1,0:T(8,128)S(1)}, f32[2,16,128]{2,1,0:T(8,128)S(1)}, u32[]{:S(2)}, u32[]{:S(2)}) collective-permute-start(f32[2,16,128]{2,1,0:T(8,128)S(1)} %get-tuple-element.25.sum_ref), channel_id=1, source_target_pairs={{0,128},{1,129},{2,130},{3,131},{4,132},{5,133},{6,134},{7,135},{8... | collective-permute-start | bytes 49160 | tf_op jit(solution)/shard_map/ppermute | solution.py:534
  43.5 2.3 %collective-permute-done.2.other_ref = f32[2,16,128]{2,1,0:T(8,128)S(1)} collective-permute-done((f32[2,16,128]{2,1,0:T(8,128)S(1)}, f32[2,16,128]{2,1,0:T(8,128)S(1)}, u32[]{:S(2)}, u32[]{:S(2)}) %collective-permute-start.2) | collective-permute-done | bytes 16416 | tf_op jit(solution)/shard_map/ppermute | solution.py:534
  46.8 2.4 %collective-permute-start.4 = (bf16[48,128]{1,0:T(8,128)(2,1)S(1)}, bf16[48,128]{1,0:T(8,128)(2,1)S(1)}, u32[]{:S(2)}, u32[]{:S(2)}) collective-permute-start(bf16[48,128]{1,0:T(8,128)(2,1)S(1)} %shard_map.137), channel_id=1, source_target_pairs={{16,0},{17,1},{18,2},{19,3},{20,4},{21,5},{22,6},{23,7},{24,8},{25... | collective-permute-start | bytes 36872 | tf_op jit(solution)/shard_map/ppermute | solution.py:539
  49.2 1.8 %collective-permute-done.5 = bf16[48,128]{1,0:T(8,128)(2,1)S(1)} collective-permute-done((bf16[48,128]{1,0:T(8,128)(2,1)S(1)}, bf16[48,128]{1,0:T(8,128)(2,1)S(1)}, u32[]{:S(2)}, u32[]{:S(2)}) %collective-permute-start.5) | collective-permute-done | bytes 12320 | tf_op jit(solution)/shard_map/ppermute | solution.py:539
  51.0 2.0 %collective-permute-start.6 = (bf16[144,128]{1,0:T(8,128)(2,1)S(1)}, bf16[144,128]{1,0:T(8,128)(2,1)S(1)}, u32[]{:S(2)}, u32[]{:S(2)}) collective-permute-start(bf16[144,128]{1,0:T(8,128)(2,1)S(1)} %pad_maximum_fusion.late_ref), channel_id=1, source_target_pairs={{48,0},{49,1},{50,2},{51,3},{52,4},{53,5},{54,6},{55,7},{56,8},{57... | collective-permute-start | bytes 110600 | tf_op jit(solution)/shard_map/ppermute | solution.py:539
  53.0 3.8 %shard_map.138.value_ref = bf16[4096,128]{1,0:T(8,128)(2,1)} custom-call(f32[128,128]{1,0:T(8,128)S(1)} %get-tuple-element.24.asked_ref, bf16[2048,128]{1,0:T(8,128)(2,1)S(1)} %get-tuple-element.23.lookup_ref.table_ref, bf16[144,128]{1,0:T(8,128)(2,1)S(1)} %pad_maximum_fusion.late_ref), custom_call_target="tpu_custom_call" | custom-call | tf_op jit(solution)/shard_map/pallas_call | solution.py:401
  57.9 8.5 %all-to-all-start.1 = ((bf16[128,32,128]{2,1,0:T(8,128)(2,1)}), bf16[128,32,128]{2,1,0:T(8,128)(2,1)S(1)}, u32[]{:S(2)}, u32[]{:S(2)}) async-start(bf16[128,32,128]{2,1,0:T(8,128)(2,1)} %bitcast.10), calls=%async_computation.1 | async-start | bytes 2097152 | tf_op jit(solution)/shard_map/all_to_all | solution.py:547
  66.4 2.7 %collective-permute-start.8 = (bf16[384,128]{1,0:T(8,128)(2,1)S(1)}, bf16[384,128]{1,0:T(8,128)(2,1)S(1)}, u32[]{:S(2)}, u32[]{:S(2)}) collective-permute-start(bf16[384,128]{1,0:T(8,128)(2,1)S(1)} %get-tuple-element.31.other_ref), channel_id=1, source_target_pairs={{0,2},{1,3},{2,0},{3,1},{4,6},{5,7},{6,4},{7,5},{8,10},{9,11},{10,... | collective-permute-start | bytes 294920 | tf_op jit(solution)/shard_map/ppermute | solution.py:534
  69.1 4.9 %collective-permute-done.8 = bf16[384,128]{1,0:T(8,128)(2,1)S(1)} collective-permute-done((bf16[384,128]{1,0:T(8,128)(2,1)S(1)}, bf16[384,128]{1,0:T(8,128)(2,1)S(1)}, u32[]{:S(2)}, u32[]{:S(2)}) %collective-permute-start.8) | collective-permute-done | bytes 98336 | tf_op jit(solution)/shard_map/ppermute | solution.py:534
  74.0 3.3 %collective-permute-start.11 = (bf16[768,128]{1,0:T(8,128)(2,1)S(1)}, bf16[768,128]{1,0:T(8,128)(2,1)S(1)}, u32[]{:S(2)}, u32[]{:S(2)}) collective-permute-start(bf16[768,128]{1,0:T(8,128)(2,1)S(1)} %constant_dynamic-update-slice_fusion.5.refs_0_), channel_id=1, source_target_pairs={{0,12},{1,13},{2,14},{3,15},{4,8},{5,9},{6,10},{7,11},{8,4},{9,5},... | collective-permute-start | bytes 589832 | tf_op jit(solution)/shard_map/ppermute | solution.py:534
  78.2 14.6 %collective-permute-done.11.refs_3_ = bf16[768,128]{1,0:T(8,128)(2,1)S(1)} collective-permute-done((bf16[768,128]{1,0:T(8,128)(2,1)S(1)}, bf16[768,128]{1,0:T(8,128)(2,1)S(1)}, u32[]{:S(2)}, u32[]{:S(2)}) %collective-permute-start.11) | collective-permute-done | bytes 196640 | tf_op jit(solution)/shard_map/ppermute | solution.py:534
  92.8 1.3 %collective-permute-done.9.refs_1_ = bf16[768,128]{1,0:T(8,128)(2,1)S(1)} collective-permute-done((bf16[768,128]{1,0:T(8,128)(2,1)S(1)}, bf16[768,128]{1,0:T(8,128)(2,1)S(1)}, u32[]{:S(2)}, u32[]{:S(2)}) %collective-permute-start.9) | collective-permute-done | bytes 196640 | tf_op jit(solution)/shard_map/ppermute | solution.py:534
  94.5 3.6 %all-to-all-done.1 = bf16[128,32,128]{2,1,0:T(8,128)(2,1)S(1)} async-done(((bf16[128,32,128]{2,1,0:T(8,128)(2,1)}), bf16[128,32,128]{2,1,0:T(8,128)(2,1)S(1)}, u32[]{:S(2)}, u32[]{:S(2)}) %all-to-all-start.1) | async-done | bytes 1048608 | tf_op jit(solution)/shard_map/all_to_all | solution.py:547
  98.1 2.6 %shard_map.140.base_ref = bf16[512,512]{1,0:T(8,128)(2,1)S(1)} custom-call(s32[8,512]{1,0:T(8,128)S(1)} %get-tuple-element.19.place_ref, bf16[4096,128]{1,0:T(8,128)(2,1)S(1)} %bitcast.17), custom_call_target="tpu_custom_call" | custom-call | flops 2147483648 | bytes 2000000 | tf_op jit(solution)/shard_map/pallas_call | solution.py:476
  100.8 1.8 %shard_map.142 = f32[1,512]{1,0:T(1,128)} custom-call(bf16[512,512]{1,0:T(8,128)(2,1)S(1)} %shard_map.140.base_ref, f32[3,512]{1,0:T(4,128)S(1)} %copy-done.6, f32[1,512]{1,0:T(1,128)S(1)} %bitcast.22, bf16[1536,256]{1,0:T(8,128)(2,1)S(1)} %shard_map.141.own_ref, bf16[1536,256]{1,0:T(8,128)(2,1)S(1)} %collective-permute-done.12.other_ref), custom_call_target="tpu_custom_call" | custom-call | flops 805306368 | bytes 3000000 | tf_op jit(solution)/shard_map/pallas_call | solution.py:518
  (42 shorter events, 5.4 us)
Async XLA Ops:
  0.6 1.7 %copy-start.3 = (s32[1,512,4]{1,2,0:T(4,128)S(1)}, s32[1,512,4]{1,2,0:T(4,128)}, u32[]{:S(2)}) copy-start(s32[1,512,4]{1,2,0:T(4,128)} %param.22) | copy-start | bytes 24580
  0.6 1.7 %copy-start.4 = (s32[1,512,4]{1,2,0:T(4,128)S(1)}, s32[1,512,4]{1,2,0:T(4,128)}, u32[]{:S(2)}) copy-start(s32[1,512,4]{1,2,0:T(4,128)} %param.23) | copy-start | bytes 24580
  2.1 18.9 %copy-start = (f32[1,2048,128]{2,1,0:T(8,128)S(1)}, f32[1,2048,128]{2,1,0:T(8,128)}, u32[]{:S(2)}) copy-start(f32[1,2048,128]{2,1,0:T(8,128)} %param.12) | copy-start | bytes 3145732
  2.1 18.9 %copy-start.1 = (f32[2048,128]{1,0:T(8,128)S(1)}, f32[2048,128]{1,0:T(8,128)}, u32[]{:S(2)}) copy-start(f32[2048,128]{1,0:T(8,128)} %square_ref.1) | copy-start | bytes 3145732
  2.2 18.9 %copy-start.2 = (f32[512,128]{1,0:T(8,128)S(1)}, f32[512,128]{1,0:T(8,128)}, u32[]{:S(2)}) copy-start(f32[512,128]{1,0:T(8,128)} %grad_ref.1) | copy-start | bytes 786436
  2.2 18.9 %copy-start.5 = (s32[512]{0:T(512)S(1)}, s32[512]{0:T(512)}, u32[]{:S(2)}) copy-start(s32[512]{0:T(512)} %param.14) | copy-start | bytes 6148
  2.2 2.4 %collective-permute-start.1 = (f32[2,32,24,128]{3,2,1,0:T(8,128)S(1)}, f32[2,32,24,128]{3,2,1,0:T(8,128)S(1)}, u32[]{:S(2)}, u32[]{:S(2)}) collective-permute-start(f32[2,32,24,128]{3,2,1,0:T(8,128)S(1)} %get-tuple-element.21), channel_id=1, source_target_pairs={{0,1},{1,0},{2,3},{3,2},{4,5},{5,4},{6,7},{7,6},{8,9},{9,8},{10,11... | collective-permute-start | bytes 2359304 | tf_op jit(solution)/shard_map/ppermute | solution.py:534
  5.5 36.4 %all-to-all-start = ((bf16[128,16,128]{2,1,0:T(8,128)(2,1)}), bf16[128,16,128]{2,1,0:T(8,128)(2,1)S(1)}, u32[]{:S(2)}, u32[]{:S(2)}) async-start(bf16[128,16,128]{2,1,0:T(8,128)(2,1)} %shard_map.135), calls=%async_computation | async-start | bytes 1048576 | tf_op jit(solution)/shard_map/all_to_all | solution.py:547
  24.8 9.8 %collective-permute-start = (bf16[512,128]{1,0:T(8,128)(2,1)S(1)}, bf16[512,128]{1,0:T(8,128)(2,1)S(1)}, u32[]{:S(2)}, u32[]{:S(2)}) collective-permute-start(bf16[512,128]{1,0:T(8,128)(2,1)S(1)} %get-tuple-element.15), channel_id=1, source_target_pairs={{0,128},{1,129},{2,130},{3,131},{4,132},{5,133},{6,134},{7,135},{8... | collective-permute-start | bytes 393224 | tf_op jit(solution)/shard_map/ppermute | solution.py:578
  26.1 17.4 %collective-permute-start.3 = (f32[2,2,24,128]{3,2,1,0:T(8,128)S(1)}, f32[2,2,24,128]{3,2,1,0:T(8,128)S(1)}, u32[]{:S(2)}, u32[]{:S(2)}) collective-permute-start(f32[2,2,24,128]{3,2,1,0:T(8,128)S(1)} %get-tuple-element.26.state_ref), channel_id=1, source_target_pairs={{0,128},{1,129},{2,130},{3,131},{4,132},{5,133},{6,134},{7,135},{8... | collective-permute-start | bytes 147464 | tf_op jit(solution)/shard_map/ppermute | solution.py:571
  42.0 3.8 %collective-permute-start.2 = (f32[2,16,128]{2,1,0:T(8,128)S(1)}, f32[2,16,128]{2,1,0:T(8,128)S(1)}, u32[]{:S(2)}, u32[]{:S(2)}) collective-permute-start(f32[2,16,128]{2,1,0:T(8,128)S(1)} %get-tuple-element.25.sum_ref), channel_id=1, source_target_pairs={{0,128},{1,129},{2,130},{3,131},{4,132},{5,133},{6,134},{7,135},{8... | collective-permute-start | bytes 49160 | tf_op jit(solution)/shard_map/ppermute | solution.py:534
  45.9 5.1 %collective-permute-start.5 = (bf16[48,128]{1,0:T(8,128)(2,1)S(1)}, bf16[48,128]{1,0:T(8,128)(2,1)S(1)}, u32[]{:S(2)}, u32[]{:S(2)}) collective-permute-start(bf16[48,128]{1,0:T(8,128)(2,1)S(1)} %shard_map.137), channel_id=1, source_target_pairs={{112,0},{113,1},{114,2},{115,3},{116,4},{117,5},{118,6},{119,7},{1... | collective-permute-start | bytes 36872 | tf_op jit(solution)/shard_map/ppermute | solution.py:539
  46.8 4.2 %collective-permute-start.4 = (bf16[48,128]{1,0:T(8,128)(2,1)S(1)}, bf16[48,128]{1,0:T(8,128)(2,1)S(1)}, u32[]{:S(2)}, u32[]{:S(2)}) collective-permute-start(bf16[48,128]{1,0:T(8,128)(2,1)S(1)} %shard_map.137), channel_id=1, source_target_pairs={{16,0},{17,1},{18,2},{19,3},{20,4},{21,5},{22,6},{23,7},{24,8},{25... | collective-permute-start | bytes 36872 | tf_op jit(solution)/shard_map/ppermute | solution.py:539
  51.0 6.8 %collective-permute-start.7 = (bf16[96,128]{1,0:T(8,128)(2,1)S(1)}, bf16[96,128]{1,0:T(8,128)(2,1)S(1)}, u32[]{:S(2)}, u32[]{:S(2)}) collective-permute-start(bf16[96,128]{1,0:T(8,128)(2,1)S(1)} %pad_maximum_fusion.1), channel_id=1, source_target_pairs={{96,0},{97,1},{98,2},{99,3},{100,4},{101,5},{102,6},{103,7},{104,8... | collective-permute-start | bytes 73736 | tf_op jit(solution)/shard_map/ppermute | solution.py:539
  51.0 6.8 %collective-permute-start.6 = (bf16[144,128]{1,0:T(8,128)(2,1)S(1)}, bf16[144,128]{1,0:T(8,128)(2,1)S(1)}, u32[]{:S(2)}, u32[]{:S(2)}) collective-permute-start(bf16[144,128]{1,0:T(8,128)(2,1)S(1)} %pad_maximum_fusion.late_ref), channel_id=1, source_target_pairs={{48,0},{49,1},{50,2},{51,3},{52,4},{53,5},{54,6},{55,7},{56,8},{57... | collective-permute-start | bytes 110600 | tf_op jit(solution)/shard_map/ppermute | solution.py:539
  57.9 40.2 %all-to-all-start.1 = ((bf16[128,32,128]{2,1,0:T(8,128)(2,1)}), bf16[128,32,128]{2,1,0:T(8,128)(2,1)S(1)}, u32[]{:S(2)}, u32[]{:S(2)}) async-start(bf16[128,32,128]{2,1,0:T(8,128)(2,1)} %bitcast.10), calls=%async_computation.1 | async-start | bytes 2097152 | tf_op jit(solution)/shard_map/all_to_all | solution.py:547
  66.4 7.6 %collective-permute-start.8 = (bf16[384,128]{1,0:T(8,128)(2,1)S(1)}, bf16[384,128]{1,0:T(8,128)(2,1)S(1)}, u32[]{:S(2)}, u32[]{:S(2)}) collective-permute-start(bf16[384,128]{1,0:T(8,128)(2,1)S(1)} %get-tuple-element.31.other_ref), channel_id=1, source_target_pairs={{0,2},{1,3},{2,0},{3,1},{4,6},{5,7},{6,4},{7,5},{8,10},{9,11},{10,... | collective-permute-start | bytes 294920 | tf_op jit(solution)/shard_map/ppermute | solution.py:534
  74.0 18.9 %collective-permute-start.11 = (bf16[768,128]{1,0:T(8,128)(2,1)S(1)}, bf16[768,128]{1,0:T(8,128)(2,1)S(1)}, u32[]{:S(2)}, u32[]{:S(2)}) collective-permute-start(bf16[768,128]{1,0:T(8,128)(2,1)S(1)} %constant_dynamic-update-slice_fusion.5.refs_0_), channel_id=1, source_target_pairs={{0,12},{1,13},{2,14},{3,15},{4,8},{5,9},{6,10},{7,11},{8,4},{9,5},... | collective-permute-start | bytes 589832 | tf_op jit(solution)/shard_map/ppermute | solution.py:534
  77.3 15.6 %collective-permute-start.10 = (bf16[768,128]{1,0:T(8,128)(2,1)S(1)}, bf16[768,128]{1,0:T(8,128)(2,1)S(1)}, u32[]{:S(2)}, u32[]{:S(2)}) collective-permute-start(bf16[768,128]{1,0:T(8,128)(2,1)S(1)} %constant_dynamic-update-slice_fusion.5.refs_0_), channel_id=1, source_target_pairs={{0,8},{1,9},{2,10},{3,11},{4,12},{5,13},{6,14},{7,15},{8,0},{9,1},... | collective-permute-start | bytes 589832 | tf_op jit(solution)/shard_map/ppermute | solution.py:534
  77.8 16.3 %collective-permute-start.9 = (bf16[768,128]{1,0:T(8,128)(2,1)S(1)}, bf16[768,128]{1,0:T(8,128)(2,1)S(1)}, u32[]{:S(2)}, u32[]{:S(2)}) collective-permute-start(bf16[768,128]{1,0:T(8,128)(2,1)S(1)} %constant_dynamic-update-slice_fusion.5.refs_0_), channel_id=1, source_target_pairs={{0,4},{1,5},{2,6},{3,7},{4,0},{5,1},{6,2},{7,3},{8,12},{9,13},{10,... | collective-permute-start | bytes 589832 | tf_op jit(solution)/shard_map/ppermute | solution.py:534
  94.4 6.3 %collective-permute-start.12 = (bf16[1536,256]{1,0:T(8,128)(2,1)S(1)}, bf16[1536,256]{1,0:T(8,128)(2,1)S(1)}, u32[]{:S(2)}, u32[]{:S(2)}) collective-permute-start(bf16[1536,256]{1,0:T(8,128)(2,1)S(1)} %shard_map.141.own_ref), channel_id=1, source_target_pairs={{0,1},{1,0},{2,3},{3,2},{4,5},{5,4},{6,7},{7,6},{8,9},{9,8},{10,11... | collective-permute-start | bytes 2359304 | tf_op jit(solution)/shard_map/ppermute | solution.py:534
  98.1 2.6 %copy-start.6 = (f32[3,512]{1,0:T(4,128)S(1)}, f32[3,512]{1,0:T(4,128)}, u32[]{:S(2)}) copy-start(f32[3,512]{1,0:T(4,128)} %bias_ref.1) | copy-start | bytes 18436
  98.1 2.6 %copy-start.7 = (f32[512]{0:T(512)S(1)}, f32[512]{0:T(512)}, u32[]{:S(2)}) copy-start(f32[512]{0:T(512)} %param.21) | copy-start | bytes 6148

commit v6 on v5

--- a/solution.py
+++ b/solution.py
@@ -346,7 +346,7 @@
     target_ref[:, LANES:] = source_ref[height:, :]
 
 
-def piece_body(sum_ref, other_ref, state_ref, trained_ref, square_ref, piece_ref):
+def piece_body(sum_ref, other_ref, state_ref, trained_ref, square_ref, answer_ref, piece_ref):
     role, shard, _ = position()
     later = lax.rem(shard // CORES, X_SIZE) == 1
 
@@ -368,16 +368,16 @@
     piece_ref[...] = jnp.concatenate(parts, axis=0).astype(jnp.bfloat16)
 
 
-def piece_weights(sums, other, state, trained, squares):
+def piece_weights(sums, other, state, trained, squares, answers):
     return kernel_call(
         piece_body,
         jax.ShapeDtypeStruct((ROLES * CORES * SHARE, LANES), jnp.bfloat16),
-        in_specs=[VMEM] * 5,
+        in_specs=[VMEM] * 5 + [ANY],
         out_specs=VMEM,
-    )(sums, other, state, trained, squares)
-
-
-def answer_body(asked_ref, table_ref, late_ref, answer_ref, columns, folded):
+    )(sums, other, state, trained, squares, answers)
+
+
+def answer_body(asked_ref, table_ref, answer_ref, columns, folded):
     digits = asked_ref[...]
     wide = jnp.concatenate(
         [
@@ -396,18 +396,18 @@
         answer_ref[at * CAP : (at + group) * CAP, :] = looked_up(asked, folded[...])
 
 
-def answer_rows(asked, table, late):
+def answer_rows(asked, table):
     rows, width = table.shape
     return kernel_call(
         answer_body,
         jax.ShapeDtypeStruct((SHARDS * CAP, width), jnp.bfloat16),
-        in_specs=[VMEM] * 2 + [ANY],
+        in_specs=[VMEM] * 2,
         out_specs=VMEM,
         scratch_shapes=[
             pltpu.VMEM((CAP, SHARDS), jnp.int32),
             pltpu.VMEM((rows // 2, 2 * width), jnp.bfloat16),
         ],
-    )(asked, table, late)
+    )(asked, table)
 
 
 def after_body(value_ref, other_ref, out_ref):
@@ -453,6 +453,7 @@
     return kernel_call(
         collect_body,
         jax.ShapeDtypeStruct((rows, CORES * LANES), jnp.bfloat16),
+        flops=9_000_000_000,
         in_specs=[VMEM] * Y_SIZE,
         out_specs=VMEM,
     )(*pieces)
@@ -580,8 +581,9 @@
         update_counts, slots, arrived, tables[0], new_linear, weights
     )
     sums, asked = unpack(packed, lookup)
+    answers = answer_rows(asked, lookup)
     piece = piece_weights(
-        sums, swapped(sums, ROLE_BIT), own_state, trained, own_squares
+        sums, swapped(sums, ROLE_BIT), own_state, trained, own_squares, answers
     )
     ahead, behind = from_ahead(piece, 1), from_ahead(piece, -1)
     three = jnp.concatenate([piece, ahead, behind], axis=0)
@@ -593,7 +595,7 @@
         ],
         axis=0,
     )
-    answers = after(answer_rows(asked, lookup, three), pieces)
+    answers = after(answers, three)
     answered = exchange(answers.reshape(SHARDS, CAP, LANES))
     pieces = jnp.concatenate([pieces, swapped(pieces, X_BIT)], axis=0)
     tiles = collect(

time: 103 us -> 103 us (level); the launches traced: 103 us -> 101 us
  waiting for transfers between devices: 43.1 us -> 39.9 us
  starting transfers between devices: 39.9 us -> 41.7 us
    ppermute x4, starting transfers between devices: 5.27 us -> 9.2 us  [from_ahead(): lax.ppermute(value, 'shard', [((source + steps * span) % SHARDS, source)...]
    ppermute x7, waiting for transfers between devices: 23.9 us -> 21.5 us  [swapped(): lax.ppermute(value, BOTH, [(source, source ^ bits) for source in range(co...]
    all_to_all x2, starting transfers between devices: 23.4 us -> 21.3 us  [exchange(): lax.all_to_all(value, 'shard', split_axis=0, concat_axis=0, tiled=True)]
    ppermute x4, waiting for transfers between devices: 2.78 us -> 1.67 us  [from_ahead(): lax.ppermute(value, 'shard', [((source + steps * span) % SHARDS, source)...]
  transfers between devices with their start and end apart: 15 -> 15, of which waited for: 10 -> 8; matrix products, arithmetic and copies ran while one was open for 0% -> 0% of each run, Pallas kernels for 13% -> 13%
where the time goes in v6:
time: 103 us; the launch traced here: 101 us
  starting transfers between devices  41.7 us (40%)
  waiting for transfers between devices  39.9 us (39%)
  Pallas kernels  17.9 us (17%)
  between operations  1.55 us (2%)
    ppermute x7, waiting for transfers between devices, swapped(): lax.ppermute(value, BOTH, [(source, source ^ bits) for source in range(co...  21.5 us
    all_to_all x2, starting transfers between devices, exchange(): lax.all_to_all(value, 'shard', split_axis=0, concat_axis=0, tiled=True)  21.3 us
    all_to_all x2, waiting for transfers between devices, exchange(): lax.all_to_all(value, 'shard', split_axis=0, concat_axis=0, tiled=True)  9.47 us
    ppermute x4, starting transfers between devices, from_ahead(): lax.ppermute(value, 'shard', [((source + steps * span) % SHARDS, source)...  9.2 us
    ppermute x7, starting transfers between devices, swapped(): lax.ppermute(value, BOTH, [(source, source ^ bits) for source in range(co...  8.64 us
    ppermute x1, waiting for transfers between devices, on_device(): arrived = lax.ppermute(fresh, 'role', [(0, 1)])  7.22 us
    pallas_call x1, Pallas kernels, answer_rows(): kernel_call(answer_body, jax.ShapeDtypeStruct((SHARDS * CAP, width), jnp....  3.84 us
    pallas_call x1, Pallas kernels, train_rows(): kernel_call(train_body, (jax.ShapeDtypeStruct((rows, width), jnp.float32)...  3.77 us
  transfers between devices with their start and end apart: 15, of which 8 were waited for; matrix products, arithmetic and copies ran while one was open for 0% of the time, Pallas kernels for 13%

profile of v6, /device:TPU:2, one launch (start us, length us, event | category | flops | bytes accessed | tf_op | source)
XLA Modules:
  0.0 101.2 jit_solution(4666854659930243937)
XLA Ops:
  0.7 1.5 %shard_map.134 = (f32[2,32,24,128]{3,2,1,0:T(8,128)S(1)}, f32[2,32,24,128]{3,2,1,0:T(8,128)S(1)}, f32[2,2,24,128]{3,2,1,0:T(8,128)S(1)}, f32[2,2,24,128]{3,2,1,0:T(8,128)S(1)}) custom-call(f32[32,2,24,512]{3,2,1,0:T(8,128)} %bitcast.23, f32[32,2,24,512]{3,2,1,0:T(8,128)} %bitcast.24, f32[32,2,24,512]{3,2,1,0:T(8,128)} %bitcast.25), custom_call_target="tpu_custom_call" | custom-call | bytes 4000000 | tf_op jit(solution)/shard_map/pallas_call | solution.py:98
  2.3 1.4 %shard_map.133 = (s32[8,512]{1,0:T(8,128)S(1)}, f32[128,128]{1,0:T(8,128)S(1)}) custom-call(s32[4,512]{1,0:T(4,128)S(1)} %bitcast.18, s32[4,512]{1,0:T(4,128)S(1)} %bitcast.19), custom_call_target="tpu_custom_call" | custom-call | tf_op jit(solution)/shard_map/pallas_call | solution.py:149
  4.6 0.9 shard_map.135
  5.5 14.9 %all-to-all-start = ((bf16[128,16,128]{2,1,0:T(8,128)(2,1)}), bf16[128,16,128]{2,1,0:T(8,128)(2,1)S(1)}, u32[]{:S(2)}, u32[]{:S(2)}) async-start(bf16[128,16,128]{2,1,0:T(8,128)(2,1)} %shard_map.135), calls=%async_computation | async-start | bytes 1048576 | tf_op jit(solution)/shard_map/all_to_all | solution.py:548
  21.1 3.8 %shard_map.131 = (f32[2048,128]{1,0:T(8,128)S(1)}, bf16[2048,128]{1,0:T(8,128)(2,1)S(1)}, bf16[512,128]{1,0:T(8,128)(2,1)S(1)}) custom-call(s32[1]{0:T(128)S(6)} %copy.25.count_ref, s32[1,512]{1,0:T(1,128)S(1)} %bitcast.20, f32[2048,128]{1,0:T(8,128)S(1)} %bitcast.15, f32[2048,128]{1,0:T(8,128)S(1)} %copy-done.1, f32[512,128]{1,0:T(8,128)S(1)} %copy-done.2), custom_call_target="tpu_custom_call" | custom-call | tf_op jit(solution)/shard_map/pallas_call | solution.py:252
  24.8 1.3 %collective-permute-start = (bf16[512,128]{1,0:T(8,128)(2,1)S(1)}, bf16[512,128]{1,0:T(8,128)(2,1)S(1)}, u32[]{:S(2)}, u32[]{:S(2)}) collective-permute-start(bf16[512,128]{1,0:T(8,128)(2,1)S(1)} %get-tuple-element.15), channel_id=1, source_target_pairs={{0,128},{1,129},{2,130},{3,131},{4,132},{5,133},{6,134},{7,135},{8... | collective-permute-start | bytes 393224 | tf_op jit(solution)/shard_map/ppermute | solution.py:579
  26.1 1.3 %collective-permute-start.3 = (f32[2,2,24,128]{3,2,1,0:T(8,128)S(1)}, f32[2,2,24,128]{3,2,1,0:T(8,128)S(1)}, u32[]{:S(2)}, u32[]{:S(2)}) collective-permute-start(f32[2,2,24,128]{3,2,1,0:T(8,128)S(1)} %get-tuple-element.26.state_ref), channel_id=1, source_target_pairs={{0,128},{1,129},{2,130},{3,131},{4,132},{5,133},{6,134},{7,135},{8... | collective-permute-start | bytes 147464 | tf_op jit(solution)/shard_map/ppermute | solution.py:572
  27.4 7.2 %collective-permute-done.arrived_ref = bf16[512,128]{1,0:T(8,128)(2,1)S(1)} collective-permute-done((bf16[512,128]{1,0:T(8,128)(2,1)S(1)}, bf16[512,128]{1,0:T(8,128)(2,1)S(1)}, u32[]{:S(2)}, u32[]{:S(2)}) %collective-permute-start) | collective-permute-done | bytes 131104 | tf_op jit(solution)/shard_map/ppermute | solution.py:579
  34.7 1.7 %shard_map.132 = (f32[2048,128]{1,0:T(8,128)}, bf16[2048,128]{1,0:T(8,128)(2,1)S(1)}) custom-call(s32[1]{0:T(128)S(6)} %copy.25.count_ref, s32[1,512]{1,0:T(1,128)S(1)} %bitcast.21, bf16[512,128]{1,0:T(8,128)(2,1)S(1)} %collective-permute-done.arrived_ref, f32[2048,128]{1,0:T(8,128)S(1)} %bitcast.16, f32[2048,128]{1,0:T(8,128)S(1)} %get-tuple-element.16.new_ref, ...), custom_call_target="tpu_custom_call" | custom-call | tf_op jit(solution)/shard_map/pallas_call | solution.py:308
  36.4 5.5 %all-to-all-done.packed_ref = bf16[128,16,128]{2,1,0:T(8,128)(2,1)S(1)} async-done(((bf16[128,16,128]{2,1,0:T(8,128)(2,1)}), bf16[128,16,128]{2,1,0:T(8,128)(2,1)S(1)}, u32[]{:S(2)}, u32[]{:S(2)}) %all-to-all-start) | async-done | bytes 524320 | tf_op jit(solution)/shard_map/all_to_all | solution.py:548
  42.0 1.5 %collective-permute-start.2 = (f32[2,16,128]{2,1,0:T(8,128)S(1)}, f32[2,16,128]{2,1,0:T(8,128)S(1)}, u32[]{:S(2)}, u32[]{:S(2)}) collective-permute-start(f32[2,16,128]{2,1,0:T(8,128)S(1)} %get-tuple-element.25.sum_ref), channel_id=1, source_target_pairs={{0,128},{1,129},{2,130},{3,131},{4,132},{5,133},{6,134},{7,135},{8... | collective-permute-start | bytes 49160 | tf_op jit(solution)/shard_map/ppermute | solution.py:535
  43.5 3.8 %shard_map.137.answer_ref.value_ref = bf16[4096,128]{1,0:T(8,128)(2,1)} custom-call(f32[128,128]{1,0:T(8,128)S(1)} %get-tuple-element.24.asked_ref, bf16[2048,128]{1,0:T(8,128)(2,1)S(1)} %get-tuple-element.23.lookup_ref.table_ref), custom_call_target="tpu_custom_call" | custom-call | tf_op jit(solution)/shard_map/pallas_call | solution.py:401
  48.3 2.4 %collective-permute-start.4 = (bf16[48,128]{1,0:T(8,128)(2,1)S(1)}, bf16[48,128]{1,0:T(8,128)(2,1)S(1)}, u32[]{:S(2)}, u32[]{:S(2)}) collective-permute-start(bf16[48,128]{1,0:T(8,128)(2,1)S(1)} %shard_map.138), channel_id=1, source_target_pairs={{16,0},{17,1},{18,2},{19,3},{20,4},{21,5},{22,6},{23,7},{24,8},{25... | collective-permute-start | bytes 36872 | tf_op jit(solution)/shard_map/ppermute | solution.py:540
  50.8 1.7 %collective-permute-done.5 = bf16[48,128]{1,0:T(8,128)(2,1)S(1)} collective-permute-done((bf16[48,128]{1,0:T(8,128)(2,1)S(1)}, bf16[48,128]{1,0:T(8,128)(2,1)S(1)}, u32[]{:S(2)}, u32[]{:S(2)}) %collective-permute-start.5) | collective-permute-done | bytes 12320 | tf_op jit(solution)/shard_map/ppermute | solution.py:540
  53.0 5.3 %collective-permute-start.7 = (bf16[96,128]{1,0:T(8,128)(2,1)S(1)}, bf16[96,128]{1,0:T(8,128)(2,1)S(1)}, u32[]{:S(2)}, u32[]{:S(2)}) collective-permute-start(bf16[96,128]{1,0:T(8,128)(2,1)S(1)} %pad_maximum_fusion.1), channel_id=1, source_target_pairs={{96,0},{97,1},{98,2},{99,3},{100,4},{101,5},{102,6},{103,7},{104,8... | collective-permute-start | bytes 73736 | tf_op jit(solution)/shard_map/ppermute | solution.py:540
  58.3 6.4 %all-to-all-start.1 = ((bf16[128,32,128]{2,1,0:T(8,128)(2,1)}), bf16[128,32,128]{2,1,0:T(8,128)(2,1)S(1)}, u32[]{:S(2)}, u32[]{:S(2)}) async-start(bf16[128,32,128]{2,1,0:T(8,128)(2,1)} %bitcast.10), calls=%async_computation.1 | async-start | bytes 2097152 | tf_op jit(solution)/shard_map/all_to_all | solution.py:548
  64.8 2.6 %collective-permute-start.8 = (bf16[384,128]{1,0:T(8,128)(2,1)S(1)}, bf16[384,128]{1,0:T(8,128)(2,1)S(1)}, u32[]{:S(2)}, u32[]{:S(2)}) collective-permute-start(bf16[384,128]{1,0:T(8,128)(2,1)S(1)} %get-tuple-element.30), channel_id=1, source_target_pairs={{0,2},{1,3},{2,0},{3,1},{4,6},{5,7},{6,4},{7,5},{8,10},{9,11},{10,... | collective-permute-start | bytes 294920 | tf_op jit(solution)/shard_map/ppermute | solution.py:535
  67.4 4.8 %collective-permute-done.8 = bf16[384,128]{1,0:T(8,128)(2,1)S(1)} collective-permute-done((bf16[384,128]{1,0:T(8,128)(2,1)S(1)}, bf16[384,128]{1,0:T(8,128)(2,1)S(1)}, u32[]{:S(2)}, u32[]{:S(2)}) %collective-permute-start.8) | collective-permute-done | bytes 98336 | tf_op jit(solution)/shard_map/ppermute | solution.py:535
  72.2 3.4 %collective-permute-start.11 = (bf16[768,128]{1,0:T(8,128)(2,1)S(1)}, bf16[768,128]{1,0:T(8,128)(2,1)S(1)}, u32[]{:S(2)}, u32[]{:S(2)}) collective-permute-start(bf16[768,128]{1,0:T(8,128)(2,1)S(1)} %constant_dynamic-update-slice_fusion.5.refs_0_), channel_id=1, source_target_pairs={{0,12},{1,13},{2,14},{3,15},{4,8},{5,9},{6,10},{7,11},{8,4},{9,5},... | collective-permute-start | bytes 589832 | tf_op jit(solution)/shard_map/ppermute | solution.py:535
  76.5 14.7 %collective-permute-done.11.refs_3_ = bf16[768,128]{1,0:T(8,128)(2,1)S(1)} collective-permute-done((bf16[768,128]{1,0:T(8,128)(2,1)S(1)}, bf16[768,128]{1,0:T(8,128)(2,1)S(1)}, u32[]{:S(2)}, u32[]{:S(2)}) %collective-permute-start.11) | collective-permute-done | bytes 196640 | tf_op jit(solution)/shard_map/ppermute | solution.py:535
  91.2 1.2 %collective-permute-done.9.refs_1_ = bf16[768,128]{1,0:T(8,128)(2,1)S(1)} collective-permute-done((bf16[768,128]{1,0:T(8,128)(2,1)S(1)}, bf16[768,128]{1,0:T(8,128)(2,1)S(1)}, u32[]{:S(2)}, u32[]{:S(2)}) %collective-permute-start.9) | collective-permute-done | bytes 196640 | tf_op jit(solution)/shard_map/ppermute | solution.py:535
  92.8 3.9 %all-to-all-done.1 = bf16[128,32,128]{2,1,0:T(8,128)(2,1)S(1)} async-done(((bf16[128,32,128]{2,1,0:T(8,128)(2,1)}), bf16[128,32,128]{2,1,0:T(8,128)(2,1)S(1)}, u32[]{:S(2)}, u32[]{:S(2)}) %all-to-all-start.1) | async-done | bytes 1048608 | tf_op jit(solution)/shard_map/all_to_all | solution.py:548
  96.7 2.6 %shard_map.140.base_ref = bf16[512,512]{1,0:T(8,128)(2,1)S(1)} custom-call(s32[8,512]{1,0:T(8,128)S(1)} %get-tuple-element.19.place_ref, bf16[4096,128]{1,0:T(8,128)(2,1)S(1)} %bitcast.17), custom_call_target="tpu_custom_call" | custom-call | flops 2147483648 | bytes 2000000 | tf_op jit(solution)/shard_map/pallas_call | solution.py:477
  99.3 1.8 %shard_map.142 = f32[1,512]{1,0:T(1,128)} custom-call(bf16[512,512]{1,0:T(8,128)(2,1)S(1)} %shard_map.140.base_ref, f32[3,512]{1,0:T(4,128)S(1)} %copy-done.6, f32[1,512]{1,0:T(1,128)S(1)} %bitcast.22, bf16[1536,256]{1,0:T(8,128)(2,1)S(1)} %shard_map.141.own_ref, bf16[1536,256]{1,0:T(8,128)(2,1)S(1)} %collective-permute-done.12.other_ref), custom_call_target="tpu_custom_call" | custom-call | flops 805306368 | bytes 3000000 | tf_op jit(solution)/shard_map/pallas_call | solution.py:519
  (42 shorter events, 4.0 us)
Async XLA Ops:
  0.6 1.7 %copy-start.3 = (s32[1,512,4]{1,2,0:T(4,128)S(1)}, s32[1,512,4]{1,2,0:T(4,128)}, u32[]{:S(2)}) copy-start(s32[1,512,4]{1,2,0:T(4,128)} %param.22) | copy-start | bytes 24580
  0.6 1.7 %copy-start.4 = (s32[1,512,4]{1,2,0:T(4,128)S(1)}, s32[1,512,4]{1,2,0:T(4,128)}, u32[]{:S(2)}) copy-start(s32[1,512,4]{1,2,0:T(4,128)} %param.23) | copy-start | bytes 24580
  2.1 18.9 %copy-start = (f32[1,2048,128]{2,1,0:T(8,128)S(1)}, f32[1,2048,128]{2,1,0:T(8,128)}, u32[]{:S(2)}) copy-start(f32[1,2048,128]{2,1,0:T(8,128)} %param.12) | copy-start | bytes 3145732
  2.1 18.9 %copy-start.1 = (f32[2048,128]{1,0:T(8,128)S(1)}, f32[2048,128]{1,0:T(8,128)}, u32[]{:S(2)}) copy-start(f32[2048,128]{1,0:T(8,128)} %square_ref.1) | copy-start | bytes 3145732
  2.2 18.9 %copy-start.2 = (f32[512,128]{1,0:T(8,128)S(1)}, f32[512,128]{1,0:T(8,128)}, u32[]{:S(2)}) copy-start(f32[512,128]{1,0:T(8,128)} %grad_ref.1) | copy-start | bytes 786436
  2.2 18.9 %copy-start.5 = (s32[512]{0:T(512)S(1)}, s32[512]{0:T(512)}, u32[]{:S(2)}) copy-start(s32[512]{0:T(512)} %param.14) | copy-start | bytes 6148
  2.2 2.4 %collective-permute-start.1 = (f32[2,32,24,128]{3,2,1,0:T(8,128)S(1)}, f32[2,32,24,128]{3,2,1,0:T(8,128)S(1)}, u32[]{:S(2)}, u32[]{:S(2)}) collective-permute-start(f32[2,32,24,128]{3,2,1,0:T(8,128)S(1)} %get-tuple-element.21), channel_id=1, source_target_pairs={{0,1},{1,0},{2,3},{3,2},{4,5},{5,4},{6,7},{7,6},{8,9},{9,8},{10,11... | collective-permute-start | bytes 2359304 | tf_op jit(solution)/shard_map/ppermute | solution.py:535
  5.5 36.4 %all-to-all-start = ((bf16[128,16,128]{2,1,0:T(8,128)(2,1)}), bf16[128,16,128]{2,1,0:T(8,128)(2,1)S(1)}, u32[]{:S(2)}, u32[]{:S(2)}) async-start(bf16[128,16,128]{2,1,0:T(8,128)(2,1)} %shard_map.135), calls=%async_computation | async-start | bytes 1048576 | tf_op jit(solution)/shard_map/all_to_all | solution.py:548
  24.8 9.8 %collective-permute-start = (bf16[512,128]{1,0:T(8,128)(2,1)S(1)}, bf16[512,128]{1,0:T(8,128)(2,1)S(1)}, u32[]{:S(2)}, u32[]{:S(2)}) collective-permute-start(bf16[512,128]{1,0:T(8,128)(2,1)S(1)} %get-tuple-element.15), channel_id=1, source_target_pairs={{0,128},{1,129},{2,130},{3,131},{4,132},{5,133},{6,134},{7,135},{8... | collective-permute-start | bytes 393224 | tf_op jit(solution)/shard_map/ppermute | solution.py:579
  26.1 21.2 %collective-permute-start.3 = (f32[2,2,24,128]{3,2,1,0:T(8,128)S(1)}, f32[2,2,24,128]{3,2,1,0:T(8,128)S(1)}, u32[]{:S(2)}, u32[]{:S(2)}) collective-permute-start(f32[2,2,24,128]{3,2,1,0:T(8,128)S(1)} %get-tuple-element.26.state_ref), channel_id=1, source_target_pairs={{0,128},{1,129},{2,130},{3,131},{4,132},{5,133},{6,134},{7,135},{8... | collective-permute-start | bytes 147464 | tf_op jit(solution)/shard_map/ppermute | solution.py:572
  42.0 5.4 %collective-permute-start.2 = (f32[2,16,128]{2,1,0:T(8,128)S(1)}, f32[2,16,128]{2,1,0:T(8,128)S(1)}, u32[]{:S(2)}, u32[]{:S(2)}) collective-permute-start(f32[2,16,128]{2,1,0:T(8,128)S(1)} %get-tuple-element.25.sum_ref), channel_id=1, source_target_pairs={{0,128},{1,129},{2,130},{3,131},{4,132},{5,133},{6,134},{7,135},{8... | collective-permute-start | bytes 49160 | tf_op jit(solution)/shard_map/ppermute | solution.py:535
  47.4 5.0 %collective-permute-start.5 = (bf16[48,128]{1,0:T(8,128)(2,1)S(1)}, bf16[48,128]{1,0:T(8,128)(2,1)S(1)}, u32[]{:S(2)}, u32[]{:S(2)}) collective-permute-start(bf16[48,128]{1,0:T(8,128)(2,1)S(1)} %shard_map.138), channel_id=1, source_target_pairs={{112,0},{113,1},{114,2},{115,3},{116,4},{117,5},{118,6},{119,7},{1... | collective-permute-start | bytes 36872 | tf_op jit(solution)/shard_map/ppermute | solution.py:540
  48.3 4.1 %collective-permute-start.4 = (bf16[48,128]{1,0:T(8,128)(2,1)S(1)}, bf16[48,128]{1,0:T(8,128)(2,1)S(1)}, u32[]{:S(2)}, u32[]{:S(2)}) collective-permute-start(bf16[48,128]{1,0:T(8,128)(2,1)S(1)} %shard_map.138), channel_id=1, source_target_pairs={{16,0},{17,1},{18,2},{19,3},{20,4},{21,5},{22,6},{23,7},{24,8},{25... | collective-permute-start | bytes 36872 | tf_op jit(solution)/shard_map/ppermute | solution.py:540
  52.4 12.3 %collective-permute-start.6 = (bf16[144,128]{1,0:T(8,128)(2,1)S(1)}, bf16[144,128]{1,0:T(8,128)(2,1)S(1)}, u32[]{:S(2)}, u32[]{:S(2)}) collective-permute-start(bf16[144,128]{1,0:T(8,128)(2,1)S(1)} %pad_maximum_fusion.other_ref), channel_id=1, source_target_pairs={{48,0},{49,1},{50,2},{51,3},{52,4},{53,5},{54,6},{55,7},{56,8},{57... | collective-permute-start | bytes 110600 | tf_op jit(solution)/shard_map/ppermute | solution.py:540
  53.0 11.8 %collective-permute-start.7 = (bf16[96,128]{1,0:T(8,128)(2,1)S(1)}, bf16[96,128]{1,0:T(8,128)(2,1)S(1)}, u32[]{:S(2)}, u32[]{:S(2)}) collective-permute-start(bf16[96,128]{1,0:T(8,128)(2,1)S(1)} %pad_maximum_fusion.1), channel_id=1, source_target_pairs={{96,0},{97,1},{98,2},{99,3},{100,4},{101,5},{102,6},{103,7},{104,8... | collective-permute-start | bytes 73736 | tf_op jit(solution)/shard_map/ppermute | solution.py:540
  58.3 38.4 %all-to-all-start.1 = ((bf16[128,32,128]{2,1,0:T(8,128)(2,1)}), bf16[128,32,128]{2,1,0:T(8,128)(2,1)S(1)}, u32[]{:S(2)}, u32[]{:S(2)}) async-start(bf16[128,32,128]{2,1,0:T(8,128)(2,1)} %bitcast.10), calls=%async_computation.1 | async-start | bytes 2097152 | tf_op jit(solution)/shard_map/all_to_all | solution.py:548
  64.8 7.4 %collective-permute-start.8 = (bf16[384,128]{1,0:T(8,128)(2,1)S(1)}, bf16[384,128]{1,0:T(8,128)(2,1)S(1)}, u32[]{:S(2)}, u32[]{:S(2)}) collective-permute-start(bf16[384,128]{1,0:T(8,128)(2,1)S(1)} %get-tuple-element.30), channel_id=1, source_target_pairs={{0,2},{1,3},{2,0},{3,1},{4,6},{5,7},{6,4},{7,5},{8,10},{9,11},{10,... | collective-permute-start | bytes 294920 | tf_op jit(solution)/shard_map/ppermute | solution.py:535
  72.2 19.0 %collective-permute-start.11 = (bf16[768,128]{1,0:T(8,128)(2,1)S(1)}, bf16[768,128]{1,0:T(8,128)(2,1)S(1)}, u32[]{:S(2)}, u32[]{:S(2)}) collective-permute-start(bf16[768,128]{1,0:T(8,128)(2,1)S(1)} %constant_dynamic-update-slice_fusion.5.refs_0_), channel_id=1, source_target_pairs={{0,12},{1,13},{2,14},{3,15},{4,8},{5,9},{6,10},{7,11},{8,4},{9,5},... | collective-permute-start | bytes 589832 | tf_op jit(solution)/shard_map/ppermute | solution.py:535
  75.6 15.6 %collective-permute-start.10 = (bf16[768,128]{1,0:T(8,128)(2,1)S(1)}, bf16[768,128]{1,0:T(8,128)(2,1)S(1)}, u32[]{:S(2)}, u32[]{:S(2)}) collective-permute-start(bf16[768,128]{1,0:T(8,128)(2,1)S(1)} %constant_dynamic-update-slice_fusion.5.refs_0_), channel_id=1, source_target_pairs={{0,8},{1,9},{2,10},{3,11},{4,12},{5,13},{6,14},{7,15},{8,0},{9,1},... | collective-permute-start | bytes 589832 | tf_op jit(solution)/shard_map/ppermute | solution.py:535
  76.1 16.3 %collective-permute-start.9 = (bf16[768,128]{1,0:T(8,128)(2,1)S(1)}, bf16[768,128]{1,0:T(8,128)(2,1)S(1)}, u32[]{:S(2)}, u32[]{:S(2)}) collective-permute-start(bf16[768,128]{1,0:T(8,128)(2,1)S(1)} %constant_dynamic-update-slice_fusion.5.refs_0_), channel_id=1, source_target_pairs={{0,4},{1,5},{2,6},{3,7},{4,0},{5,1},{6,2},{7,3},{8,12},{9,13},{10,... | collective-permute-start | bytes 589832 | tf_op jit(solution)/shard_map/ppermute | solution.py:535
  92.7 6.6 %collective-permute-start.12 = (bf16[1536,256]{1,0:T(8,128)(2,1)S(1)}, bf16[1536,256]{1,0:T(8,128)(2,1)S(1)}, u32[]{:S(2)}, u32[]{:S(2)}) collective-permute-start(bf16[1536,256]{1,0:T(8,128)(2,1)S(1)} %shard_map.141.own_ref), channel_id=1, source_target_pairs={{0,1},{1,0},{2,3},{3,2},{4,5},{5,4},{6,7},{7,6},{8,9},{9,8},{10,11... | collective-permute-start | bytes 2359304 | tf_op jit(solution)/shard_map/ppermute | solution.py:535
  96.7 2.6 %copy-start.6 = (f32[3,512]{1,0:T(4,128)S(1)}, f32[3,512]{1,0:T(4,128)}, u32[]{:S(2)}) copy-start(f32[3,512]{1,0:T(4,128)} %bias_ref.1) | copy-start | bytes 18436
  96.7 2.6 %copy-start.7 = (f32[512]{0:T(512)S(1)}, f32[512]{0:T(512)}, u32[]{:S(2)}) copy-start(f32[512]{0:T(512)} %param.21) | copy-start | bytes 6148

commit v7 on v6

--- a/solution.py
+++ b/solution.py
@@ -13,11 +13,12 @@
 ROLES = 2
 Z_SIZE, Y_SIZE, X_SIZE, CORES = 8, 4, 2, 2
 BLOCKS = Z_SIZE * Y_SIZE
-Z_ORDER = (0, 1, 7, 3, 4, 2, 6, 5)
+Z_ORDER = (0, 1, 7, 5, 6, 4, 2, 3)
 TILES = 2
 SHARE = 12
 PACKED = 16
 VMEM_LIMIT = 24 * 1024 * 1024
+FETCH_LIMIT = 52 * 1024 * 1024
 
 
 def ftrl_weight(linear, squares, shrink):
@@ -71,42 +72,40 @@
     return copies
 
 
-def fetch_body(grad_ref, state_ref, square_ref, send_ref, keep_ref, own_state_ref, own_square_ref, arrived):
+def fetch_body(grad_ref, send_ref, arrived):
+    copies = half_copies(grad_ref, send_ref, 1, arrived)
+    for copy in copies:
+        copy.start()
+    for copy in copies:
+        copy.wait()
+
+
+def fetch(grads):
+    return kernel_call(
+        fetch_body,
+        jax.ShapeDtypeStruct((TILES, BLOCKS, 2 * SHARE, LANES), jnp.float32),
+        vmem=FETCH_LIMIT,
+        in_specs=[HBM],
+        out_specs=VMEM,
+        scratch_shapes=[pltpu.SemaphoreType.DMA((TILES,))],
+    )(grads)
+
+
+def route_body(owner_ref, slot_ref, grad_ref, state_ref, square_ref, place_ref, request_ref, keep_ref, own_state_ref, own_square_ref, arrived):
     _, shard, core = position()
-    copies = half_copies(grad_ref, send_ref, 1, arrived.at[:TILES])
-    copies += half_copies(grad_ref, keep_ref, 0, arrived.at[TILES : 2 * TILES])
-    block = shard // (X_SIZE * CORES)
+    copies = half_copies(grad_ref, keep_ref, 0, arrived)
     for source, target in ((state_ref, own_state_ref), (square_ref, own_square_ref)):
         for column in range(CORES):
             left = pl.multiple_of((column * TILES + core) * LANES, LANES)
             copies.append(
                 pltpu.make_async_copy(
-                    source.at[block, :, :, pl.ds(left, LANES)],
+                    source.at[shard // (X_SIZE * CORES), :, :, pl.ds(left, LANES)],
                     target.at[column],
                     arrived.at[len(copies)],
                 )
             )
     for copy in copies:
         copy.start()
-    for copy in copies:
-        copy.wait()
-
-
-def fetch(grads, state, squares):
-    halves = jax.ShapeDtypeStruct((TILES, BLOCKS, 2 * SHARE, LANES), jnp.float32)
-    own = jax.ShapeDtypeStruct((CORES, ROLES, 2 * SHARE, LANES), jnp.float32)
-    return kernel_call(
-        fetch_body,
-        (halves, halves, own, own),
-        bytes_accessed=4_000_000,
-        vmem=52 * 1024 * 1024,
-        in_specs=[HBM] * 3,
-        out_specs=(VMEM,) * 4,
-        scratch_shapes=[pltpu.SemaphoreType.DMA((2 * TILES + 2 * CORES,))],
-    )(grads, state, squares)
-
-
-def route_body(owner_ref, slot_ref, place_ref, request_ref):
     fields, examples = owner_ref.shape
     shape = (SHARDS, examples)
     shard_ids = iota(shape, 0)
@@ -142,19 +141,27 @@
     request_ref[...] = jnp.concatenate(
         [asked >> 4, asked & 15, jnp.zeros((SHARDS, LANES - 2 * CAP), jnp.int32)], axis=1
     ).astype(jnp.float32)
-
-
-def route(owners, slots):
+    for copy in copies:
+        copy.wait()
+
+
+def route(owners, slots, grads, state, squares):
     examples = owners.shape[1]
+    own = jax.ShapeDtypeStruct((CORES, ROLES, 2 * SHARE, LANES), jnp.float32)
     return kernel_call(
         route_body,
         (
             jax.ShapeDtypeStruct((8, examples), jnp.int32),
             jax.ShapeDtypeStruct((SHARDS, LANES), jnp.float32),
+            jax.ShapeDtypeStruct((TILES, BLOCKS, 2 * SHARE, LANES), jnp.float32),
+            own,
+            own,
         ),
-        in_specs=[VMEM, VMEM],
-        out_specs=(VMEM, VMEM),
-    )(owners, slots)
+        vmem=FETCH_LIMIT,
+        in_specs=[VMEM] * 2 + [HBM] * 3,
+        out_specs=(VMEM,) * 5,
+        scratch_shapes=[pltpu.SemaphoreType.DMA((TILES + 2 * CORES,))],
+    )(owners, slots, grads, state, squares)
 
 
 def pack_body(keep_ref, arrived_ref, request_ref, packed_ref):
@@ -565,12 +572,15 @@
     fields = cand_owner.shape[2]
     blocks = (BLOCKS, ROLES, 2 * SHARE, dense_squares.shape[2])
     grads = dense_grads.reshape(blocks)
-    send, keep, own_state, own_squares = fetch(
-        grads, dense_state.reshape(blocks), dense_squares.reshape(blocks)
-    )
-    paired = swapped(send, CORE_BIT)
+    paired = swapped(fetch(grads), CORE_BIT)
+    places, requests, keep, own_state, own_squares = route(
+        cand_owner[0].T,
+        cand_slot[0].T,
+        grads,
+        dense_state.reshape(blocks),
+        dense_squares.reshape(blocks),
+    )
     trained = lax.ppermute(own_state, "role", [(0, 1)])
-    places, requests = route(cand_owner[0].T, cand_slot[0].T)
     packed = exchange(pack(keep, paired, requests))
     slots = update_slots.reshape(1, -1)
     new_linear, weights, fresh = train_rows(
@@ -590,8 +600,8 @@
     pieces = jnp.concatenate(
         [
             three,
-            from_ahead(three, 3),
-            from_ahead(jnp.concatenate([piece, behind], axis=0), -2),
+            from_ahead(three, -3),
+            from_ahead(jnp.concatenate([piece, ahead], axis=0), 2),
         ],
         axis=0,
     )

time: 103 us -> 101 us (0.981)
  starting transfers between devices: 41.7 us -> 40.2 us
  waiting for transfers between devices: 39.9 us -> 38.8 us
    ppermute x4, starting transfers between devices: 9.2 us -> 6.57 us  [from_ahead(): lax.ppermute(value, 'shard', [((source + steps * span) % SHARDS, source)...]
    all_to_all x2, starting transfers between devices: 21.3 us -> 22.4 us  [exchange(): lax.all_to_all(value, 'shard', split_axis=0, concat_axis=0, tiled=True)]
  transfers between devices with their start and end apart: 15 -> 15, of which waited for: 8 -> 7; matrix products, arithmetic and copies ran while one was open for 0% -> 0% of each run, Pallas kernels for 13% -> 15%
where the time goes in v7:
time: 101 us; the launch traced here: 99.1 us
  starting transfers between devices  40.2 us (40%)
  waiting for transfers between devices  38.8 us (38%)
  Pallas kernels  18.4 us (18%)
  between operations  1.54 us (2%)
    all_to_all x2, starting transfers between devices, exchange(): lax.all_to_all(value, 'shard', split_axis=0, concat_axis=0, tiled=True)  22.4 us
    ppermute x7, waiting for transfers between devices, swapped(): lax.ppermute(value, BOTH, [(source, source ^ bits) for source in range(co...  20.7 us
    all_to_all x2, waiting for transfers between devices, exchange(): lax.all_to_all(value, 'shard', split_axis=0, concat_axis=0, tiled=True)  9.19 us
    ppermute x7, starting transfers between devices, swapped(): lax.ppermute(value, BOTH, [(source, source ^ bits) for source in range(co...  8.67 us
    ppermute x1, waiting for transfers between devices, on_device(): arrived = lax.ppermute(fresh, 'role', [(0, 1)])  7.22 us
    ppermute x4, starting transfers between devices, from_ahead(): lax.ppermute(value, 'shard', [((source + steps * span) % SHARDS, source)...  6.57 us
    pallas_call x1, Pallas kernels, answer_rows(): kernel_call(answer_body, jax.ShapeDtypeStruct((SHARDS * CAP, width), jnp....  3.83 us
    pallas_call x1, Pallas kernels, train_rows(): kernel_call(train_body, (jax.ShapeDtypeStruct((rows, width), jnp.float32)...  3.77 us
  transfers between devices with their start and end apart: 15, of which 7 were waited for; matrix products, arithmetic and copies ran while one was open for 0% of the time, Pallas kernels for 15%

profile of v7, /device:TPU:2, one launch (start us, length us, event | category | flops | bytes accessed | tf_op | source)
XLA Modules:
  0.0 99.1 jit_solution(12444731126414515036)
XLA Ops:
  0.6 1.2 %shard_map.134 = f32[2,32,24,128]{3,2,1,0:T(8,128)S(1)} custom-call(f32[32,2,24,512]{3,2,1,0:T(8,128)} %bitcast.23), custom_call_target="tpu_custom_call" | custom-call | tf_op jit(solution)/shard_map/pallas_call | solution.py:84
  1.9 2.2 %shard_map.133 = (s32[8,512]{1,0:T(8,128)S(1)}, f32[128,128]{1,0:T(8,128)S(1)}, f32[2,32,24,128]{3,2,1,0:T(8,128)S(1)}, f32[2,2,24,128]{3,2,1,0:T(8,128)S(1)}, f32[2,2,24,128]{3,2,1,0:T(8,128)S(1)}) custom-call(s32[4,512]{1,0:T(4,128)S(1)} %bitcast.18, s32[4,512]{1,0:T(4,128)S(1)} %bitcast.19, f32[32,2,24,512]{3,2,1,0:T(8,128)} %bitcast.24, ...), custom_call_target="tpu_custom_call" | custom-call | tf_op jit(solution)/shard_map/pallas_call | solution.py:151
  4.2 0.9 shard_map.135
  5.1 14.9 %all-to-all-start = ((bf16[128,16,128]{2,1,0:T(8,128)(2,1)}), bf16[128,16,128]{2,1,0:T(8,128)(2,1)S(1)}, u32[]{:S(2)}, u32[]{:S(2)}) async-start(bf16[128,16,128]{2,1,0:T(8,128)(2,1)} %shard_map.135), calls=%async_computation | async-start | bytes 1048576 | tf_op jit(solution)/shard_map/all_to_all | solution.py:555
  20.7 3.8 %shard_map.131 = (f32[2048,128]{1,0:T(8,128)S(1)}, bf16[2048,128]{1,0:T(8,128)(2,1)S(1)}, bf16[512,128]{1,0:T(8,128)(2,1)S(1)}) custom-call(s32[1]{0:T(128)S(6)} %copy.25.count_ref, s32[1,512]{1,0:T(1,128)S(1)} %bitcast.20, f32[2048,128]{1,0:T(8,128)S(1)} %bitcast.15, f32[2048,128]{1,0:T(8,128)S(1)} %copy-done.1, f32[512,128]{1,0:T(8,128)S(1)} %copy-done.2), custom_call_target="tpu_custom_call" | custom-call | tf_op jit(solution)/shard_map/pallas_call | solution.py:259
  24.5 1.3 %collective-permute-start = (bf16[512,128]{1,0:T(8,128)(2,1)S(1)}, bf16[512,128]{1,0:T(8,128)(2,1)S(1)}, u32[]{:S(2)}, u32[]{:S(2)}) collective-permute-start(bf16[512,128]{1,0:T(8,128)(2,1)S(1)} %get-tuple-element.14), channel_id=1, source_target_pairs={{0,128},{1,129},{2,130},{3,131},{4,132},{5,133},{6,134},{7,135},{8... | collective-permute-start | bytes 393224 | tf_op jit(solution)/shard_map/ppermute | solution.py:589
  25.8 1.3 %collective-permute-start.3 = (f32[2,2,24,128]{3,2,1,0:T(8,128)S(1)}, f32[2,2,24,128]{3,2,1,0:T(8,128)S(1)}, u32[]{:S(2)}, u32[]{:S(2)}) collective-permute-start(f32[2,2,24,128]{3,2,1,0:T(8,128)S(1)} %get-tuple-element.24.state_ref), channel_id=1, source_target_pairs={{0,128},{1,129},{2,130},{3,131},{4,132},{5,133},{6,134},{7,135},{8... | collective-permute-start | bytes 147464 | tf_op jit(solution)/shard_map/ppermute | solution.py:583
  27.1 7.2 %collective-permute-done.arrived_ref = bf16[512,128]{1,0:T(8,128)(2,1)S(1)} collective-permute-done((bf16[512,128]{1,0:T(8,128)(2,1)S(1)}, bf16[512,128]{1,0:T(8,128)(2,1)S(1)}, u32[]{:S(2)}, u32[]{:S(2)}) %collective-permute-start) | collective-permute-done | bytes 131104 | tf_op jit(solution)/shard_map/ppermute | solution.py:589
  34.3 1.7 %shard_map.132 = (f32[2048,128]{1,0:T(8,128)}, bf16[2048,128]{1,0:T(8,128)(2,1)S(1)}) custom-call(s32[1]{0:T(128)S(6)} %copy.25.count_ref, s32[1,512]{1,0:T(1,128)S(1)} %bitcast.21, bf16[512,128]{1,0:T(8,128)(2,1)S(1)} %collective-permute-done.arrived_ref, f32[2048,128]{1,0:T(8,128)S(1)} %bitcast.16, f32[2048,128]{1,0:T(8,128)S(1)} %get-tuple-element.15.new_ref, ...), custom_call_target="tpu_custom_call" | custom-call | tf_op jit(solution)/shard_map/pallas_call | solution.py:315
  36.0 5.5 %all-to-all-done.packed_ref = bf16[128,16,128]{2,1,0:T(8,128)(2,1)S(1)} async-done(((bf16[128,16,128]{2,1,0:T(8,128)(2,1)}), bf16[128,16,128]{2,1,0:T(8,128)(2,1)S(1)}, u32[]{:S(2)}, u32[]{:S(2)}) %all-to-all-start) | async-done | bytes 524320 | tf_op jit(solution)/shard_map/all_to_all | solution.py:555
  41.7 1.5 %collective-permute-start.2 = (f32[2,16,128]{2,1,0:T(8,128)S(1)}, f32[2,16,128]{2,1,0:T(8,128)S(1)}, u32[]{:S(2)}, u32[]{:S(2)}) collective-permute-start(f32[2,16,128]{2,1,0:T(8,128)S(1)} %get-tuple-element.23.sum_ref), channel_id=1, source_target_pairs={{0,128},{1,129},{2,130},{3,131},{4,132},{5,133},{6,134},{7,135},{8... | collective-permute-start | bytes 49160 | tf_op jit(solution)/shard_map/ppermute | solution.py:542
  43.2 3.8 %shard_map.137.answer_ref.value_ref = bf16[4096,128]{1,0:T(8,128)(2,1)} custom-call(f32[128,128]{1,0:T(8,128)S(1)} %get-tuple-element.22.asked_ref, bf16[2048,128]{1,0:T(8,128)(2,1)S(1)} %get-tuple-element.21.lookup_ref.table_ref), custom_call_target="tpu_custom_call" | custom-call | tf_op jit(solution)/shard_map/pallas_call | solution.py:408
  48.0 2.4 %collective-permute-start.4 = (bf16[48,128]{1,0:T(8,128)(2,1)S(1)}, bf16[48,128]{1,0:T(8,128)(2,1)S(1)}, u32[]{:S(2)}, u32[]{:S(2)}) collective-permute-start(bf16[48,128]{1,0:T(8,128)(2,1)S(1)} %shard_map.138), channel_id=1, source_target_pairs={{16,0},{17,1},{18,2},{19,3},{20,4},{21,5},{22,6},{23,7},{24,8},{25... | collective-permute-start | bytes 36872 | tf_op jit(solution)/shard_map/ppermute | solution.py:547
  50.4 1.7 %collective-permute-done.5 = bf16[48,128]{1,0:T(8,128)(2,1)S(1)} collective-permute-done((bf16[48,128]{1,0:T(8,128)(2,1)S(1)}, bf16[48,128]{1,0:T(8,128)(2,1)S(1)}, u32[]{:S(2)}, u32[]{:S(2)}) %collective-permute-start.5) | collective-permute-done | bytes 12320 | tf_op jit(solution)/shard_map/ppermute | solution.py:547
  52.5 2.9 %collective-permute-start.7 = (bf16[96,128]{1,0:T(8,128)(2,1)S(1)}, bf16[96,128]{1,0:T(8,128)(2,1)S(1)}, u32[]{:S(2)}, u32[]{:S(2)}) collective-permute-start(bf16[96,128]{1,0:T(8,128)(2,1)S(1)} %pad_maximum_fusion.1), channel_id=1, source_target_pairs={{32,0},{33,1},{34,2},{35,3},{36,4},{37,5},{38,6},{39,7},{40,8},{41... | collective-permute-start | bytes 73736 | tf_op jit(solution)/shard_map/ppermute | solution.py:547
  55.4 7.5 %all-to-all-start.1 = ((bf16[128,32,128]{2,1,0:T(8,128)(2,1)}), bf16[128,32,128]{2,1,0:T(8,128)(2,1)S(1)}, u32[]{:S(2)}, u32[]{:S(2)}) async-start(bf16[128,32,128]{2,1,0:T(8,128)(2,1)} %bitcast.10), calls=%async_computation.1 | async-start | bytes 2097152 | tf_op jit(solution)/shard_map/all_to_all | solution.py:555
  63.0 2.7 %collective-permute-start.8 = (bf16[384,128]{1,0:T(8,128)(2,1)S(1)}, bf16[384,128]{1,0:T(8,128)(2,1)S(1)}, u32[]{:S(2)}, u32[]{:S(2)}) collective-permute-start(bf16[384,128]{1,0:T(8,128)(2,1)S(1)} %get-tuple-element.28), channel_id=1, source_target_pairs={{0,2},{1,3},{2,0},{3,1},{4,6},{5,7},{6,4},{7,5},{8,10},{9,11},{10,... | collective-permute-start | bytes 294920 | tf_op jit(solution)/shard_map/ppermute | solution.py:542
  65.7 4.8 %collective-permute-done.8 = bf16[384,128]{1,0:T(8,128)(2,1)S(1)} collective-permute-done((bf16[384,128]{1,0:T(8,128)(2,1)S(1)}, bf16[384,128]{1,0:T(8,128)(2,1)S(1)}, u32[]{:S(2)}, u32[]{:S(2)}) %collective-permute-start.8) | collective-permute-done | bytes 98336 | tf_op jit(solution)/shard_map/ppermute | solution.py:542
  70.5 3.3 %collective-permute-start.11 = (bf16[768,128]{1,0:T(8,128)(2,1)S(1)}, bf16[768,128]{1,0:T(8,128)(2,1)S(1)}, u32[]{:S(2)}, u32[]{:S(2)}) collective-permute-start(bf16[768,128]{1,0:T(8,128)(2,1)S(1)} %constant_dynamic-update-slice_fusion.5.refs_0_), channel_id=1, source_target_pairs={{0,12},{1,13},{2,14},{3,15},{4,8},{5,9},{6,10},{7,11},{8,4},{9,5},... | collective-permute-start | bytes 589832 | tf_op jit(solution)/shard_map/ppermute | solution.py:542
  74.7 14.6 %collective-permute-done.11.refs_3_ = bf16[768,128]{1,0:T(8,128)(2,1)S(1)} collective-permute-done((bf16[768,128]{1,0:T(8,128)(2,1)S(1)}, bf16[768,128]{1,0:T(8,128)(2,1)S(1)}, u32[]{:S(2)}, u32[]{:S(2)}) %collective-permute-start.11) | collective-permute-done | bytes 196640 | tf_op jit(solution)/shard_map/ppermute | solution.py:542
  89.3 1.3 %collective-permute-done.9.refs_1_ = bf16[768,128]{1,0:T(8,128)(2,1)S(1)} collective-permute-done((bf16[768,128]{1,0:T(8,128)(2,1)S(1)}, bf16[768,128]{1,0:T(8,128)(2,1)S(1)}, u32[]{:S(2)}, u32[]{:S(2)}) %collective-permute-start.9) | collective-permute-done | bytes 196640 | tf_op jit(solution)/shard_map/ppermute | solution.py:542
  91.0 3.6 %all-to-all-done.1 = bf16[128,32,128]{2,1,0:T(8,128)(2,1)S(1)} async-done(((bf16[128,32,128]{2,1,0:T(8,128)(2,1)}), bf16[128,32,128]{2,1,0:T(8,128)(2,1)S(1)}, u32[]{:S(2)}, u32[]{:S(2)}) %all-to-all-start.1) | async-done | bytes 1048608 | tf_op jit(solution)/shard_map/all_to_all | solution.py:555
  94.6 2.6 %shard_map.140.base_ref = bf16[512,512]{1,0:T(8,128)(2,1)S(1)} custom-call(s32[8,512]{1,0:T(8,128)S(1)} %get-tuple-element.18.place_ref, bf16[4096,128]{1,0:T(8,128)(2,1)S(1)} %bitcast.17), custom_call_target="tpu_custom_call" | custom-call | flops 2147483648 | bytes 2000000 | tf_op jit(solution)/shard_map/pallas_call | solution.py:484
  97.3 1.8 %shard_map.142 = f32[1,512]{1,0:T(1,128)} custom-call(bf16[512,512]{1,0:T(8,128)(2,1)S(1)} %shard_map.140.base_ref, f32[3,512]{1,0:T(4,128)S(1)} %copy-done.6, f32[1,512]{1,0:T(1,128)S(1)} %bitcast.22, bf16[1536,256]{1,0:T(8,128)(2,1)S(1)} %shard_map.141.own_ref, bf16[1536,256]{1,0:T(8,128)(2,1)S(1)} %collective-permute-done.12.other_ref), custom_call_target="tpu_custom_call" | custom-call | flops 805306368 | bytes 3000000 | tf_op jit(solution)/shard_map/pallas_call | solution.py:526
  (42 shorter events, 3.0 us)
Async XLA Ops:
  0.6 1.3 %copy-start.4 = (s32[1,512,4]{1,2,0:T(4,128)S(1)}, s32[1,512,4]{1,2,0:T(4,128)}, u32[]{:S(2)}) copy-start(s32[1,512,4]{1,2,0:T(4,128)} %param.23) | copy-start | bytes 24580
  0.6 1.3 %copy-start.3 = (s32[1,512,4]{1,2,0:T(4,128)S(1)}, s32[1,512,4]{1,2,0:T(4,128)}, u32[]{:S(2)}) copy-start(s32[1,512,4]{1,2,0:T(4,128)} %param.22) | copy-start | bytes 24580
  1.8 2.4 %collective-permute-start.1 = (f32[2,32,24,128]{3,2,1,0:T(8,128)S(1)}, f32[2,32,24,128]{3,2,1,0:T(8,128)S(1)}, u32[]{:S(2)}, u32[]{:S(2)}) collective-permute-start(f32[2,32,24,128]{3,2,1,0:T(8,128)S(1)} %shard_map.134), channel_id=1, source_target_pairs={{0,1},{1,0},{2,3},{3,2},{4,5},{5,4},{6,7},{7,6},{8,9},{9,8},{10,11... | collective-permute-start | bytes 2359304 | tf_op jit(solution)/shard_map/ppermute | solution.py:542
  4.1 16.6 %copy-start = (f32[1,2048,128]{2,1,0:T(8,128)S(1)}, f32[1,2048,128]{2,1,0:T(8,128)}, u32[]{:S(2)}) copy-start(f32[1,2048,128]{2,1,0:T(8,128)} %param.12) | copy-start | bytes 3145732
  4.1 16.6 %copy-start.1 = (f32[2048,128]{1,0:T(8,128)S(1)}, f32[2048,128]{1,0:T(8,128)}, u32[]{:S(2)}) copy-start(f32[2048,128]{1,0:T(8,128)} %square_ref.1) | copy-start | bytes 3145732
  4.1 16.6 %copy-start.2 = (f32[512,128]{1,0:T(8,128)S(1)}, f32[512,128]{1,0:T(8,128)}, u32[]{:S(2)}) copy-start(f32[512,128]{1,0:T(8,128)} %grad_ref.1) | copy-start | bytes 786436
  4.1 16.6 %copy-start.5 = (s32[512]{0:T(512)S(1)}, s32[512]{0:T(512)}, u32[]{:S(2)}) copy-start(s32[512]{0:T(512)} %param.14) | copy-start | bytes 6148
  5.1 36.5 %all-to-all-start = ((bf16[128,16,128]{2,1,0:T(8,128)(2,1)}), bf16[128,16,128]{2,1,0:T(8,128)(2,1)S(1)}, u32[]{:S(2)}, u32[]{:S(2)}) async-start(bf16[128,16,128]{2,1,0:T(8,128)(2,1)} %shard_map.135), calls=%async_computation | async-start | bytes 1048576 | tf_op jit(solution)/shard_map/all_to_all | solution.py:555
  24.5 9.8 %collective-permute-start = (bf16[512,128]{1,0:T(8,128)(2,1)S(1)}, bf16[512,128]{1,0:T(8,128)(2,1)S(1)}, u32[]{:S(2)}, u32[]{:S(2)}) collective-permute-start(bf16[512,128]{1,0:T(8,128)(2,1)S(1)} %get-tuple-element.14), channel_id=1, source_target_pairs={{0,128},{1,129},{2,130},{3,131},{4,132},{5,133},{6,134},{7,135},{8... | collective-permute-start | bytes 393224 | tf_op jit(solution)/shard_map/ppermute | solution.py:589
  25.8 21.2 %collective-permute-start.3 = (f32[2,2,24,128]{3,2,1,0:T(8,128)S(1)}, f32[2,2,24,128]{3,2,1,0:T(8,128)S(1)}, u32[]{:S(2)}, u32[]{:S(2)}) collective-permute-start(f32[2,2,24,128]{3,2,1,0:T(8,128)S(1)} %get-tuple-element.24.state_ref), channel_id=1, source_target_pairs={{0,128},{1,129},{2,130},{3,131},{4,132},{5,133},{6,134},{7,135},{8... | collective-permute-start | bytes 147464 | tf_op jit(solution)/shard_map/ppermute | solution.py:583
  41.7 5.3 %collective-permute-start.2 = (f32[2,16,128]{2,1,0:T(8,128)S(1)}, f32[2,16,128]{2,1,0:T(8,128)S(1)}, u32[]{:S(2)}, u32[]{:S(2)}) collective-permute-start(f32[2,16,128]{2,1,0:T(8,128)S(1)} %get-tuple-element.23.sum_ref), channel_id=1, source_target_pairs={{0,128},{1,129},{2,130},{3,131},{4,132},{5,133},{6,134},{7,135},{8... | collective-permute-start | bytes 49160 | tf_op jit(solution)/shard_map/ppermute | solution.py:542
  47.1 5.0 %collective-permute-start.5 = (bf16[48,128]{1,0:T(8,128)(2,1)S(1)}, bf16[48,128]{1,0:T(8,128)(2,1)S(1)}, u32[]{:S(2)}, u32[]{:S(2)}) collective-permute-start(bf16[48,128]{1,0:T(8,128)(2,1)S(1)} %shard_map.138), channel_id=1, source_target_pairs={{112,0},{113,1},{114,2},{115,3},{116,4},{117,5},{118,6},{119,7},{1... | collective-permute-start | bytes 36872 | tf_op jit(solution)/shard_map/ppermute | solution.py:547
  48.0 4.1 %collective-permute-start.4 = (bf16[48,128]{1,0:T(8,128)(2,1)S(1)}, bf16[48,128]{1,0:T(8,128)(2,1)S(1)}, u32[]{:S(2)}, u32[]{:S(2)}) collective-permute-start(bf16[48,128]{1,0:T(8,128)(2,1)S(1)} %shard_map.138), channel_id=1, source_target_pairs={{16,0},{17,1},{18,2},{19,3},{20,4},{21,5},{22,6},{23,7},{24,8},{25... | collective-permute-start | bytes 36872 | tf_op jit(solution)/shard_map/ppermute | solution.py:547
  52.1 10.8 %collective-permute-start.6 = (bf16[144,128]{1,0:T(8,128)(2,1)S(1)}, bf16[144,128]{1,0:T(8,128)(2,1)S(1)}, u32[]{:S(2)}, u32[]{:S(2)}) collective-permute-start(bf16[144,128]{1,0:T(8,128)(2,1)S(1)} %pad_maximum_fusion.other_ref), channel_id=1, source_target_pairs={{80,0},{81,1},{82,2},{83,3},{84,4},{85,5},{86,6},{87,7},{88,8},{89... | collective-permute-start | bytes 110600 | tf_op jit(solution)/shard_map/ppermute | solution.py:547
  52.5 10.4 %collective-permute-start.7 = (bf16[96,128]{1,0:T(8,128)(2,1)S(1)}, bf16[96,128]{1,0:T(8,128)(2,1)S(1)}, u32[]{:S(2)}, u32[]{:S(2)}) collective-permute-start(bf16[96,128]{1,0:T(8,128)(2,1)S(1)} %pad_maximum_fusion.1), channel_id=1, source_target_pairs={{32,0},{33,1},{34,2},{35,3},{36,4},{37,5},{38,6},{39,7},{40,8},{41... | collective-permute-start | bytes 73736 | tf_op jit(solution)/shard_map/ppermute | solution.py:547
  55.4 39.3 %all-to-all-start.1 = ((bf16[128,32,128]{2,1,0:T(8,128)(2,1)}), bf16[128,32,128]{2,1,0:T(8,128)(2,1)S(1)}, u32[]{:S(2)}, u32[]{:S(2)}) async-start(bf16[128,32,128]{2,1,0:T(8,128)(2,1)} %bitcast.10), calls=%async_computation.1 | async-start | bytes 2097152 | tf_op jit(solution)/shard_map/all_to_all | solution.py:555
  63.0 7.5 %collective-permute-start.8 = (bf16[384,128]{1,0:T(8,128)(2,1)S(1)}, bf16[384,128]{1,0:T(8,128)(2,1)S(1)}, u32[]{:S(2)}, u32[]{:S(2)}) collective-permute-start(bf16[384,128]{1,0:T(8,128)(2,1)S(1)} %get-tuple-element.28), channel_id=1, source_target_pairs={{0,2},{1,3},{2,0},{3,1},{4,6},{5,7},{6,4},{7,5},{8,10},{9,11},{10,... | collective-permute-start | bytes 294920 | tf_op jit(solution)/shard_map/ppermute | solution.py:542
  70.5 18.9 %collective-permute-start.11 = (bf16[768,128]{1,0:T(8,128)(2,1)S(1)}, bf16[768,128]{1,0:T(8,128)(2,1)S(1)}, u32[]{:S(2)}, u32[]{:S(2)}) collective-permute-start(bf16[768,128]{1,0:T(8,128)(2,1)S(1)} %constant_dynamic-update-slice_fusion.5.refs_0_), channel_id=1, source_target_pairs={{0,12},{1,13},{2,14},{3,15},{4,8},{5,9},{6,10},{7,11},{8,4},{9,5},... | collective-permute-start | bytes 589832 | tf_op jit(solution)/shard_map/ppermute | solution.py:542
  73.8 15.6 %collective-permute-start.10 = (bf16[768,128]{1,0:T(8,128)(2,1)S(1)}, bf16[768,128]{1,0:T(8,128)(2,1)S(1)}, u32[]{:S(2)}, u32[]{:S(2)}) collective-permute-start(bf16[768,128]{1,0:T(8,128)(2,1)S(1)} %constant_dynamic-update-slice_fusion.5.refs_0_), channel_id=1, source_target_pairs={{0,8},{1,9},{2,10},{3,11},{4,12},{5,13},{6,14},{7,15},{8,0},{9,1},... | collective-permute-start | bytes 589832 | tf_op jit(solution)/shard_map/ppermute | solution.py:542
  74.3 16.3 %collective-permute-start.9 = (bf16[768,128]{1,0:T(8,128)(2,1)S(1)}, bf16[768,128]{1,0:T(8,128)(2,1)S(1)}, u32[]{:S(2)}, u32[]{:S(2)}) collective-permute-start(bf16[768,128]{1,0:T(8,128)(2,1)S(1)} %constant_dynamic-update-slice_fusion.5.refs_0_), channel_id=1, source_target_pairs={{0,4},{1,5},{2,6},{3,7},{4,0},{5,1},{6,2},{7,3},{8,12},{9,13},{10,... | collective-permute-start | bytes 589832 | tf_op jit(solution)/shard_map/ppermute | solution.py:542
  90.9 6.3 %collective-permute-start.12 = (bf16[1536,256]{1,0:T(8,128)(2,1)S(1)}, bf16[1536,256]{1,0:T(8,128)(2,1)S(1)}, u32[]{:S(2)}, u32[]{:S(2)}) collective-permute-start(bf16[1536,256]{1,0:T(8,128)(2,1)S(1)} %shard_map.141.own_ref), channel_id=1, source_target_pairs={{0,1},{1,0},{2,3},{3,2},{4,5},{5,4},{6,7},{7,6},{8,9},{9,8},{10,11... | collective-permute-start | bytes 2359304 | tf_op jit(solution)/shard_map/ppermute | solution.py:542
  94.6 2.6 %copy-start.6 = (f32[3,512]{1,0:T(4,128)S(1)}, f32[3,512]{1,0:T(4,128)}, u32[]{:S(2)}) copy-start(f32[3,512]{1,0:T(4,128)} %bias_ref.1) | copy-start | bytes 18436
  94.6 2.6 %copy-start.7 = (f32[512]{0:T(512)S(1)}, f32[512]{0:T(512)}, u32[]{:S(2)}) copy-start(f32[512]{0:T(512)} %param.21) | copy-start | bytes 6148

commit v8 on v7

--- a/solution.py
+++ b/solution.py
@@ -8,6 +8,7 @@
 ROW_SHRINK = 0.25
 DENSE_SHRINK = 0.05
 CAP = 32
+FIRST = 96
 LANES = 128
 SHARDS = 128
 ROLES = 2
@@ -384,7 +385,7 @@
     )(sums, other, state, trained, squares, answers)
 
 
-def answer_body(asked_ref, table_ref, answer_ref, columns, folded):
+def columns_of(asked_ref, columns):
     digits = asked_ref[...]
     wide = jnp.concatenate(
         [
@@ -394,13 +395,50 @@
         axis=1,
     )
     columns[...] = jnp.transpose(wide)[:CAP, :].astype(jnp.int32)
+
+
+def answer_body(asked_ref, table_ref, answer_ref, columns, folded):
+    columns_of(asked_ref, columns)
     fold(table_ref, folded)
+    answer_some(columns, folded, answer_ref, 0, FIRST, 0)
+
+
+def answer_some(columns, folded, out_ref, first, last, offset):
     group = 8
-    for at in range(0, SHARDS, group):
+    for at in range(first, last, group):
         asked = jnp.concatenate(
             [columns[:, shard : shard + 1] for shard in range(at, at + group)], axis=0
         )
-        answer_ref[at * CAP : (at + group) * CAP, :] = looked_up(asked, folded[...])
+        out_ref[at * CAP - offset : (at + group) * CAP - offset, :] = looked_up(asked, folded[...])
+
+
+def answer_rest_body(asked_ref, table_ref, early_ref, late_ref, answer_ref, columns, folded, rest, written):
+    del early_ref, late_ref
+    columns_of(asked_ref, columns)
+    fold(table_ref, folded)
+    answer_some(columns, folded, rest, FIRST, SHARDS, FIRST * CAP)
+    copy = pltpu.make_async_copy(
+        rest, answer_ref.at[pl.ds(FIRST * CAP, (SHARDS - FIRST) * CAP)], written
+    )
+    copy.start()
+    copy.wait()
+
+
+def answer_rest(asked, table, answers, late):
+    rows, width = table.shape
+    return kernel_call(
+        answer_rest_body,
+        jax.ShapeDtypeStruct(answers.shape, answers.dtype),
+        in_specs=[VMEM, VMEM, ANY, ANY],
+        out_specs=ANY,
+        input_output_aliases={2: 0},
+        scratch_shapes=[
+            pltpu.VMEM((CAP, SHARDS), jnp.int32),
+            pltpu.VMEM((rows // 2, 2 * width), jnp.bfloat16),
+            pltpu.VMEM(((SHARDS - FIRST) * CAP, width), jnp.bfloat16),
+            pltpu.SemaphoreType.DMA,
+        ],
+    )(asked, table, answers, late)
 
 
 def answer_rows(asked, table):
@@ -605,7 +643,7 @@
         ],
         axis=0,
     )
-    answers = after(answers, three)
+    answers = after(answer_rest(asked, lookup, answers, piece), three)
     answered = exchange(answers.reshape(SHARDS, CAP, LANES))
     pieces = jnp.concatenate([pieces, swapped(pieces, X_BIT)], axis=0)
     tiles = collect(

time: 101 us -> 101 us (level)
  waiting for transfers between devices: 38.8 us -> 37.1 us
  Pallas kernels: 18.4 us -> 19.6 us
    all_to_all x2, starting transfers between devices: 22.4 us -> 24.5 us  [exchange(): lax.all_to_all(value, 'shard', split_axis=0, concat_axis=0, tiled=True)]
    pallas_call x0 -> x1, Pallas kernels: none -> 1.82 us  [answer_rest(): kernel_call(answer_rest_body, jax.ShapeDtypeStruct(answers.shape, answers...]
    ppermute x4, waiting for transfers between devices: 1.67 us -> 0.01 us  [from_ahead(): lax.ppermute(value, 'shard', [((source + steps * span) % SHARDS, source)...]
    ppermute x4, starting transfers between devices: 6.57 us -> 5.35 us  [from_ahead(): lax.ppermute(value, 'shard', [((source + steps * span) % SHARDS, source)...]
  transfers between devices with their start and end apart: 15 -> 15, of which waited for: 7 -> 6; matrix products, arithmetic and copies ran while one was open for 0% -> 0% of each run, Pallas kernels for 15% -> 16%
where the time goes in v8:
time: 101 us; the launch traced here: 99.6 us
  starting transfers between devices  41.1 us (41%)
  waiting for transfers between devices  37.1 us (37%)
  Pallas kernels  19.6 us (19%)
  between operations  1.56 us (2%)
    all_to_all x2, starting transfers between devices, exchange(): lax.all_to_all(value, 'shard', split_axis=0, concat_axis=0, tiled=True)  24.5 us
    ppermute x7, waiting for transfers between devices, swapped(): lax.ppermute(value, BOTH, [(source, source ^ bits) for source in range(co...  20.7 us
    all_to_all x2, waiting for transfers between devices, exchange(): lax.all_to_all(value, 'shard', split_axis=0, concat_axis=0, tiled=True)  9.19 us
    ppermute x7, starting transfers between devices, swapped(): lax.ppermute(value, BOTH, [(source, source ^ bits) for source in range(co...  8.67 us
    ppermute x1, waiting for transfers between devices, on_device(): arrived = lax.ppermute(fresh, 'role', [(0, 1)])  7.22 us
    ppermute x4, starting transfers between devices, from_ahead(): lax.ppermute(value, 'shard', [((source + steps * span) % SHARDS, source)...  5.35 us
    pallas_call x1, Pallas kernels, train_rows(): kernel_call(train_body, (jax.ShapeDtypeStruct((rows, width), jnp.float32)...  3.77 us
    pallas_call x1, Pallas kernels, answer_rows(): kernel_call(answer_body, jax.ShapeDtypeStruct((SHARDS * CAP, width), jnp....  3.26 us
  transfers between devices with their start and end apart: 15, of which 6 were waited for; matrix products, arithmetic and copies ran while one was open for 0% of the time, Pallas kernels for 16%

profile of v8, /device:TPU:2, one launch (start us, length us, event | category | flops | bytes accessed | tf_op | source)
XLA Modules:
  0.0 99.6 jit_solution(16917587788495054056)
XLA Ops:
  0.6 1.2 %shard_map.134 = f32[2,32,24,128]{3,2,1,0:T(8,128)S(1)} custom-call(f32[32,2,24,512]{3,2,1,0:T(8,128)} %bitcast.23), custom_call_target="tpu_custom_call" | custom-call | tf_op jit(solution)/shard_map/pallas_call | solution.py:85
  1.9 2.2 %shard_map.133 = (s32[8,512]{1,0:T(8,128)S(1)}, f32[128,128]{1,0:T(8,128)S(1)}, f32[2,32,24,128]{3,2,1,0:T(8,128)S(1)}, f32[2,2,24,128]{3,2,1,0:T(8,128)S(1)}, f32[2,2,24,128]{3,2,1,0:T(8,128)S(1)}) custom-call(s32[4,512]{1,0:T(4,128)S(1)} %bitcast.18, s32[4,512]{1,0:T(4,128)S(1)} %bitcast.19, f32[32,2,24,512]{3,2,1,0:T(8,128)} %bitcast.24, ...), custom_call_target="tpu_custom_call" | custom-call | tf_op jit(solution)/shard_map/pallas_call | solution.py:152
  4.2 0.9 shard_map.135
  5.1 14.9 %all-to-all-start = ((bf16[128,16,128]{2,1,0:T(8,128)(2,1)}), bf16[128,16,128]{2,1,0:T(8,128)(2,1)S(1)}, u32[]{:S(2)}, u32[]{:S(2)}) async-start(bf16[128,16,128]{2,1,0:T(8,128)(2,1)} %shard_map.135), calls=%async_computation | async-start | bytes 1048576 | tf_op jit(solution)/shard_map/all_to_all | solution.py:593
  20.7 3.8 %shard_map.131 = (f32[2048,128]{1,0:T(8,128)S(1)}, bf16[2048,128]{1,0:T(8,128)(2,1)S(1)}, bf16[512,128]{1,0:T(8,128)(2,1)S(1)}) custom-call(s32[1]{0:T(128)S(6)} %copy.27.count_ref, s32[1,512]{1,0:T(1,128)S(1)} %bitcast.20, f32[2048,128]{1,0:T(8,128)S(1)} %bitcast.15, f32[2048,128]{1,0:T(8,128)S(1)} %copy-done.1, f32[512,128]{1,0:T(8,128)S(1)} %copy-done.2), custom_call_target="tpu_custom_call" | custom-call | tf_op jit(solution)/shard_map/pallas_call | solution.py:260
  24.5 1.3 %collective-permute-start = (bf16[512,128]{1,0:T(8,128)(2,1)S(1)}, bf16[512,128]{1,0:T(8,128)(2,1)S(1)}, u32[]{:S(2)}, u32[]{:S(2)}) collective-permute-start(bf16[512,128]{1,0:T(8,128)(2,1)S(1)} %get-tuple-element.14), channel_id=1, source_target_pairs={{0,128},{1,129},{2,130},{3,131},{4,132},{5,133},{6,134},{7,135},{8... | collective-permute-start | bytes 393224 | tf_op jit(solution)/shard_map/ppermute | solution.py:627
  25.8 1.3 %collective-permute-start.3 = (f32[2,2,24,128]{3,2,1,0:T(8,128)S(1)}, f32[2,2,24,128]{3,2,1,0:T(8,128)S(1)}, u32[]{:S(2)}, u32[]{:S(2)}) collective-permute-start(f32[2,2,24,128]{3,2,1,0:T(8,128)S(1)} %get-tuple-element.24.state_ref), channel_id=1, source_target_pairs={{0,128},{1,129},{2,130},{3,131},{4,132},{5,133},{6,134},{7,135},{8... | collective-permute-start | bytes 147464 | tf_op jit(solution)/shard_map/ppermute | solution.py:621
  27.1 7.2 %collective-permute-done.arrived_ref = bf16[512,128]{1,0:T(8,128)(2,1)S(1)} collective-permute-done((bf16[512,128]{1,0:T(8,128)(2,1)S(1)}, bf16[512,128]{1,0:T(8,128)(2,1)S(1)}, u32[]{:S(2)}, u32[]{:S(2)}) %collective-permute-start) | collective-permute-done | bytes 131104 | tf_op jit(solution)/shard_map/ppermute | solution.py:627
  34.3 1.7 %shard_map.132 = (f32[2048,128]{1,0:T(8,128)}, bf16[2048,128]{1,0:T(8,128)(2,1)S(1)}) custom-call(s32[1]{0:T(128)S(6)} %copy.27.count_ref, s32[1,512]{1,0:T(1,128)S(1)} %bitcast.21, bf16[512,128]{1,0:T(8,128)(2,1)S(1)} %collective-permute-done.arrived_ref, f32[2048,128]{1,0:T(8,128)S(1)} %bitcast.16, f32[2048,128]{1,0:T(8,128)S(1)} %get-tuple-element.15.new_ref, ...), custom_call_target="tpu_custom_call" | custom-call | tf_op jit(solution)/shard_map/pallas_call | solution.py:316
  36.0 5.5 %all-to-all-done.packed_ref = bf16[128,16,128]{2,1,0:T(8,128)(2,1)S(1)} async-done(((bf16[128,16,128]{2,1,0:T(8,128)(2,1)}), bf16[128,16,128]{2,1,0:T(8,128)(2,1)S(1)}, u32[]{:S(2)}, u32[]{:S(2)}) %all-to-all-start) | async-done | bytes 524320 | tf_op jit(solution)/shard_map/all_to_all | solution.py:593
  41.7 1.5 %collective-permute-start.2 = (f32[2,16,128]{2,1,0:T(8,128)S(1)}, f32[2,16,128]{2,1,0:T(8,128)S(1)}, u32[]{:S(2)}, u32[]{:S(2)}) collective-permute-start(f32[2,16,128]{2,1,0:T(8,128)S(1)} %get-tuple-element.23.sum_ref), channel_id=1, source_target_pairs={{0,128},{1,129},{2,130},{3,131},{4,132},{5,133},{6,134},{7,135},{8... | collective-permute-start | bytes 49160 | tf_op jit(solution)/shard_map/ppermute | solution.py:580
  43.2 3.3 %shard_map.137.answer_ref.early_ref = bf16[4096,128]{1,0:T(8,128)(2,1)} custom-call(f32[128,128]{1,0:T(8,128)S(1)} %get-tuple-element.22.asked_ref, bf16[2048,128]{1,0:T(8,128)(2,1)S(1)} %get-tuple-element.21.lookup_ref.table_ref), custom_call_target="tpu_custom_call" | custom-call | tf_op jit(solution)/shard_map/pallas_call | solution.py:446
  47.4 2.4 %collective-permute-start.4 = (bf16[48,128]{1,0:T(8,128)(2,1)S(1)}, bf16[48,128]{1,0:T(8,128)(2,1)S(1)}, u32[]{:S(2)}, u32[]{:S(2)}) collective-permute-start(bf16[48,128]{1,0:T(8,128)(2,1)S(1)} %shard_map.138.late_ref), channel_id=1, source_target_pairs={{16,0},{17,1},{18,2},{19,3},{20,4},{21,5},{22,6},{23,7},{24,8},{25... | collective-permute-start | bytes 36872 | tf_op jit(solution)/shard_map/ppermute | solution.py:585
  49.9 1.8 %shard_map.139.value_ref = bf16[4096,128]{1,0:T(8,128)(2,1)} custom-call(f32[128,128]{1,0:T(8,128)S(1)} %get-tuple-element.22.asked_ref, bf16[2048,128]{1,0:T(8,128)(2,1)S(1)} %get-tuple-element.21.lookup_ref.table_ref, bf16[4096,128]{1,0:T(8,128)(2,1)} %shard_map.137.answer_ref.early_ref, ...), custom_call_target="tpu_custom_call", output_to_operand_aliasing={{}: (2, {})} | custom-call | tf_op jit(solution)/shard_map/pallas_call | solution.py:429
  51.7 1.3 %collective-permute-start.7 = (bf16[96,128]{1,0:T(8,128)(2,1)S(1)}, bf16[96,128]{1,0:T(8,128)(2,1)S(1)}, u32[]{:S(2)}, u32[]{:S(2)}) collective-permute-start(bf16[96,128]{1,0:T(8,128)(2,1)S(1)} %pad_maximum_fusion.1), channel_id=1, source_target_pairs={{32,0},{33,1},{34,2},{35,3},{36,4},{37,5},{38,6},{39,7},{40,8},{41... | collective-permute-start | bytes 73736 | tf_op jit(solution)/shard_map/ppermute | solution.py:585
  53.8 9.6 %all-to-all-start.1 = ((bf16[128,32,128]{2,1,0:T(8,128)(2,1)}), bf16[128,32,128]{2,1,0:T(8,128)(2,1)S(1)}, u32[]{:S(2)}, u32[]{:S(2)}) async-start(bf16[128,32,128]{2,1,0:T(8,128)(2,1)} %bitcast.10), calls=%async_computation.1 | async-start | bytes 2097152 | tf_op jit(solution)/shard_map/all_to_all | solution.py:593
  63.4 2.7 %collective-permute-start.8 = (bf16[384,128]{1,0:T(8,128)(2,1)S(1)}, bf16[384,128]{1,0:T(8,128)(2,1)S(1)}, u32[]{:S(2)}, u32[]{:S(2)}) collective-permute-start(bf16[384,128]{1,0:T(8,128)(2,1)S(1)} %get-tuple-element.28), channel_id=1, source_target_pairs={{0,2},{1,3},{2,0},{3,1},{4,6},{5,7},{6,4},{7,5},{8,10},{9,11},{10,... | collective-permute-start | bytes 294920 | tf_op jit(solution)/shard_map/ppermute | solution.py:580
  66.1 4.8 %collective-permute-done.8 = bf16[384,128]{1,0:T(8,128)(2,1)S(1)} collective-permute-done((bf16[384,128]{1,0:T(8,128)(2,1)S(1)}, bf16[384,128]{1,0:T(8,128)(2,1)S(1)}, u32[]{:S(2)}, u32[]{:S(2)}) %collective-permute-start.8) | collective-permute-done | bytes 98336 | tf_op jit(solution)/shard_map/ppermute | solution.py:580
  70.9 3.3 %collective-permute-start.11 = (bf16[768,128]{1,0:T(8,128)(2,1)S(1)}, bf16[768,128]{1,0:T(8,128)(2,1)S(1)}, u32[]{:S(2)}, u32[]{:S(2)}) collective-permute-start(bf16[768,128]{1,0:T(8,128)(2,1)S(1)} %constant_dynamic-update-slice_fusion.5.refs_0_), channel_id=1, source_target_pairs={{0,12},{1,13},{2,14},{3,15},{4,8},{5,9},{6,10},{7,11},{8,4},{9,5},... | collective-permute-start | bytes 589832 | tf_op jit(solution)/shard_map/ppermute | solution.py:580
  75.2 14.6 %collective-permute-done.11.refs_3_ = bf16[768,128]{1,0:T(8,128)(2,1)S(1)} collective-permute-done((bf16[768,128]{1,0:T(8,128)(2,1)S(1)}, bf16[768,128]{1,0:T(8,128)(2,1)S(1)}, u32[]{:S(2)}, u32[]{:S(2)}) %collective-permute-start.11) | collective-permute-done | bytes 196640 | tf_op jit(solution)/shard_map/ppermute | solution.py:580
  89.8 1.3 %collective-permute-done.9.refs_1_ = bf16[768,128]{1,0:T(8,128)(2,1)S(1)} collective-permute-done((bf16[768,128]{1,0:T(8,128)(2,1)S(1)}, bf16[768,128]{1,0:T(8,128)(2,1)S(1)}, u32[]{:S(2)}, u32[]{:S(2)}) %collective-permute-start.9) | collective-permute-done | bytes 196640 | tf_op jit(solution)/shard_map/ppermute | solution.py:580
  91.5 3.6 %all-to-all-done.1 = bf16[128,32,128]{2,1,0:T(8,128)(2,1)S(1)} async-done(((bf16[128,32,128]{2,1,0:T(8,128)(2,1)}), bf16[128,32,128]{2,1,0:T(8,128)(2,1)S(1)}, u32[]{:S(2)}, u32[]{:S(2)}) %all-to-all-start.1) | async-done | bytes 1048608 | tf_op jit(solution)/shard_map/all_to_all | solution.py:593
  95.1 2.6 %shard_map.141.base_ref = bf16[512,512]{1,0:T(8,128)(2,1)S(1)} custom-call(s32[8,512]{1,0:T(8,128)S(1)} %get-tuple-element.18.place_ref, bf16[4096,128]{1,0:T(8,128)(2,1)S(1)} %bitcast.17), custom_call_target="tpu_custom_call" | custom-call | flops 2147483648 | bytes 2000000 | tf_op jit(solution)/shard_map/pallas_call | solution.py:522
  97.7 1.8 %shard_map.143 = f32[1,512]{1,0:T(1,128)} custom-call(bf16[512,512]{1,0:T(8,128)(2,1)S(1)} %shard_map.141.base_ref, f32[3,512]{1,0:T(4,128)S(1)} %copy-done.6, f32[1,512]{1,0:T(1,128)S(1)} %bitcast.22, bf16[1536,256]{1,0:T(8,128)(2,1)S(1)} %shard_map.142.own_ref, bf16[1536,256]{1,0:T(8,128)(2,1)S(1)} %collective-permute-done.12.other_ref), custom_call_target="tpu_custom_call" | custom-call | flops 805306368 | bytes 3000000 | tf_op jit(solution)/shard_map/pallas_call | solution.py:564
  (43 shorter events, 3.4 us)
Async XLA Ops:
  0.6 1.3 %copy-start.4 = (s32[1,512,4]{1,2,0:T(4,128)S(1)}, s32[1,512,4]{1,2,0:T(4,128)}, u32[]{:S(2)}) copy-start(s32[1,512,4]{1,2,0:T(4,128)} %param.23) | copy-start | bytes 24580
  0.6 1.3 %copy-start.3 = (s32[1,512,4]{1,2,0:T(4,128)S(1)}, s32[1,512,4]{1,2,0:T(4,128)}, u32[]{:S(2)}) copy-start(s32[1,512,4]{1,2,0:T(4,128)} %param.22) | copy-start | bytes 24580
  1.8 2.4 %collective-permute-start.1 = (f32[2,32,24,128]{3,2,1,0:T(8,128)S(1)}, f32[2,32,24,128]{3,2,1,0:T(8,128)S(1)}, u32[]{:S(2)}, u32[]{:S(2)}) collective-permute-start(f32[2,32,24,128]{3,2,1,0:T(8,128)S(1)} %shard_map.134), channel_id=1, source_target_pairs={{0,1},{1,0},{2,3},{3,2},{4,5},{5,4},{6,7},{7,6},{8,9},{9,8},{10,11... | collective-permute-start | bytes 2359304 | tf_op jit(solution)/shard_map/ppermute | solution.py:580
  4.1 16.6 %copy-start = (f32[1,2048,128]{2,1,0:T(8,128)S(1)}, f32[1,2048,128]{2,1,0:T(8,128)}, u32[]{:S(2)}) copy-start(f32[1,2048,128]{2,1,0:T(8,128)} %param.12) | copy-start | bytes 3145732
  4.1 16.6 %copy-start.1 = (f32[2048,128]{1,0:T(8,128)S(1)}, f32[2048,128]{1,0:T(8,128)}, u32[]{:S(2)}) copy-start(f32[2048,128]{1,0:T(8,128)} %square_ref.1) | copy-start | bytes 3145732
  4.1 16.6 %copy-start.2 = (f32[512,128]{1,0:T(8,128)S(1)}, f32[512,128]{1,0:T(8,128)}, u32[]{:S(2)}) copy-start(f32[512,128]{1,0:T(8,128)} %grad_ref.1) | copy-start | bytes 786436
  4.1 16.6 %copy-start.5 = (s32[512]{0:T(512)S(1)}, s32[512]{0:T(512)}, u32[]{:S(2)}) copy-start(s32[512]{0:T(512)} %param.14) | copy-start | bytes 6148
  5.1 36.5 %all-to-all-start = ((bf16[128,16,128]{2,1,0:T(8,128)(2,1)}), bf16[128,16,128]{2,1,0:T(8,128)(2,1)S(1)}, u32[]{:S(2)}, u32[]{:S(2)}) async-start(bf16[128,16,128]{2,1,0:T(8,128)(2,1)} %shard_map.135), calls=%async_computation | async-start | bytes 1048576 | tf_op jit(solution)/shard_map/all_to_all | solution.py:593
  24.5 9.8 %collective-permute-start = (bf16[512,128]{1,0:T(8,128)(2,1)S(1)}, bf16[512,128]{1,0:T(8,128)(2,1)S(1)}, u32[]{:S(2)}, u32[]{:S(2)}) collective-permute-start(bf16[512,128]{1,0:T(8,128)(2,1)S(1)} %get-tuple-element.14), channel_id=1, source_target_pairs={{0,128},{1,129},{2,130},{3,131},{4,132},{5,133},{6,134},{7,135},{8... | collective-permute-start | bytes 393224 | tf_op jit(solution)/shard_map/ppermute | solution.py:627
  25.8 20.6 %collective-permute-start.3 = (f32[2,2,24,128]{3,2,1,0:T(8,128)S(1)}, f32[2,2,24,128]{3,2,1,0:T(8,128)S(1)}, u32[]{:S(2)}, u32[]{:S(2)}) collective-permute-start(f32[2,2,24,128]{3,2,1,0:T(8,128)S(1)} %get-tuple-element.24.state_ref), channel_id=1, source_target_pairs={{0,128},{1,129},{2,130},{3,131},{4,132},{5,133},{6,134},{7,135},{8... | collective-permute-start | bytes 147464 | tf_op jit(solution)/shard_map/ppermute | solution.py:621
  41.7 4.8 %collective-permute-start.2 = (f32[2,16,128]{2,1,0:T(8,128)S(1)}, f32[2,16,128]{2,1,0:T(8,128)S(1)}, u32[]{:S(2)}, u32[]{:S(2)}) collective-permute-start(f32[2,16,128]{2,1,0:T(8,128)S(1)} %get-tuple-element.23.sum_ref), channel_id=1, source_target_pairs={{0,128},{1,129},{2,130},{3,131},{4,132},{5,133},{6,134},{7,135},{8... | collective-permute-start | bytes 49160 | tf_op jit(solution)/shard_map/ppermute | solution.py:580
  46.5 6.5 %collective-permute-start.5 = (bf16[48,128]{1,0:T(8,128)(2,1)S(1)}, bf16[48,128]{1,0:T(8,128)(2,1)S(1)}, u32[]{:S(2)}, u32[]{:S(2)}) collective-permute-start(bf16[48,128]{1,0:T(8,128)(2,1)S(1)} %shard_map.138.late_ref), channel_id=1, source_target_pairs={{112,0},{113,1},{114,2},{115,3},{116,4},{117,5},{118,6},{119,7},{1... | collective-permute-start | bytes 36872 | tf_op jit(solution)/shard_map/ppermute | solution.py:585
  47.4 4.3 %collective-permute-start.4 = (bf16[48,128]{1,0:T(8,128)(2,1)S(1)}, bf16[48,128]{1,0:T(8,128)(2,1)S(1)}, u32[]{:S(2)}, u32[]{:S(2)}) collective-permute-start(bf16[48,128]{1,0:T(8,128)(2,1)S(1)} %shard_map.138.late_ref), channel_id=1, source_target_pairs={{16,0},{17,1},{18,2},{19,3},{20,4},{21,5},{22,6},{23,7},{24,8},{25... | collective-permute-start | bytes 36872 | tf_op jit(solution)/shard_map/ppermute | solution.py:585
  51.7 11.7 %collective-permute-start.7 = (bf16[96,128]{1,0:T(8,128)(2,1)S(1)}, bf16[96,128]{1,0:T(8,128)(2,1)S(1)}, u32[]{:S(2)}, u32[]{:S(2)}) collective-permute-start(bf16[96,128]{1,0:T(8,128)(2,1)S(1)} %pad_maximum_fusion.1), channel_id=1, source_target_pairs={{32,0},{33,1},{34,2},{35,3},{36,4},{37,5},{38,6},{39,7},{40,8},{41... | collective-permute-start | bytes 73736 | tf_op jit(solution)/shard_map/ppermute | solution.py:585
  53.0 10.4 %collective-permute-start.6 = (bf16[144,128]{1,0:T(8,128)(2,1)S(1)}, bf16[144,128]{1,0:T(8,128)(2,1)S(1)}, u32[]{:S(2)}, u32[]{:S(2)}) collective-permute-start(bf16[144,128]{1,0:T(8,128)(2,1)S(1)} %pad_maximum_fusion.other_ref), channel_id=1, source_target_pairs={{80,0},{81,1},{82,2},{83,3},{84,4},{85,5},{86,6},{87,7},{88,8},{89... | collective-permute-start | bytes 110600 | tf_op jit(solution)/shard_map/ppermute | solution.py:585
  53.8 41.3 %all-to-all-start.1 = ((bf16[128,32,128]{2,1,0:T(8,128)(2,1)}), bf16[128,32,128]{2,1,0:T(8,128)(2,1)S(1)}, u32[]{:S(2)}, u32[]{:S(2)}) async-start(bf16[128,32,128]{2,1,0:T(8,128)(2,1)} %bitcast.10), calls=%async_computation.1 | async-start | bytes 2097152 | tf_op jit(solution)/shard_map/all_to_all | solution.py:593
  63.4 7.5 %collective-permute-start.8 = (bf16[384,128]{1,0:T(8,128)(2,1)S(1)}, bf16[384,128]{1,0:T(8,128)(2,1)S(1)}, u32[]{:S(2)}, u32[]{:S(2)}) collective-permute-start(bf16[384,128]{1,0:T(8,128)(2,1)S(1)} %get-tuple-element.28), channel_id=1, source_target_pairs={{0,2},{1,3},{2,0},{3,1},{4,6},{5,7},{6,4},{7,5},{8,10},{9,11},{10,... | collective-permute-start | bytes 294920 | tf_op jit(solution)/shard_map/ppermute | solution.py:580
  70.9 18.9 %collective-permute-start.11 = (bf16[768,128]{1,0:T(8,128)(2,1)S(1)}, bf16[768,128]{1,0:T(8,128)(2,1)S(1)}, u32[]{:S(2)}, u32[]{:S(2)}) collective-permute-start(bf16[768,128]{1,0:T(8,128)(2,1)S(1)} %constant_dynamic-update-slice_fusion.5.refs_0_), channel_id=1, source_target_pairs={{0,12},{1,13},{2,14},{3,15},{4,8},{5,9},{6,10},{7,11},{8,4},{9,5},... | collective-permute-start | bytes 589832 | tf_op jit(solution)/shard_map/ppermute | solution.py:580
  74.2 15.6 %collective-permute-start.10 = (bf16[768,128]{1,0:T(8,128)(2,1)S(1)}, bf16[768,128]{1,0:T(8,128)(2,1)S(1)}, u32[]{:S(2)}, u32[]{:S(2)}) collective-permute-start(bf16[768,128]{1,0:T(8,128)(2,1)S(1)} %constant_dynamic-update-slice_fusion.5.refs_0_), channel_id=1, source_target_pairs={{0,8},{1,9},{2,10},{3,11},{4,12},{5,13},{6,14},{7,15},{8,0},{9,1},... | collective-permute-start | bytes 589832 | tf_op jit(solution)/shard_map/ppermute | solution.py:580
  74.8 16.3 %collective-permute-start.9 = (bf16[768,128]{1,0:T(8,128)(2,1)S(1)}, bf16[768,128]{1,0:T(8,128)(2,1)S(1)}, u32[]{:S(2)}, u32[]{:S(2)}) collective-permute-start(bf16[768,128]{1,0:T(8,128)(2,1)S(1)} %constant_dynamic-update-slice_fusion.5.refs_0_), channel_id=1, source_target_pairs={{0,4},{1,5},{2,6},{3,7},{4,0},{5,1},{6,2},{7,3},{8,12},{9,13},{10,... | collective-permute-start | bytes 589832 | tf_op jit(solution)/shard_map/ppermute | solution.py:580
  91.4 6.3 %collective-permute-start.12 = (bf16[1536,256]{1,0:T(8,128)(2,1)S(1)}, bf16[1536,256]{1,0:T(8,128)(2,1)S(1)}, u32[]{:S(2)}, u32[]{:S(2)}) collective-permute-start(bf16[1536,256]{1,0:T(8,128)(2,1)S(1)} %shard_map.142.own_ref), channel_id=1, source_target_pairs={{0,1},{1,0},{2,3},{3,2},{4,5},{5,4},{6,7},{7,6},{8,9},{9,8},{10,11... | collective-permute-start | bytes 2359304 | tf_op jit(solution)/shard_map/ppermute | solution.py:580
  95.1 2.6 %copy-start.6 = (f32[3,512]{1,0:T(4,128)S(1)}, f32[3,512]{1,0:T(4,128)}, u32[]{:S(2)}) copy-start(f32[3,512]{1,0:T(4,128)} %bias_ref.1) | copy-start | bytes 18436
  95.1 2.6 %copy-start.7 = (f32[512]{0:T(512)S(1)}, f32[512]{0:T(512)}, u32[]{:S(2)}) copy-start(f32[512]{0:T(512)} %param.21) | copy-start | bytes 6148

commit v9 on v8

--- a/solution.py
+++ b/solution.py
@@ -559,16 +559,28 @@
     score_ref[...] = jnp.transpose(jnp.broadcast_to(scores, (scores.shape[0], LANES)))[:1, :]
 
 
-def cross_scores(base, bias, out_weight, own, other):
-    examples, width = base.shape
-    return kernel_call(
-        cross_body,
+def score_body(place_ref, answer_ref, bias_ref, out_ref, own_ref, other_ref, score_ref, columns, folded, base):
+    arrange_body(place_ref, answer_ref, base, columns, folded)
+    cross_body(base, bias_ref, out_ref, own_ref, other_ref, score_ref)
+
+
+def score(places, answers, bias, out_weight, own, other):
+    examples = places.shape[1]
+    rows, lanes = answers.shape
+    width = out_weight.shape[1]
+    return kernel_call(
+        score_body,
         jax.ShapeDtypeStruct((1, examples), jnp.float32),
-        flops=2 * examples * width * width * bias.shape[0],
+        flops=2 * examples * width * (rows + width * bias.shape[0]),
         bytes_accessed=3_000_000,
-        in_specs=[VMEM] * 5,
+        in_specs=[VMEM] * 6,
         out_specs=VMEM,
-    )(base, bias, out_weight, own, other)
+        scratch_shapes=[
+            pltpu.VMEM((examples, 8), jnp.int32),
+            pltpu.VMEM((rows // 2, 2 * lanes), jnp.bfloat16),
+            pltpu.VMEM((examples, width), jnp.bfloat16),
+        ],
+    )(places, answers, bias, out_weight, own, other)
 
 
 BOTH = ("role", "shard")
@@ -649,9 +661,13 @@
     tiles = collect(
         [pieces] + [swapped(pieces, flip * Y_BIT) for flip in range(1, Y_SIZE)]
     )
-    base = arrange_rows(places, answered.reshape(SHARDS * CAP, LANES), fields)
-    scores = cross_scores(
-        base, cross_bias, out_weight.reshape(1, -1), tiles, swapped(tiles, CORE_BIT)
+    scores = score(
+        places,
+        answered.reshape(SHARDS * CAP, LANES),
+        cross_bias,
+        out_weight.reshape(1, -1),
+        tiles,
+        swapped(tiles, CORE_BIT),
     )
     return (table_result[None], scores)
 

time: 101 us -> 100 us (0.990)
    all_to_all x2, waiting for transfers between devices: 9.19 us -> 6.91 us  [exchange(): lax.all_to_all(value, 'shard', split_axis=0, concat_axis=0, tiled=True)]
    ppermute x7, waiting for transfers between devices: 20.7 us -> 23 us  [swapped(): lax.ppermute(value, BOTH, [(source, source ^ bits) for source in range(co...]
    pallas_call x2 -> x1, Pallas kernels: 4.42 us -> 4.26 us  [score(): kernel_call(score_body, jax.ShapeDtypeStruct((1, examples), jnp.float32),...]
  transfers between devices with their start and end apart: 15 -> 15, of which waited for: 6 -> 7; matrix products, arithmetic and copies ran while one was open for 0% -> 0% of each run, Pallas kernels for 16% -> 13%
where the time goes in v9:
time: 100 us; the launch traced here: 99.4 us
  starting transfers between devices  41.1 us (41%)
  waiting for transfers between devices  37.1 us (37%)
  Pallas kernels  19.5 us (20%)
  between operations  1.55 us (2%)
    all_to_all x2, starting transfers between devices, exchange(): lax.all_to_all(value, 'shard', split_axis=0, concat_axis=0, tiled=True)  24.5 us
    ppermute x7, waiting for transfers between devices, swapped(): lax.ppermute(value, BOTH, [(source, source ^ bits) for source in range(co...  23 us
    ppermute x7, starting transfers between devices, swapped(): lax.ppermute(value, BOTH, [(source, source ^ bits) for source in range(co...  8.67 us
    ppermute x1, waiting for transfers between devices, on_device(): arrived = lax.ppermute(fresh, 'role', [(0, 1)])  7.22 us
    all_to_all x2, waiting for transfers between devices, exchange(): lax.all_to_all(value, 'shard', split_axis=0, concat_axis=0, tiled=True)  6.91 us
    ppermute x4, starting transfers between devices, from_ahead(): lax.ppermute(value, 'shard', [((source + steps * span) % SHARDS, source)...  5.36 us
    pallas_call x1, Pallas kernels, score(): kernel_call(score_body, jax.ShapeDtypeStruct((1, examples), jnp.float32),...  4.26 us
    pallas_call x1, Pallas kernels, train_rows(): kernel_call(train_body, (jax.ShapeDtypeStruct((rows, width), jnp.float32)...  3.77 us
  transfers between devices with their start and end apart: 15, of which 7 were waited for; matrix products, arithmetic and copies ran while one was open for 0% of the time, Pallas kernels for 13%

profile of v9, /device:TPU:2, one launch (start us, length us, event | category | flops | bytes accessed | tf_op | source)
XLA Modules:
  0.0 99.4 jit_solution(3076203402422411223)
XLA Ops:
  0.6 1.2 %shard_map.134 = f32[2,32,24,128]{3,2,1,0:T(8,128)S(1)} custom-call(f32[32,2,24,512]{3,2,1,0:T(8,128)} %bitcast.23), custom_call_target="tpu_custom_call" | custom-call | tf_op jit(solution)/shard_map/pallas_call | solution.py:85
  1.9 2.2 %shard_map.133 = (s32[8,512]{1,0:T(8,128)S(1)}, f32[128,128]{1,0:T(8,128)S(1)}, f32[2,32,24,128]{3,2,1,0:T(8,128)S(1)}, f32[2,2,24,128]{3,2,1,0:T(8,128)S(1)}, f32[2,2,24,128]{3,2,1,0:T(8,128)S(1)}) custom-call(s32[4,512]{1,0:T(4,128)S(1)} %bitcast.18, s32[4,512]{1,0:T(4,128)S(1)} %bitcast.19, f32[32,2,24,512]{3,2,1,0:T(8,128)} %bitcast.24, ...), custom_call_target="tpu_custom_call" | custom-call | tf_op jit(solution)/shard_map/pallas_call | solution.py:152
  4.2 0.9 shard_map.135
  5.1 14.9 %all-to-all-start = ((bf16[128,16,128]{2,1,0:T(8,128)(2,1)}), bf16[128,16,128]{2,1,0:T(8,128)(2,1)S(1)}, u32[]{:S(2)}, u32[]{:S(2)}) async-start(bf16[128,16,128]{2,1,0:T(8,128)(2,1)} %shard_map.135), calls=%async_computation | async-start | bytes 1048576 | tf_op jit(solution)/shard_map/all_to_all | solution.py:605
  20.7 3.8 %shard_map.131 = (f32[2048,128]{1,0:T(8,128)S(1)}, bf16[2048,128]{1,0:T(8,128)(2,1)S(1)}, bf16[512,128]{1,0:T(8,128)(2,1)S(1)}) custom-call(s32[1]{0:T(128)S(6)} %copy.27.count_ref, s32[1,512]{1,0:T(1,128)S(1)} %bitcast.20, f32[2048,128]{1,0:T(8,128)S(1)} %bitcast.15, f32[2048,128]{1,0:T(8,128)S(1)} %copy-done.1, f32[512,128]{1,0:T(8,128)S(1)} %copy-done.2), custom_call_target="tpu_custom_call" | custom-call | tf_op jit(solution)/shard_map/pallas_call | solution.py:260
  24.5 1.3 %collective-permute-start = (bf16[512,128]{1,0:T(8,128)(2,1)S(1)}, bf16[512,128]{1,0:T(8,128)(2,1)S(1)}, u32[]{:S(2)}, u32[]{:S(2)}) collective-permute-start(bf16[512,128]{1,0:T(8,128)(2,1)S(1)} %get-tuple-element.14), channel_id=1, source_target_pairs={{0,128},{1,129},{2,130},{3,131},{4,132},{5,133},{6,134},{7,135},{8... | collective-permute-start | bytes 393224 | tf_op jit(solution)/shard_map/ppermute | solution.py:639
  25.8 1.3 %collective-permute-start.3 = (f32[2,2,24,128]{3,2,1,0:T(8,128)S(1)}, f32[2,2,24,128]{3,2,1,0:T(8,128)S(1)}, u32[]{:S(2)}, u32[]{:S(2)}) collective-permute-start(f32[2,2,24,128]{3,2,1,0:T(8,128)S(1)} %get-tuple-element.24.state_ref), channel_id=1, source_target_pairs={{0,128},{1,129},{2,130},{3,131},{4,132},{5,133},{6,134},{7,135},{8... | collective-permute-start | bytes 147464 | tf_op jit(solution)/shard_map/ppermute | solution.py:633
  27.1 7.2 %collective-permute-done.arrived_ref = bf16[512,128]{1,0:T(8,128)(2,1)S(1)} collective-permute-done((bf16[512,128]{1,0:T(8,128)(2,1)S(1)}, bf16[512,128]{1,0:T(8,128)(2,1)S(1)}, u32[]{:S(2)}, u32[]{:S(2)}) %collective-permute-start) | collective-permute-done | bytes 131104 | tf_op jit(solution)/shard_map/ppermute | solution.py:639
  34.3 1.7 %shard_map.132 = (f32[2048,128]{1,0:T(8,128)}, bf16[2048,128]{1,0:T(8,128)(2,1)S(1)}) custom-call(s32[1]{0:T(128)S(6)} %copy.27.count_ref, s32[1,512]{1,0:T(1,128)S(1)} %bitcast.21, bf16[512,128]{1,0:T(8,128)(2,1)S(1)} %collective-permute-done.arrived_ref, f32[2048,128]{1,0:T(8,128)S(1)} %bitcast.16, f32[2048,128]{1,0:T(8,128)S(1)} %get-tuple-element.15.new_ref, ...), custom_call_target="tpu_custom_call" | custom-call | tf_op jit(solution)/shard_map/pallas_call | solution.py:316
  36.0 5.5 %all-to-all-done.packed_ref = bf16[128,16,128]{2,1,0:T(8,128)(2,1)S(1)} async-done(((bf16[128,16,128]{2,1,0:T(8,128)(2,1)}), bf16[128,16,128]{2,1,0:T(8,128)(2,1)S(1)}, u32[]{:S(2)}, u32[]{:S(2)}) %all-to-all-start) | async-done | bytes 524320 | tf_op jit(solution)/shard_map/all_to_all | solution.py:605
  41.7 1.5 %collective-permute-start.2 = (f32[2,16,128]{2,1,0:T(8,128)S(1)}, f32[2,16,128]{2,1,0:T(8,128)S(1)}, u32[]{:S(2)}, u32[]{:S(2)}) collective-permute-start(f32[2,16,128]{2,1,0:T(8,128)S(1)} %get-tuple-element.23.sum_ref), channel_id=1, source_target_pairs={{0,128},{1,129},{2,130},{3,131},{4,132},{5,133},{6,134},{7,135},{8... | collective-permute-start | bytes 49160 | tf_op jit(solution)/shard_map/ppermute | solution.py:592
  43.2 3.3 %shard_map.137.answer_ref.early_ref = bf16[4096,128]{1,0:T(8,128)(2,1)} custom-call(f32[128,128]{1,0:T(8,128)S(1)} %get-tuple-element.22.asked_ref, bf16[2048,128]{1,0:T(8,128)(2,1)S(1)} %get-tuple-element.21.lookup_ref.table_ref), custom_call_target="tpu_custom_call" | custom-call | tf_op jit(solution)/shard_map/pallas_call | solution.py:446
  47.4 2.4 %collective-permute-start.4 = (bf16[48,128]{1,0:T(8,128)(2,1)S(1)}, bf16[48,128]{1,0:T(8,128)(2,1)S(1)}, u32[]{:S(2)}, u32[]{:S(2)}) collective-permute-start(bf16[48,128]{1,0:T(8,128)(2,1)S(1)} %shard_map.138.late_ref), channel_id=1, source_target_pairs={{16,0},{17,1},{18,2},{19,3},{20,4},{21,5},{22,6},{23,7},{24,8},{25... | collective-permute-start | bytes 36872 | tf_op jit(solution)/shard_map/ppermute | solution.py:597
  49.9 1.8 %shard_map.139.value_ref = bf16[4096,128]{1,0:T(8,128)(2,1)} custom-call(f32[128,128]{1,0:T(8,128)S(1)} %get-tuple-element.22.asked_ref, bf16[2048,128]{1,0:T(8,128)(2,1)S(1)} %get-tuple-element.21.lookup_ref.table_ref, bf16[4096,128]{1,0:T(8,128)(2,1)} %shard_map.137.answer_ref.early_ref, ...), custom_call_target="tpu_custom_call", output_to_operand_aliasing={{}: (2, {})} | custom-call | tf_op jit(solution)/shard_map/pallas_call | solution.py:429
  51.7 1.3 %collective-permute-start.7 = (bf16[96,128]{1,0:T(8,128)(2,1)S(1)}, bf16[96,128]{1,0:T(8,128)(2,1)S(1)}, u32[]{:S(2)}, u32[]{:S(2)}) collective-permute-start(bf16[96,128]{1,0:T(8,128)(2,1)S(1)} %pad_maximum_fusion.1), channel_id=1, source_target_pairs={{32,0},{33,1},{34,2},{35,3},{36,4},{37,5},{38,6},{39,7},{40,8},{41... | collective-permute-start | bytes 73736 | tf_op jit(solution)/shard_map/ppermute | solution.py:597
  53.8 9.6 %all-to-all-start.1 = ((bf16[128,32,128]{2,1,0:T(8,128)(2,1)}), bf16[128,32,128]{2,1,0:T(8,128)(2,1)S(1)}, u32[]{:S(2)}, u32[]{:S(2)}) async-start(bf16[128,32,128]{2,1,0:T(8,128)(2,1)} %bitcast.10), calls=%async_computation.1 | async-start | bytes 2097152 | tf_op jit(solution)/shard_map/all_to_all | solution.py:605
  63.4 2.7 %collective-permute-start.8 = (bf16[384,128]{1,0:T(8,128)(2,1)S(1)}, bf16[384,128]{1,0:T(8,128)(2,1)S(1)}, u32[]{:S(2)}, u32[]{:S(2)}) collective-permute-start(bf16[384,128]{1,0:T(8,128)(2,1)S(1)} %get-tuple-element.28), channel_id=1, source_target_pairs={{0,2},{1,3},{2,0},{3,1},{4,6},{5,7},{6,4},{7,5},{8,10},{9,11},{10,... | collective-permute-start | bytes 294920 | tf_op jit(solution)/shard_map/ppermute | solution.py:592
  66.1 4.8 %collective-permute-done.8 = bf16[384,128]{1,0:T(8,128)(2,1)S(1)} collective-permute-done((bf16[384,128]{1,0:T(8,128)(2,1)S(1)}, bf16[384,128]{1,0:T(8,128)(2,1)S(1)}, u32[]{:S(2)}, u32[]{:S(2)}) %collective-permute-start.8) | collective-permute-done | bytes 98336 | tf_op jit(solution)/shard_map/ppermute | solution.py:592
  71.0 3.3 %collective-permute-start.11 = (bf16[768,128]{1,0:T(8,128)(2,1)S(1)}, bf16[768,128]{1,0:T(8,128)(2,1)S(1)}, u32[]{:S(2)}, u32[]{:S(2)}) collective-permute-start(bf16[768,128]{1,0:T(8,128)(2,1)S(1)} %constant_dynamic-update-slice_fusion.5.refs_0_), channel_id=1, source_target_pairs={{0,12},{1,13},{2,14},{3,15},{4,8},{5,9},{6,10},{7,11},{8,4},{9,5},... | collective-permute-start | bytes 589832 | tf_op jit(solution)/shard_map/ppermute | solution.py:592
  75.2 14.6 %collective-permute-done.11.refs_3_ = bf16[768,128]{1,0:T(8,128)(2,1)S(1)} collective-permute-done((bf16[768,128]{1,0:T(8,128)(2,1)S(1)}, bf16[768,128]{1,0:T(8,128)(2,1)S(1)}, u32[]{:S(2)}, u32[]{:S(2)}) %collective-permute-start.11) | collective-permute-done | bytes 196640 | tf_op jit(solution)/shard_map/ppermute | solution.py:592
  89.8 1.3 %collective-permute-done.9.refs_1_ = bf16[768,128]{1,0:T(8,128)(2,1)S(1)} collective-permute-done((bf16[768,128]{1,0:T(8,128)(2,1)S(1)}, bf16[768,128]{1,0:T(8,128)(2,1)S(1)}, u32[]{:S(2)}, u32[]{:S(2)}) %collective-permute-start.9) | collective-permute-done | bytes 196640 | tf_op jit(solution)/shard_map/ppermute | solution.py:592
  91.5 2.3 %collective-permute-done.12.other_ref = bf16[1536,256]{1,0:T(8,128)(2,1)S(1)} collective-permute-done((bf16[1536,256]{1,0:T(8,128)(2,1)S(1)}, bf16[1536,256]{1,0:T(8,128)(2,1)S(1)}, u32[]{:S(2)}, u32[]{:S(2)}) %collective-permute-start.12) | collective-permute-done | bytes 786464 | tf_op jit(solution)/shard_map/ppermute | solution.py:592
  93.7 1.4 %all-to-all-done.1 = bf16[128,32,128]{2,1,0:T(8,128)(2,1)S(1)} async-done(((bf16[128,32,128]{2,1,0:T(8,128)(2,1)}), bf16[128,32,128]{2,1,0:T(8,128)(2,1)S(1)}, u32[]{:S(2)}, u32[]{:S(2)}) %all-to-all-start.1) | async-done | bytes 1048608 | tf_op jit(solution)/shard_map/all_to_all | solution.py:605
  95.1 4.3 %shard_map.142 = f32[1,512]{1,0:T(1,128)} custom-call(s32[8,512]{1,0:T(8,128)S(1)} %get-tuple-element.18.place_ref, bf16[4096,128]{1,0:T(8,128)(2,1)S(1)} %bitcast.17, f32[3,512]{1,0:T(4,128)S(1)} %copy-done.6, f32[1,512]{1,0:T(1,128)S(1)} %bitcast.22, bf16[1536,256]{1,0:T(8,128)(2,1)S(1)} %shard_map.141.own_ref, ...), custom_call_target="tpu_custom_call" | custom-call | flops 2952790016 | bytes 3000000 | tf_op jit(solution)/shard_map/pallas_call | solution.py:571
  (42 shorter events, 3.4 us)
Async XLA Ops:
  0.6 1.3 %copy-start.4 = (s32[1,512,4]{1,2,0:T(4,128)S(1)}, s32[1,512,4]{1,2,0:T(4,128)}, u32[]{:S(2)}) copy-start(s32[1,512,4]{1,2,0:T(4,128)} %param.23) | copy-start | bytes 24580
  0.6 1.3 %copy-start.3 = (s32[1,512,4]{1,2,0:T(4,128)S(1)}, s32[1,512,4]{1,2,0:T(4,128)}, u32[]{:S(2)}) copy-start(s32[1,512,4]{1,2,0:T(4,128)} %param.22) | copy-start | bytes 24580
  1.8 2.4 %collective-permute-start.1 = (f32[2,32,24,128]{3,2,1,0:T(8,128)S(1)}, f32[2,32,24,128]{3,2,1,0:T(8,128)S(1)}, u32[]{:S(2)}, u32[]{:S(2)}) collective-permute-start(f32[2,32,24,128]{3,2,1,0:T(8,128)S(1)} %shard_map.134), channel_id=1, source_target_pairs={{0,1},{1,0},{2,3},{3,2},{4,5},{5,4},{6,7},{7,6},{8,9},{9,8},{10,11... | collective-permute-start | bytes 2359304 | tf_op jit(solution)/shard_map/ppermute | solution.py:592
  4.1 16.6 %copy-start = (f32[1,2048,128]{2,1,0:T(8,128)S(1)}, f32[1,2048,128]{2,1,0:T(8,128)}, u32[]{:S(2)}) copy-start(f32[1,2048,128]{2,1,0:T(8,128)} %param.12) | copy-start | bytes 3145732
  4.1 16.6 %copy-start.1 = (f32[2048,128]{1,0:T(8,128)S(1)}, f32[2048,128]{1,0:T(8,128)}, u32[]{:S(2)}) copy-start(f32[2048,128]{1,0:T(8,128)} %square_ref.1) | copy-start | bytes 3145732
  4.1 16.6 %copy-start.2 = (f32[512,128]{1,0:T(8,128)S(1)}, f32[512,128]{1,0:T(8,128)}, u32[]{:S(2)}) copy-start(f32[512,128]{1,0:T(8,128)} %grad_ref.1) | copy-start | bytes 786436
  4.1 16.6 %copy-start.5 = (s32[512]{0:T(512)S(1)}, s32[512]{0:T(512)}, u32[]{:S(2)}) copy-start(s32[512]{0:T(512)} %param.14) | copy-start | bytes 6148
  5.1 36.5 %all-to-all-start = ((bf16[128,16,128]{2,1,0:T(8,128)(2,1)}), bf16[128,16,128]{2,1,0:T(8,128)(2,1)S(1)}, u32[]{:S(2)}, u32[]{:S(2)}) async-start(bf16[128,16,128]{2,1,0:T(8,128)(2,1)} %shard_map.135), calls=%async_computation | async-start | bytes 1048576 | tf_op jit(solution)/shard_map/all_to_all | solution.py:605
  24.5 9.8 %collective-permute-start = (bf16[512,128]{1,0:T(8,128)(2,1)S(1)}, bf16[512,128]{1,0:T(8,128)(2,1)S(1)}, u32[]{:S(2)}, u32[]{:S(2)}) collective-permute-start(bf16[512,128]{1,0:T(8,128)(2,1)S(1)} %get-tuple-element.14), channel_id=1, source_target_pairs={{0,128},{1,129},{2,130},{3,131},{4,132},{5,133},{6,134},{7,135},{8... | collective-permute-start | bytes 393224 | tf_op jit(solution)/shard_map/ppermute | solution.py:639
  25.8 20.6 %collective-permute-start.3 = (f32[2,2,24,128]{3,2,1,0:T(8,128)S(1)}, f32[2,2,24,128]{3,2,1,0:T(8,128)S(1)}, u32[]{:S(2)}, u32[]{:S(2)}) collective-permute-start(f32[2,2,24,128]{3,2,1,0:T(8,128)S(1)} %get-tuple-element.24.state_ref), channel_id=1, source_target_pairs={{0,128},{1,129},{2,130},{3,131},{4,132},{5,133},{6,134},{7,135},{8... | collective-permute-start | bytes 147464 | tf_op jit(solution)/shard_map/ppermute | solution.py:633
  41.7 4.8 %collective-permute-start.2 = (f32[2,16,128]{2,1,0:T(8,128)S(1)}, f32[2,16,128]{2,1,0:T(8,128)S(1)}, u32[]{:S(2)}, u32[]{:S(2)}) collective-permute-start(f32[2,16,128]{2,1,0:T(8,128)S(1)} %get-tuple-element.23.sum_ref), channel_id=1, source_target_pairs={{0,128},{1,129},{2,130},{3,131},{4,132},{5,133},{6,134},{7,135},{8... | collective-permute-start | bytes 49160 | tf_op jit(solution)/shard_map/ppermute | solution.py:592
  46.5 6.5 %collective-permute-start.5 = (bf16[48,128]{1,0:T(8,128)(2,1)S(1)}, bf16[48,128]{1,0:T(8,128)(2,1)S(1)}, u32[]{:S(2)}, u32[]{:S(2)}) collective-permute-start(bf16[48,128]{1,0:T(8,128)(2,1)S(1)} %shard_map.138.late_ref), channel_id=1, source_target_pairs={{112,0},{113,1},{114,2},{115,3},{116,4},{117,5},{118,6},{119,7},{1... | collective-permute-start | bytes 36872 | tf_op jit(solution)/shard_map/ppermute | solution.py:597
  47.4 4.3 %collective-permute-start.4 = (bf16[48,128]{1,0:T(8,128)(2,1)S(1)}, bf16[48,128]{1,0:T(8,128)(2,1)S(1)}, u32[]{:S(2)}, u32[]{:S(2)}) collective-permute-start(bf16[48,128]{1,0:T(8,128)(2,1)S(1)} %shard_map.138.late_ref), channel_id=1, source_target_pairs={{16,0},{17,1},{18,2},{19,3},{20,4},{21,5},{22,6},{23,7},{24,8},{25... | collective-permute-start | bytes 36872 | tf_op jit(solution)/shard_map/ppermute | solution.py:597
  51.7 11.7 %collective-permute-start.7 = (bf16[96,128]{1,0:T(8,128)(2,1)S(1)}, bf16[96,128]{1,0:T(8,128)(2,1)S(1)}, u32[]{:S(2)}, u32[]{:S(2)}) collective-permute-start(bf16[96,128]{1,0:T(8,128)(2,1)S(1)} %pad_maximum_fusion.1), channel_id=1, source_target_pairs={{32,0},{33,1},{34,2},{35,3},{36,4},{37,5},{38,6},{39,7},{40,8},{41... | collective-permute-start | bytes 73736 | tf_op jit(solution)/shard_map/ppermute | solution.py:597
  53.0 10.4 %collective-permute-start.6 = (bf16[144,128]{1,0:T(8,128)(2,1)S(1)}, bf16[144,128]{1,0:T(8,128)(2,1)S(1)}, u32[]{:S(2)}, u32[]{:S(2)}) collective-permute-start(bf16[144,128]{1,0:T(8,128)(2,1)S(1)} %pad_maximum_fusion.other_ref), channel_id=1, source_target_pairs={{80,0},{81,1},{82,2},{83,3},{84,4},{85,5},{86,6},{87,7},{88,8},{89... | collective-permute-start | bytes 110600 | tf_op jit(solution)/shard_map/ppermute | solution.py:597
  53.8 41.3 %all-to-all-start.1 = ((bf16[128,32,128]{2,1,0:T(8,128)(2,1)}), bf16[128,32,128]{2,1,0:T(8,128)(2,1)S(1)}, u32[]{:S(2)}, u32[]{:S(2)}) async-start(bf16[128,32,128]{2,1,0:T(8,128)(2,1)} %bitcast.10), calls=%async_computation.1 | async-start | bytes 2097152 | tf_op jit(solution)/shard_map/all_to_all | solution.py:605
  63.4 7.5 %collective-permute-start.8 = (bf16[384,128]{1,0:T(8,128)(2,1)S(1)}, bf16[384,128]{1,0:T(8,128)(2,1)S(1)}, u32[]{:S(2)}, u32[]{:S(2)}) collective-permute-start(bf16[384,128]{1,0:T(8,128)(2,1)S(1)} %get-tuple-element.28), channel_id=1, source_target_pairs={{0,2},{1,3},{2,0},{3,1},{4,6},{5,7},{6,4},{7,5},{8,10},{9,11},{10,... | collective-permute-start | bytes 294920 | tf_op jit(solution)/shard_map/ppermute | solution.py:592
  70.9 24.2 %copy-start.6 = (f32[3,512]{1,0:T(4,128)S(1)}, f32[3,512]{1,0:T(4,128)}, u32[]{:S(2)}) copy-start(f32[3,512]{1,0:T(4,128)} %bias_ref.1) | copy-start | bytes 18436
  70.9 24.2 %copy-start.7 = (f32[512]{0:T(512)S(1)}, f32[512]{0:T(512)}, u32[]{:S(2)}) copy-start(f32[512]{0:T(512)} %param.21) | copy-start | bytes 6148
  71.0 18.8 %collective-permute-start.11 = (bf16[768,128]{1,0:T(8,128)(2,1)S(1)}, bf16[768,128]{1,0:T(8,128)(2,1)S(1)}, u32[]{:S(2)}, u32[]{:S(2)}) collective-permute-start(bf16[768,128]{1,0:T(8,128)(2,1)S(1)} %constant_dynamic-update-slice_fusion.5.refs_0_), channel_id=1, source_target_pairs={{0,12},{1,13},{2,14},{3,15},{4,8},{5,9},{6,10},{7,11},{8,4},{9,5},... | collective-permute-start | bytes 589832 | tf_op jit(solution)/shard_map/ppermute | solution.py:592
  74.2 15.6 %collective-permute-start.10 = (bf16[768,128]{1,0:T(8,128)(2,1)S(1)}, bf16[768,128]{1,0:T(8,128)(2,1)S(1)}, u32[]{:S(2)}, u32[]{:S(2)}) collective-permute-start(bf16[768,128]{1,0:T(8,128)(2,1)S(1)} %constant_dynamic-update-slice_fusion.5.refs_0_), channel_id=1, source_target_pairs={{0,8},{1,9},{2,10},{3,11},{4,12},{5,13},{6,14},{7,15},{8,0},{9,1},... | collective-permute-start | bytes 589832 | tf_op jit(solution)/shard_map/ppermute | solution.py:592
  74.8 16.3 %collective-permute-start.9 = (bf16[768,128]{1,0:T(8,128)(2,1)S(1)}, bf16[768,128]{1,0:T(8,128)(2,1)S(1)}, u32[]{:S(2)}, u32[]{:S(2)}) collective-permute-start(bf16[768,128]{1,0:T(8,128)(2,1)S(1)} %constant_dynamic-update-slice_fusion.5.refs_0_), channel_id=1, source_target_pairs={{0,4},{1,5},{2,6},{3,7},{4,0},{5,1},{6,2},{7,3},{8,12},{9,13},{10,... | collective-permute-start | bytes 589832 | tf_op jit(solution)/shard_map/ppermute | solution.py:592
  91.4 2.4 %collective-permute-start.12 = (bf16[1536,256]{1,0:T(8,128)(2,1)S(1)}, bf16[1536,256]{1,0:T(8,128)(2,1)S(1)}, u32[]{:S(2)}, u32[]{:S(2)}) collective-permute-start(bf16[1536,256]{1,0:T(8,128)(2,1)S(1)} %shard_map.141.own_ref), channel_id=1, source_target_pairs={{0,1},{1,0},{2,3},{3,2},{4,5},{5,4},{6,7},{7,6},{8,9},{9,8},{10,11... | collective-permute-start | bytes 2359304 | tf_op jit(solution)/shard_map/ppermute | solution.py:592
